TPU v7x, 128 devices: a whole 4x4x4 slice. The times are simulated.
128 devices in a mesh: gx: 16 (over x, z), gy: 8 (over y, core).
Axes of the slice: x: 4, y: 4, z: 4, core: 2. Of those that a mesh axis runs over, the one named last changes fastest.
Arguments:
- old_state: float32 [256, 13, 16384], P(('gx', 'gy')), may hold values from -4 to 4, as said below
- new_owner: int32 [256], P(('gx', 'gy')), may hold values from 0 to 127, as said below
- new_slot: int32 [256], P(('gx', 'gy')), may hold values from 0 to 1, as said below
- neighbours: int32 [256, 6], P(('gx', 'gy')), may hold values from -1 to 1, as said below
- diffusivity: float32 [13], replicated, may hold values from 0.01 to 0.06
- stoichiometry: float32 [9], replicated, may hold values from -1 to 1
- heat_release: float32 [1], replicated, may hold values from 0.5 to 2
- prefactor: float32 [1], replicated, may hold values from 0.02 to 0.1
- activation: float32 [1], replicated, may hold values from 1 to 3
Outputs:
- final_state: float32 [256, 13, 16384], P(('gx', 'gy'))
Inputs may be any that keep to these rules, and one draw needn't show every extreme that they name: `old_state`: species within 0 to 1, velocity within -4 to 4, temperature within 1 to 3. `new_owner`: devices are numbered gx index times 8 plus gy index. A box's new owner differs from its old owner in at most one of the two indices. Of one device's boxes at most one goes to a device with another gx index and at most one to a device with another gy index; both bounds are reached in every draw. Every device owns 2 boxes afterwards. The pairs (new_owner, new_slot) name every slot of every device once. The x neighbours of a box on device (i, j) are on devices ((i - 1) mod 16, j) and ((i + 1) mod 16, j), its y neighbours on (i, (j - 1) mod 8) and (i, (j + 1) mod 8), its z neighbours on the same device; -1 marks the boundary of the domain and stands only in the z columns. The relation is symmetric.
All inputs are finite; a program needn't handle non-finite values.
Results may differ from a plain program's by a relative error of at most 0.00005.
Values sent between devices are 32-bit elements; how exact they have to be, the bound alone decides.
No kernel may reach another device: no remote copies, remote signals or barrier semaphores. Data moves between devices by JAX's collectives and lax.ppermute only.
A program may use at most 192 MiB of HBM per device.

v0:
```python
import jax
import jax.numpy as jnp
from jax import lax
from jax.sharding import PartitionSpec as P

NSPEC = 9
BX = 32
STEPS = 3


PRECISE = lax.Precision.HIGHEST


def shifted(value, axis, steps):
    count = lax.axis_size(axis)
    pairs = [(source, (source + steps) % count) for source in range(count)]
    return lax.ppermute(value, axis, pairs)


def indicator(values, count):
    return (values[:, None] == jnp.arange(count, dtype=jnp.int32)[None, :]).astype(jnp.float32)


def select_faces(selector, faces):
    return jnp.einsum("tn,ncf->tcf", selector, faces, precision=PRECISE)


def outgoing(selector, old_state, values):
    outbox = jnp.einsum("ps,sck->pck", selector, old_state, precision=PRECISE)
    labels = jnp.dot(selector, values, precision=PRECISE)
    return (outbox, labels)


def place(slot_labels, arrived, slot_count):
    selector = indicator(slot_labels.astype(jnp.int32) - 1, slot_count)
    return jnp.einsum("pt,pck->tck", selector, arrived, precision=PRECISE)


def advance(current, neighbours, diffusivity, source, prefactor, activation, receive):
    slot_count, comp_count, layer_count, plane_size = current.shape
    face_shape = (slot_count, comp_count, layer_count * BX)
    x_low = current[..., 0::BX].reshape(face_shape)
    x_high = current[..., BX - 1 :: BX].reshape(face_shape)
    y_low = current[..., :BX].reshape(face_shape)
    y_high = current[..., plane_size - BX :].reshape(face_shape)
    from_below_x, from_above_x, from_below_y, from_above_y = receive(x_low, x_high, y_low, y_high)
    line_shape = (slot_count, comp_count, layer_count, BX)
    ghost_xm = select_faces(indicator(neighbours[:, 0], slot_count), from_below_x).reshape(
        line_shape
    )
    ghost_xp = select_faces(indicator(neighbours[:, 1], slot_count), from_above_x).reshape(
        line_shape
    )
    ghost_ym = select_faces(indicator(neighbours[:, 2], slot_count), from_below_y).reshape(
        line_shape
    )
    ghost_yp = select_faces(indicator(neighbours[:, 3], slot_count), from_above_y).reshape(
        line_shape
    )
    z_low = current[:, :, 0]
    z_high = current[:, :, layer_count - 1]
    ghost_zm = jnp.where(
        (neighbours[:, 4] < 0)[:, None, None],
        z_low,
        select_faces(indicator(neighbours[:, 4], slot_count), z_high),
    )
    ghost_zp = jnp.where(
        (neighbours[:, 5] < 0)[:, None, None],
        z_high,
        select_faces(indicator(neighbours[:, 5], slot_count), z_low),
    )
    position = jnp.arange(plane_size, dtype=jnp.int32)
    x_index = position % BX
    vertical_index = position // BX
    right_side = jnp.where(
        x_index == BX - 1, jnp.repeat(ghost_xp, BX, axis=3), jnp.roll(current, -1, axis=3)
    )
    left_side = jnp.where(
        x_index == 0, jnp.repeat(ghost_xm, BX, axis=3), jnp.roll(current, 1, axis=3)
    )
    upper_side = jnp.where(
        vertical_index == BX - 1, jnp.tile(ghost_yp, (1, 1, 1, BX)), jnp.roll(current, -BX, axis=3)
    )
    lower_side = jnp.where(
        vertical_index == 0, jnp.tile(ghost_ym, (1, 1, 1, BX)), jnp.roll(current, BX, axis=3)
    )
    front_side = jnp.concatenate([current[:, :, 1:], ghost_zp[:, :, None]], axis=2)
    back_side = jnp.concatenate([ghost_zm[:, :, None], current[:, :, :-1]], axis=2)
    rates = diffusivity[None, :, None, None]
    center_power = (current[:, NSPEC + 3] ** 0.7)[:, None]
    change = jnp.zeros_like(current)
    for beside in (back_side, front_side, lower_side, upper_side, left_side, right_side):
        beside_power = (beside[:, NSPEC + 3] ** 0.7)[:, None]
        change = change + 0.5 * (rates * center_power + rates * beside_power) * (beside - current)
    reaction_rate = (
        prefactor[0]
        * current[:, 0]
        * current[:, 1]
        * jnp.exp(-activation[0] / current[:, NSPEC + 3])
    )
    return current + change + source[None, :, None, None] * reaction_rate[:, None]


def shards(
    old_state,
    new_owner,
    new_slot,
    neighbours,
    diffusivity,
    stoichiometry,
    heat_release,
    prefactor,
    activation,
):
    slot_count, comp_count, cell_count = old_state.shape
    count_y = lax.axis_size("gy")
    index_x = lax.axis_index("gx")
    index_y = lax.axis_index("gy")
    dest_x = new_owner // count_y
    dest_y = new_owner % count_y
    stays = (dest_x == index_x) & (dest_y == index_y)
    moves_x = (dest_y == index_y) & (dest_x != index_x)
    moves_y = (dest_x == index_x) & (dest_y != index_y)
    slot_ids = jnp.arange(slot_count, dtype=jnp.int32)
    kept_table = (stays[None, :] & (new_slot[None, :] == slot_ids[:, None])).astype(jnp.float32)
    regridded = jnp.einsum("ts,sck->tck", kept_table, old_state, precision=PRECISE)
    slot_plus = (new_slot + 1).astype(jnp.float32)
    values_x = jnp.stack((dest_x.astype(jnp.float32), slot_plus), axis=1)
    outbox_x, labels_x = outgoing(moves_x[None, :].astype(jnp.float32), old_state, values_x)
    piece_boxes = lax.all_gather(outbox_x, "gx", axis=0, tiled=True)
    piece_labels = lax.all_gather(labels_x, "gx", axis=0, tiled=True)
    is_mine = piece_labels[:, 0].astype(jnp.int32) == index_x
    regridded = regridded + place(
        jnp.where(is_mine, piece_labels[:, 1], 0.0), piece_boxes, slot_count
    )
    values_y = jnp.stack((dest_y.astype(jnp.float32), slot_plus), axis=1)
    outbox_y, labels_y = outgoing(moves_y[None, :].astype(jnp.float32), old_state, values_y)
    piece_boxes = lax.all_gather(outbox_y, "gy", axis=0, tiled=True)
    piece_labels = lax.all_gather(labels_y, "gy", axis=0, tiled=True)
    is_mine = piece_labels[:, 0].astype(jnp.int32) == index_y
    regridded = regridded + place(
        jnp.where(is_mine, piece_labels[:, 1], 0.0), piece_boxes, slot_count
    )

    def receive(x_low, x_high, y_low, y_high):
        from_below_x = shifted(x_high, "gx", 1)
        from_above_x = shifted(x_low, "gx", -1)
        from_below_y = shifted(y_high, "gy", 1)
        from_above_y = shifted(y_low, "gy", -1)
        return (from_below_x, from_above_x, from_below_y, from_above_y)

    source = jnp.concatenate([stoichiometry, jnp.zeros((3,), jnp.float32), heat_release])
    layer_count = cell_count // (BX * BX)
    current = regridded.reshape(slot_count, comp_count, layer_count, BX * BX)
    for step_index in range(STEPS):
        current = advance(current, neighbours, diffusivity, source, prefactor, activation, receive)
    return current.reshape(slot_count, comp_count, cell_count)


def solution(mesh):
    return jax.shard_map(
        shards,
        mesh=mesh,
        in_specs=(
            P(("gx", "gy"), None, None),
            P(("gx", "gy")),
            P(("gx", "gy")),
            P(("gx", "gy"), None),
            P(),
            P(),
            P(),
            P(),
            P(),
        ),
        out_specs=P(("gx", "gy"), None, None),
        check_vma=False,
    )
```

profile of v0, /device:TPU:0, one launch (start us, length us, event | category | flops | bytes accessed | tf_op | source)
XLA Modules:
  0.0 739.1 jit_solution(5741506932752084354)
XLA Ops:
  8.0 3.4 fusion.200
  13.0 3.4 fusion.198
  22.6 15.3 %all-reduce.1 = f32[16]{0:T(128)S(1)} all-reduce(f32[16]{0:T(128)S(1)} %dynamic-update-slice.1), channel_id=4, replica_groups=mesh['gx'=16,'gy'=8] {'gy'}, use_global_device_ids=true, to_apply=%add.1 | all-reduce | flops 16 | bytes 128
  38.3 43.1 %all-reduce = f32[32]{0:T(128)S(1)} all-reduce(f32[32]{0:T(128)S(1)} %dynamic-update-slice), channel_id=2, replica_groups=mesh['gx'=16,'gy'=8] {'gx'}, use_global_device_ids=true, to_apply=%add | all-reduce | flops 32 | bytes 256
  86.4 41.1 %all-gather.9.cloned.1.call-done = f32[16,13,16384]{2,1,0:T(8,128)} async-done(((f32[1,13,16384]{2,1,0:T(8,128)}), f32[16,13,16384]{2,1,0:T(8,128)}) %all-gather.9.cloned.1.call-update) | async-done | bytes 13631504 | tf_op jit(solution)/shard_map/all_gather | solution.py:130
  127.6 17.4 %fusion = f32[2,13,16384]{2,0,1:T(2,128)S(1)} fusion(f32[16,13,16384]{2,1,0:T(8,128)} %all-gather.9.cloned.1.call-done, s32[16]{0:T(128)S(1)} %fusion.146), kind=kOutput, calls=%fused_computation.2 | convolution fusion | flops 81788960 | bytes 15335488 | tf_op jit(solution)/shard_map/pt,pck->tck/dot_general | solution.py:36
  145.0 4.7 convolution_add_fusion.1
  149.6 28.7 %all-gather.11.cloned.1.call-done = f32[8,13,16384]{2,1,0:T(8,128)} async-done(((f32[1,13,16384]{2,1,0:T(8,128)}), f32[8,13,16384]{2,1,0:T(8,128)}) %all-gather.11.cloned.1.call-update) | async-done | bytes 6815760 | tf_op jit(solution)/shard_map/all_gather | solution.py:138
  178.4 11.2 %convolution_add_fusion = f32[2,13,16384]{2,0,1:T(2,128)S(1)} fusion(f32[2,13,16384]{2,0,1:T(2,128)} %convolution_add_fusion.1, f32[8,13,16384]{2,1,0:T(8,128)} %all-gather.11.cloned.1.call-done, s32[8]{0:T(128)S(1)} %add_reduce_fusion), kind=kOutput, calls=%fused_computation | convolution fusion | flops 41320464 | bytes 10223648 | tf_op jit(solution)/shard_map/pt,pck->tck/dot_general | solution.py:36
  191.0 5.9 slice.294
  196.9 6.0 slice.299
  210.7 4.1 fusion.252
  214.7 4.2 fusion.255
  223.8 3.8 collective-permute-start.3
  255.0 7.2 tile.79
  262.3 5.4 reshape.304
  269.3 4.2 tile.73
  273.5 6.8 tile.75
  280.3 6.3 reshape.303
  288.2 5.1 broadcast_in_dim.256
  293.4 6.8 reshape.241
  300.2 6.3 reshape.305
  309.9 5.1 broadcast_in_dim.261
  315.0 6.8 reshape.245
  321.8 6.3 reshape.306
  328.1 9.2 %fusion.113 = (f32[16,13,1,2,1024]{4,3,2,1,0:T(2,128)}, f32[2,13,16,1024]{3,0,1,2:T(2,128)S(1)}, f32[2,13,16,1024]{3,0,1,2:T(2,128)S(1)}, f32[16,13,1,2,1024]{4,3,2,1,0:T(2,128)}) fusion(f32[2,13,16,1]{3,0,1,2:T(2,128)} %get-tuple-element.82, f32[2,13,16,1023]{3,0,1,2:T(2,128)} %get-tuple-element.84, f32[2,13,16,1024]{3,2,0,1:T(8,128)} %reshape.306, ...), kind=kLoop, calls=%fused_computation.203 | loop fusion | flops 1703936 | bytes 13633536
  346.8 11.7 %multiply_add_fusion.32 = f32[2,13,16,1024]{3,0,1,2:T(2,128)S(1)} fusion(f32[2,13,16,1024]{3,0,1,2:T(2,128)S(1)} %get-tuple-element.22, f32[2,13,16,1024]{3,0,1,2:T(2,128)S(1)} %get-tuple-element.87, f32[2,13,16,1024]{3,0,1,2:T(2,128)S(1)} %get-tuple-element.18, f32[2,13,16,1024]{3,0,1,2:T(2,128)S(1)} %get-tuple-element.16, ...), kind=kLoop, calls=%fused_computation.170 | loop fusion | flops 17465344 | bytes 14680168 | tf_op jit(solution)/shard_map/add | solution.py:101
  359.3 7.1 slice.318
  366.4 7.4 %slice.322 = f32[2,13,16,32]{3,0,1,2:T(2,128)} slice(f32[2,13,16,1024]{3,0,1,2:T(2,128)S(1)} %multiply_add_fusion.32), slice={[0:2:1], [0:13:1], [0:16:1], [0:1024:32]} | slice | bytes 106496 | tf_op jit(solution)/shard_map/slice | solution.py:42
  382.0 4.1 fusion.247
  386.1 4.0 fusion.250
  402.1 5.3 collective-permute-start.7
  430.2 7.0 tile.87
  437.2 6.3 reshape.308
  446.9 6.8 tile.83
  453.7 6.3 reshape.307
  460.1 4.1 broadcast_in_dim.268
  464.2 6.8 reshape.255
  471.1 5.4 reshape.310
  479.8 5.1 broadcast_in_dim.267
  485.0 6.8 reshape.251
  491.8 6.3 reshape.309
  498.1 5.3 fusion.111
  504.4 3.5 fusion.112
  517.2 11.3 %multiply_add_fusion.31 = f32[2,13,16,1024]{3,0,1,2:T(2,128)S(1)} fusion(f32[2,13,16,1024]{3,0,1,2:T(2,128)S(1)} %multiply_add_fusion.32, f32[2,13,16,1024]{3,0,1,2:T(2,128)S(1)} %get-tuple-element.30, f32[2,13,16,1024]{3,0,1,2:T(2,128)S(1)} %get-tuple-element.28, f32[2,13,16,1024]{3,0,1,2:T(2,128)S(1)} %get-tuple-element.26, ...), kind=kLoop, calls=%fused_computation.169 | loop fusion | flops 17465344 | bytes 14680168 | tf_op jit(solution)/shard_map/add | solution.py:101
  529.3 7.1 slice.341
  536.4 7.4 %slice.345 = f32[2,13,16,32]{3,0,1,2:T(2,128)} slice(f32[2,13,16,1024]{3,0,1,2:T(2,128)S(1)} %multiply_add_fusion.31), slice={[0:2:1], [0:13:1], [0:16:1], [0:1024:32]} | slice | bytes 106496 | tf_op jit(solution)/shard_map/slice | solution.py:42
  550.9 3.5 fusion.244
  554.4 4.1 fusion.242
  564.2 5.5 collective-permute-start.11
  577.2 3.5 fusion.6
  612.5 4.2 tile.93
  616.7 7.0 tile.95
  623.7 6.3 reshape.312
  630.9 4.2 tile.89
  635.1 6.8 tile.91
  641.9 6.3 reshape.311
  649.1 5.1 broadcast_in_dim.272
  654.2 6.8 reshape.265
  661.1 6.3 reshape.314
  669.3 5.1 broadcast_in_dim.271
  674.5 6.8 reshape.261
  681.3 6.3 reshape.313
  692.6 39.4 %multiply_add_fusion.30 = f32[2,13,16384]{2,0,1:T(2,128)} fusion(f32[2,13,16384]{2,0,1:T(2,128)} %reshape.265, f32[2,13,16384]{2,0,1:T(2,128)} %bitcast.456, f32[2,13,16384]{2,0,1:T(2,128)} %reshape.261, f32[2,13,16384]{2,0,1:T(2,128)} %bitcast.455, f32[2,13,16384]{2,0,1:T(2,128)} %tile.95, f32[2,13,16384]{2,0,1:T(2,128)} %bitcast.458, ...), kind=kLoop, calls=%fused_computation.168 | loop fusion | flops 54951936 | bytes 57737320 | tf_op jit(solution)/shard_map/add | solution.py:101
  (411 shorter events, 190.1 us)
Async XLA Ops:
  6.5 121.0 %all-gather.9.cloned.1.call-start = ((), (), s32[]{:S(2)}) async-start(), calls=%async_computation | async-start | bytes 17825792 | tf_op jit(solution)/shard_map/all_gather | solution.py:130
  12.9 165.5 %all-gather.11.cloned.1.call-start = ((), (), s32[]{:S(2)}) async-start(), calls=%async_computation.1 | async-start | bytes 9437184 | tf_op jit(solution)/shard_map/all_gather | solution.py:138
  16.4 5.9 copy-start.110
  16.4 67.6 %copy-start.104 = (f32[9]{0:T(128)S(1)}, f32[9]{0:T(128)}, u32[]{:S(2)}) copy-start(f32[9]{0:T(128)} %param.14) | copy-start | bytes 112
  16.4 68.4 %copy-start.74 = (s32[2,6]{1,0:T(2,128)S(1)}, s32[2,6]{1,0:T(2,128)}, u32[]{:S(2)}) copy-start(s32[2,6]{1,0:T(2,128)} %param.12) | copy-start | bytes 148
  81.5 427.3 %copy-start.77 = (pred[1024]{0:T(1024)(128)(4,1)}, pred[1024]{0:T(1024)(128)(4,1)S(1)}, u32[]{:S(2)}) copy-start(pred[1024]{0:T(1024)(128)(4,1)S(1)} %fusion.154) | copy-start | bytes 3076
  82.2 430.6 %copy-start.75 = (pred[1024]{0:T(1024)(128)(4,1)}, pred[1024]{0:T(1024)(128)(4,1)S(1)}, u32[]{:S(2)}) copy-start(pred[1024]{0:T(1024)(128)(4,1)S(1)} %fusion.155) | copy-start | bytes 3076
  82.8 415.3 %copy-start.81 = (pred[1024]{0:T(1024)(128)(4,1)}, pred[1024]{0:T(1024)(128)(4,1)S(1)}, u32[]{:S(2)}) copy-start(pred[1024]{0:T(1024)(128)(4,1)S(1)} %fusion.157) | copy-start | bytes 3076
  83.4 420.9 %copy-start.79 = (pred[1024]{0:T(1024)(128)(4,1)}, pred[1024]{0:T(1024)(128)(4,1)S(1)}, u32[]{:S(2)}) copy-start(pred[1024]{0:T(1024)(128)(4,1)S(1)} %fusion.158) | copy-start | bytes 3076
  85.7 59.2 %copy-start.91 = (s32[2]{0:T(128)}, s32[2]{0:T(128)S(1)}, u32[]{:S(2)}) copy-start(s32[2]{0:T(128)S(1)} %get-tuple-element.8) | copy-start | bytes 28
  85.7 121.9 %copy-start.88 = (s32[2]{0:T(128)}, s32[2]{0:T(128)S(1)}, u32[]{:S(2)}) copy-start(s32[2]{0:T(128)S(1)} %get-tuple-element.5) | copy-start | bytes 28
  86.4 121.1 %copy-start.105 = (pred[2]{0:T(512)(128)(4,1)}, pred[2]{0:T(512)(128)(4,1)S(1)}, u32[]{:S(2)}) copy-start(pred[2]{0:T(512)(128)(4,1)S(1)} %get-tuple-element.90) | copy-start | bytes 10
  189.5 157.2 %copy-start.2 = (f32[2,13,16384]{2,0,1:T(2,128)}, f32[2,13,16384]{2,0,1:T(2,128)S(1)}, u32[]{:S(2)}) copy-start(f32[2,13,16384]{2,0,1:T(2,128)S(1)} %convolution_add_fusion) | copy-start | bytes 5111812
  208.7 138.0 %copy-start.48 = (f32[2,1,16,1024]{3,0,1,2:T(2,128)}, f32[2,1,16,1024]{3,0,1,2:T(2,128)S(1)}, u32[]{:S(2)}) copy-start(f32[2,1,16,1024]{3,0,1,2:T(2,128)S(1)} %fusion.134) | copy-start | bytes 393220
  222.3 25.6 %collective-permute-start.2 = (f32[2,13,512]{2,0,1:T(2,128)}, f32[2,13,512]{2,0,1:T(2,128)}, u32[]{:S(2)}, u32[]{:S(2)}) collective-permute-start(f32[2,13,512]{2,0,1:T(2,128)} %reshape.238), channel_id=1, source_target_pairs={{0,8},{8,16},{16,24},{24,32},{32,40},{40,48},{48,56},{56,64},{64,7... | collective-permute-start | bytes 159752 | tf_op jit(solution)/shard_map/ppermute | solution.py:17
  223.8 82.7 %collective-permute-start.3 = (f32[2,13,512]{2,0,1:T(2,128)}, f32[2,13,512]{2,0,1:T(2,128)}, u32[]{:S(2)}, u32[]{:S(2)}) collective-permute-start(f32[2,13,512]{2,0,1:T(2,128)} %reshape.242), channel_id=1, source_target_pairs={{0,120},{8,0},{16,8},{24,16},{32,24},{40,32},{48,40},{56,48},{64,5... | collective-permute-start | bytes 159752 | tf_op jit(solution)/shard_map/ppermute | solution.py:17
  232.6 17.0 %collective-permute-start = (f32[2,13,512]{2,0,1:T(2,128)}, f32[2,13,512]{2,0,1:T(2,128)}, u32[]{:S(2)}, u32[]{:S(2)}) collective-permute-start(f32[2,13,512]{2,0,1:T(2,128)} %reshape.236), channel_id=1, source_target_pairs={{0,1},{1,2},{2,3},{3,4},{4,5},{5,6},{6,7},{7,0},{8,9},{9,10},{10,1... | collective-permute-start | bytes 159752 | tf_op jit(solution)/shard_map/ppermute | solution.py:17
  235.9 15.4 %collective-permute-start.1 = (f32[2,13,512]{2,0,1:T(2,128)}, f32[2,13,512]{2,0,1:T(2,128)S(1)}, u32[]{:S(2)}, u32[]{:S(2)}) collective-permute-start(f32[2,13,512]{2,0,1:T(2,128)} %reshape.237), channel_id=1, source_target_pairs={{0,7},{1,0},{2,1},{3,2},{4,3},{5,4},{6,5},{7,6},{8,15},{9,8},{10,9... | collective-permute-start | bytes 159752 | tf_op jit(solution)/shard_map/ppermute | solution.py:17
  245.8 5.5 copy-start.96
  328.1 11.1 %copy-start.34 = (f32[2,13,16,992]{3,0,1,2:T(2,128)S(1)}, f32[2,13,16,992]{3,0,1,2:T(2,128)}, u32[]{:S(2)}) copy-start(f32[2,13,16,992]{3,0,1,2:T(2,128)} %get-tuple-element.78) | copy-start | bytes 4952068
  328.1 11.1 %copy-start.46 = (f32[2,13,16,32]{3,0,1,2:T(2,128)S(1)}, f32[2,13,16,32]{3,0,1,2:T(2,128)}, u32[]{:S(2)}) copy-start(f32[2,13,16,32]{3,0,1,2:T(2,128)} %get-tuple-element.80) | copy-start | bytes 159748
  342.3 4.5 copy-start.9
  342.3 4.4 copy-start.11
  342.3 4.4 copy-start.50
  342.3 4.4 copy-start.54
  342.3 4.4 copy-start.61
  342.3 4.4 copy-start.63
  342.3 4.4 copy-start.69
  342.3 4.4 copy-start.82
  342.3 4.4 copy-start.85
  346.8 11.7 %copy-start.92 = (s32[2]{0:T(128)S(1)}, s32[2]{0:T(128)}, u32[]{:S(2)}) copy-start(s32[2]{0:T(128)} %copy-done.91) | copy-start | bytes 28
  346.8 11.7 %copy-start.108 = (pred[2]{0:T(512)(128)(4,1)S(1)}, pred[2]{0:T(512)(128)(4,1)}, u32[]{:S(2)}) copy-start(pred[2]{0:T(512)(128)(4,1)} %get-tuple-element.89) | copy-start | bytes 10
  346.8 12.1 %copy-start.89 = (s32[2]{0:T(128)S(1)}, s32[2]{0:T(128)}, u32[]{:S(2)}) copy-start(s32[2]{0:T(128)} %copy-done.88) | copy-start | bytes 28
  346.8 12.1 %copy-start.106 = (pred[2]{0:T(512)(128)(4,1)S(1)}, pred[2]{0:T(512)(128)(4,1)}, u32[]{:S(2)}) copy-start(pred[2]{0:T(512)(128)(4,1)} %copy-done.105) | copy-start | bytes 10
  358.9 21.1 %copy-start.56 = (f32[2,13,1,1024]{3,0,1,2:T(2,128)}, f32[2,13,1,1024]{3,0,1,2:T(2,128)S(1)}, u32[]{:S(2)}) copy-start(f32[2,13,1,1024]{3,0,1,2:T(2,128)S(1)} %fusion.101) | copy-start | bytes 319492
  359.3 17.8 %copy-start.58 = (f32[2,13,1,1024]{3,0,1,2:T(2,128)}, f32[2,13,1,1024]{3,0,1,2:T(2,128)S(1)}, u32[]{:S(2)}) copy-start(f32[2,13,1,1024]{3,0,1,2:T(2,128)S(1)} %fusion.102) | copy-start | bytes 319492
  377.1 140.0 %copy-start.52 = (f32[2,1,16,1024]{3,0,1,2:T(2,128)}, f32[2,1,16,1024]{3,0,1,2:T(2,128)S(1)}, u32[]{:S(2)}) copy-start(f32[2,1,16,1024]{3,0,1,2:T(2,128)S(1)} %fusion.136) | copy-start | bytes 393220
  396.4 21.7 %copy-start.19 = (f32[16,13,1,2,1024]{4,3,2,1,0:T(2,128)S(1)}, f32[16,13,1,2,1024]{4,3,2,1,0:T(2,128)}, u32[]{:S(2)}) copy-start(f32[16,13,1,2,1024]{4,3,2,1,0:T(2,128)} %get-tuple-element.88) | copy-start | bytes 5111812
  398.7 77.7 %collective-permute-start.6 = (f32[2,13,512]{2,0,1:T(2,128)}, f32[2,13,512]{2,0,1:T(2,128)}, u32[]{:S(2)}, u32[]{:S(2)}) collective-permute-start(f32[2,13,512]{2,0,1:T(2,128)} %reshape.248), channel_id=1, source_target_pairs={{0,8},{8,16},{16,24},{24,32},{32,40},{40,48},{48,56},{56,64},{64,7... | collective-permute-start | bytes 159752 | tf_op jit(solution)/shard_map/ppermute | solution.py:17
  402.1 22.1 %collective-permute-start.7 = (f32[2,13,512]{2,0,1:T(2,128)}, f32[2,13,512]{2,0,1:T(2,128)}, u32[]{:S(2)}, u32[]{:S(2)}) collective-permute-start(f32[2,13,512]{2,0,1:T(2,128)} %reshape.252), channel_id=1, source_target_pairs={{0,120},{8,0},{16,8},{24,16},{32,24},{40,32},{48,40},{56,48},{64,5... | collective-permute-start | bytes 159752 | tf_op jit(solution)/shard_map/ppermute | solution.py:17
  411.8 13.5 %collective-permute-start.4 = (f32[2,13,512]{2,0,1:T(2,128)}, f32[2,13,512]{2,0,1:T(2,128)}, u32[]{:S(2)}, u32[]{:S(2)}) collective-permute-start(f32[2,13,512]{2,0,1:T(2,128)} %reshape.246), channel_id=1, source_target_pairs={{0,1},{1,2},{2,3},{3,4},{4,5},{5,6},{6,7},{7,0},{8,9},{9,10},{10,1... | collective-permute-start | bytes 159752 | tf_op jit(solution)/shard_map/ppermute | solution.py:17
  415.1 11.3 %collective-permute-start.5 = (f32[2,13,512]{2,0,1:T(2,128)}, f32[2,13,512]{2,0,1:T(2,128)S(1)}, u32[]{:S(2)}, u32[]{:S(2)}) collective-permute-start(f32[2,13,512]{2,0,1:T(2,128)} %reshape.247), channel_id=1, source_target_pairs={{0,7},{1,0},{2,1},{3,2},{4,3},{5,4},{6,5},{7,6},{8,15},{9,8},{10,9... | collective-permute-start | bytes 159752 | tf_op jit(solution)/shard_map/ppermute | solution.py:17
  422.1 4.3 copy-start.97
  498.1 6.3 copy-start.29
  498.1 6.3 copy-start.35
  498.1 6.3 copy-start.47
  504.4 4.4 copy-start.33
  504.4 4.4 copy-start.67
  512.8 4.3 copy-start.5
  512.8 4.3 copy-start.7
  512.8 4.3 copy-start.53
  517.2 11.3 %copy-start.93 = (s32[2]{0:T(128)S(1)}, s32[2]{0:T(128)}, u32[]{:S(2)}) copy-start(s32[2]{0:T(128)} %copy-done.91) | copy-start | bytes 28
  517.2 11.3 %copy-start.109 = (pred[2]{0:T(512)(128)(4,1)S(1)}, pred[2]{0:T(512)(128)(4,1)}, u32[]{:S(2)}) copy-start(pred[2]{0:T(512)(128)(4,1)} %get-tuple-element.89) | copy-start | bytes 10
  517.2 11.7 %copy-start.90 = (s32[2]{0:T(128)S(1)}, s32[2]{0:T(128)}, u32[]{:S(2)}) copy-start(s32[2]{0:T(128)} %copy-done.88) | copy-start | bytes 28
  517.2 11.7 %copy-start.107 = (pred[2]{0:T(512)(128)(4,1)S(1)}, pred[2]{0:T(512)(128)(4,1)}, u32[]{:S(2)}) copy-start(pred[2]{0:T(512)(128)(4,1)} %copy-done.105) | copy-start | bytes 10
  560.9 106.5 %collective-permute-start.10 = (f32[2,13,512]{2,0,1:T(2,128)}, f32[2,13,512]{2,0,1:T(2,128)}, u32[]{:S(2)}, u32[]{:S(2)}) collective-permute-start(f32[2,13,512]{2,0,1:T(2,128)} %reshape.258), channel_id=1, source_target_pairs={{0,8},{8,16},{16,24},{24,32},{32,40},{40,48},{48,56},{56,64},{64,7... | collective-permute-start | bytes 159752 | tf_op jit(solution)/shard_map/ppermute | solution.py:17
  564.2 43.5 %collective-permute-start.11 = (f32[2,13,512]{2,0,1:T(2,128)}, f32[2,13,512]{2,0,1:T(2,128)}, u32[]{:S(2)}, u32[]{:S(2)}) collective-permute-start(f32[2,13,512]{2,0,1:T(2,128)} %reshape.262), channel_id=1, source_target_pairs={{0,120},{8,0},{16,8},{24,16},{32,24},{40,32},{48,40},{56,48},{64,5... | collective-permute-start | bytes 159752 | tf_op jit(solution)/shard_map/ppermute | solution.py:17
  572.5 36.3 %collective-permute-start.8 = (f32[2,13,512]{2,0,1:T(2,128)}, f32[2,13,512]{2,0,1:T(2,128)}, u32[]{:S(2)}, u32[]{:S(2)}) collective-permute-start(f32[2,13,512]{2,0,1:T(2,128)} %reshape.256), channel_id=1, source_target_pairs={{0,1},{1,2},{2,3},{3,4},{4,5},{5,6},{6,7},{7,0},{8,9},{9,10},{10,1... | collective-permute-start | bytes 159752 | tf_op jit(solution)/shard_map/ppermute | solution.py:17
  574.3 35.7 %collective-permute-start.9 = (f32[2,13,512]{2,0,1:T(2,128)}, f32[2,13,512]{2,0,1:T(2,128)S(1)}, u32[]{:S(2)}, u32[]{:S(2)}) collective-permute-start(f32[2,13,512]{2,0,1:T(2,128)} %reshape.257), channel_id=1, source_target_pairs={{0,7},{1,0},{2,1},{3,2},{4,3},{5,4},{6,5},{7,6},{8,15},{9,8},{10,9... | collective-permute-start | bytes 159752 | tf_op jit(solution)/shard_map/ppermute | solution.py:17
  605.6 4.3 copy-start.98
  661.1 6.3 copy-start.95
  681.3 6.3 slice-start
  681.3 10.5 %copy-start.71 = (pred[2,8,8,128]{3,1,2,0:T(8,128)(4,1)S(1)}, pred[2,8,8,128]{3,1,2,0:T(8,128)(4,1)}, u32[]{:S(2)}) copy-start(pred[2,8,8,128]{3,1,2,0:T(8,128)(4,1)} %copy.227) | copy-start | bytes 49156
  692.6 39.4 %copy-start.1 = (f32[2,13,16384]{2,0,1:T(2,128)S(1)}, f32[2,13,16384]{2,0,1:T(2,128)}, u32[]{:S(2)}) copy-start(f32[2,13,16384]{2,0,1:T(2,128)} %param.9) | copy-start | bytes 5111812
  (67 other events, 179.3 us)
Sparse Core Ops, SparseCore 0:
  13.0 114.4 all-gather.8
  129.3 49.0 all-gather.10
where the time goes:
time: 747 us; the launch traced here: 739 us
  local copies, waits for them, and re-layouts  386 us (52%)
  other arithmetic  124 us (17%)
  waiting for transfers between devices  69.9 us (9%)
  blocking collectives  58.4 us (8%)
  matrix products  57.7 us (8%)
  starting transfers between devices  25.1 us (3%)
  between operations  18.2 us (2%)
    add x3, other arithmetic, advance(): current + change + source[None, :, None, None] * reaction_rate[:, None]  62.3 us
    unnamed x2, blocking collectives  58.4 us
    another operation x12, local copies, waits for them, and re-layouts, advance(): jnp.tile(ghost_ym, (1, 1, 1, BX))  53.7 us
    another operation x12, local copies, waits for them, and re-layouts, advance(): jnp.tile(ghost_yp, (1, 1, 1, BX))  51.9 us
    unnamed x17, other arithmetic  48.6 us
    all_gather x1, waiting for transfers between devices, shards(): piece_boxes = lax.all_gather(outbox_x, 'gx', axis=0, tiled=True)  41.1 us
    reshape x6, local copies, waits for them, and re-layouts, advance(): jnp.repeat(ghost_xm, BX, axis=3)  39.4 us
    reshape x6, local copies, waits for them, and re-layouts, advance(): jnp.repeat(ghost_xp, BX, axis=3)  38.5 us
  transfers between devices with their start and end apart: 14, of which 2 were waited for; matrix products, arithmetic and copies ran while one was open for 37% of the time, Pallas kernels for 0%

commit v1 on v0

v1 whole, which is shorter than its diff:
```python
import functools

import jax
import jax.numpy as jnp
from jax import lax
from jax.experimental import pallas as pl
from jax.experimental.pallas import tpu as pltpu
from jax.sharding import PartitionSpec as P

NSPEC = 9
COMPS = 13
TEMP = 12
BX = 32
BZ = 16
SLOTS = 2
STEPS = 3
LAYERS = SLOTS * BZ
LROWS = COMPS * 8
BROWS = BZ * LROWS
ROWS = SLOTS * BROWS
TAG = 8
PIECE = LROWS + TAG
YBOX = BROWS + TAG
NONE = -1.0
SMEM = pltpu.SMEM
VMEM = pltpu.VMEM
F32 = jnp.float32
PARAMS = pltpu.CompilerParams(vmem_limit_bytes=48 * 1024 * 1024)


def shifted(value, axis, steps):
    count = lax.axis_size(axis)
    pairs = [(source, (source + steps) % count) for source in range(count)]
    return lax.ppermute(value, axis, pairs)


def moves(owner_ref, row, count_y, index_x, index_y):
    owner = owner_ref[row]
    dest_x = owner // count_y
    dest_y = owner - dest_x * count_y
    goes_x = (dest_y == index_y) & (dest_x != index_x)
    goes_y = (dest_x == index_x) & (dest_y != index_y)
    return dest_x, dest_y, goes_x, goes_y


def pack_kernel(count_y, owner_ref, slot_ref, old_ref, box_ref, outx_ref, outy_ref):
    index_x = lax.axis_index("gx")
    index_y = lax.axis_index("gy")

    def layer(z, carry):
        for n in range(SLOTS):
            row = pl.multiple_of(n * BROWS + z * LROWS, 8)
            for t in range(8):
                cells = pl.ds(pl.multiple_of(z * 1024 + t * 128, 128), 128)
                box_ref[pl.ds(row + t, COMPS, stride=8), :] = old_ref[n, :, cells]
        return carry

    lax.fori_loop(0, BZ, layer, 0)
    row_x = jnp.int32(0)
    row_y = jnp.int32(0)
    tag_x = jnp.int32(-1)
    tag_y = jnp.int32(-1)
    for n in range(SLOTS):
        dest_x, dest_y, goes_x, goes_y = moves(owner_ref, n, count_y, index_x, index_y)
        row_x = jnp.where(goes_x, n, row_x)
        row_y = jnp.where(goes_y, n, row_y)
        tag_x = jnp.where(goes_x, dest_x * SLOTS + slot_ref[n], tag_x)
        tag_y = jnp.where(goes_y, dest_y * SLOTS + slot_ref[n], tag_y)

    def copy(z, carry):
        source_x = pl.ds(pl.multiple_of(row_x * BROWS + z * LROWS, 8), LROWS)
        source_y = pl.ds(pl.multiple_of(row_y * BROWS + z * LROWS, 8), LROWS)
        outx_ref[z, :LROWS, :] = box_ref[source_x, :]
        outx_ref[z, LROWS:, :] = jnp.full((TAG, 128), tag_x, jnp.int32).astype(F32)
        outy_ref[0, pl.ds(pl.multiple_of(z * LROWS, 8), LROWS), :] = box_ref[source_y, :]
        return carry

    lax.fori_loop(0, BZ, copy, 0)
    outy_ref[0, BROWS:, :] = jnp.full((TAG, 128), tag_y, jnp.int32).astype(F32)


def tag_of(tile):
    return jnp.max(tile).astype(jnp.int32)


def sort_kernel(pieces_ref, first_ref, second_ref, more_ref, used_ref):
    count = pieces_ref.shape[0]
    empty = jnp.full((TAG, 128), NONE, F32)
    more_ref[0] = 0
    tags = []
    for d in range(count):
        first_ref[d, LROWS:, :] = empty
        second_ref[d, LROWS:, :] = empty
        used_ref[d] = 0
        tags.append(tag_of(pieces_ref[d, LROWS:, :]))
    for s in range(count):
        tag = tags[s]
        there = jnp.maximum(tag, 0) // SLOTS
        used = used_ref[there]

        @pl.when((tag >= 0) & (used == 0))
        def _():
            first_ref[there, :, :] = pieces_ref[s]
            used_ref[there] = 1

        @pl.when((tag >= 0) & (used == 1))
        def _():
            second_ref[there, :, :] = pieces_ref[s]
            more_ref[0] = 1


def roll(value, shift, axis):
    if isinstance(shift, int):
        shift = shift % value.shape[axis]
        if shift == 0:
            return value
        return pltpu.roll(value, shift, axis)
    return pltpu.roll(value, lax.rem(shift + 256, 128), axis)


def lanes():
    return lax.broadcasted_iota(jnp.int32, (8, 128), 1)


def sublanes():
    return lax.broadcasted_iota(jnp.int32, (8, 128), 0)


def put_x_faces(layer_index, c, value, low_ref, high_ref):
    here = (lanes() & 31) == layer_index
    rows = pl.ds(c * 8, 8)
    low_ref[rows, :] = jnp.where(here, roll(value, layer_index, 1), low_ref[rows, :])
    high_ref[rows, :] = jnp.where(here, roll(value, layer_index - 31, 1), high_ref[rows, :])


def put_y_faces(state_ref, low_ref, high_ref):
    group = lanes() >> 5

    for c in range(COMPS):
        low = jnp.zeros((8, 128), F32)
        high = jnp.zeros((8, 128), F32)
        for n in range(SLOTS):
            for half in range(2):
                where = 2 * n + half
                base = n * BROWS + half * 8 * LROWS + c * 8
                bottom = state_ref[pl.ds(base, 8, stride=LROWS), :]
                top = state_ref[pl.ds(base + 7, 8, stride=LROWS), :]
                low = jnp.where(group == where, roll(bottom, 32 * where, 1), low)
                high = jnp.where(group == where, roll(top, 32 * where - 96, 1), high)
        low_ref[c * 8 : c * 8 + 8, :] = low
        high_ref[c * 8 : c * 8 + 8, :] = high


def place_kernel(
    count_y, owner_ref, slot_ref, box_ref, first_ref, second_ref, ally_ref,
    state_ref, xl_ref, xh_ref, yl_ref, yh_ref, tagx_ref, tagy_ref, tag_sem, sems,
):
    index_x = lax.axis_index("gx")
    index_y = lax.axis_index("gy")
    loads = [
        pltpu.make_async_copy(ally_ref.at[:, pl.ds(BROWS, TAG), :], tagy_ref, tag_sem.at[0]),
        pltpu.make_async_copy(first_ref.at[0, pl.ds(LROWS, TAG), :], tagx_ref.at[0], tag_sem.at[1]),
        pltpu.make_async_copy(second_ref.at[0, pl.ds(LROWS, TAG), :], tagx_ref.at[1], tag_sem.at[2]),
    ]
    for load in loads:
        load.start()
    for load in loads:
        load.wait()

    def into(slot):
        return state_ref.at[pl.ds(slot * BROWS, BROWS), :]

    for n in range(SLOTS):
        dest_x, dest_y, goes_x, goes_y = moves(owner_ref, n, count_y, index_x, index_y)
        slot = slot_ref[n]

        @pl.when((dest_x == index_x) & (dest_y == index_y))
        def _():
            pltpu.make_async_copy(box_ref.at[pl.ds(n * BROWS, BROWS), :], into(slot), sems.at[slot]).start()

    for k, source in enumerate((first_ref, second_ref)):
        tag = tag_of(tagx_ref[k])

        @pl.when(tag >= 0)
        def _():
            slot = lax.rem(tag, SLOTS)
            for z in range(BZ):
                rows = pl.ds(pl.multiple_of(slot * BROWS + z * LROWS, 8), LROWS)
                pltpu.make_async_copy(
                    source.at[z, pl.ds(0, LROWS), :], state_ref.at[rows, :], sems.at[slot]
                ).start()

    for p in range(tagy_ref.shape[0]):
        tag = tag_of(tagy_ref[p])

        @pl.when((tag >= 0) & (tag // SLOTS == index_y))
        def _():
            slot = lax.rem(tag, SLOTS)
            pltpu.make_async_copy(ally_ref.at[p, pl.ds(0, BROWS), :], into(slot), sems.at[slot]).start()

    for slot in range(SLOTS):
        pltpu.make_async_copy(box_ref.at[pl.ds(0, BROWS), :], into(slot), sems.at[slot]).wait()

    def layer(index, carry):
        row = pl.multiple_of(index * LROWS, 8)
        for c in range(COMPS):
            put_x_faces(index, c, state_ref[pl.ds(row + c * 8, 8), :], xl_ref, xh_ref)
        return carry

    xl_ref[...] = jnp.zeros_like(xl_ref)
    xh_ref[...] = jnp.zeros_like(xh_ref)
    lax.fori_loop(0, LAYERS, layer, 0)
    put_y_faces(state_ref, yl_ref, yh_ref)


def power(value):
    return jnp.exp(0.7 * jnp.log(value))


def step_kernel(
    last, near_ref, diff_ref, stoi_ref, heat_ref, pre_ref, act_ref,
    state_ref, bx_ref, ax_ref, by_ref, ay_ref, *rest,
):
    if last:
        out_ref, coef_ref, gx_ref, ym_ref, yp_ref, new_ref = rest
    else:
        new_ref, xl_ref, xh_ref, yl_ref, yh_ref, coef_ref, gx_ref, ym_ref, yp_ref = rest
    lane = lanes()
    sub = sublanes()
    x_first = (lane & 31) == 0
    x_last = (lane & 31) == 31
    y_low_lanes = lane < 32
    y_high_lanes = lane >= 96
    sub_first = sub == 0
    sub_last = sub == 7

    def power_layer(index, carry):
        row = pl.multiple_of(index * LROWS, 8)
        coef_ref[pl.ds(pl.multiple_of(index * 8, 8), 8), :] = power(state_ref[pl.ds(row + TEMP * 8, 8), :])
        return carry

    lax.fori_loop(0, LAYERS, power_layer, 0)
    gx_ref[0] = power(bx_ref[TEMP * 8 :, :])
    gx_ref[1] = power(ax_ref[TEMP * 8 :, :])
    for c in range(COMPS + 1):
        if c < COMPS:
            below = by_ref[c * 8 : c * 8 + 8, :]
            above = ay_ref[c * 8 : c * 8 + 8, :]
        else:
            below = power(by_ref[TEMP * 8 :, :])
            above = power(ay_ref[TEMP * 8 :, :])
        for n in range(SLOTS):
            from_below = near_ref[n, 2]
            from_above = near_ref[n, 3]
            for half in range(2):
                rows = pl.ds((n * (COMPS + 1) + c) * BZ + half * 8, 8)
                ym_ref[rows, :] = roll(below, -32 * (2 * from_below + half), 1)
                yp_ref[rows, :] = roll(above, 96 - 32 * (2 * from_above + half), 1)
    if not last:
        xl_ref[...] = jnp.zeros_like(xl_ref)
        xh_ref[...] = jnp.zeros_like(xh_ref)

    def layer(index, carry):
        n = index // BZ
        z = index - n * BZ
        near_zm = near_ref[n, 4]
        near_zp = near_ref[n, 5]
        index_m = jnp.where(z == 0, jnp.where(near_zm < 0, index, near_zm * BZ + BZ - 1), index - 1)
        index_p = jnp.where(z == BZ - 1, jnp.where(near_zp < 0, index, near_zp * BZ), index + 1)
        shift_m = 128 - (near_ref[n, 0] * BZ + z)
        shift_p = 128 + 31 - (near_ref[n, 1] * BZ + z)

        def beside(value, face_m, face_p, y_row):
            xm = jnp.where(x_first, roll(face_m, shift_m, 1), roll(value, 1, 1))
            xp = jnp.where(x_last, roll(face_p, shift_p, 1), roll(value, -1, 1))
            down = roll(value, 32, 1)
            ghost = jnp.broadcast_to(ym_ref[pl.ds(y_row, 1), :], (8, 128))
            ym = jnp.where(y_low_lanes, jnp.where(sub_first, ghost, roll(down, 1, 0)), down)
            up = roll(value, -32, 1)
            ghost = jnp.broadcast_to(yp_ref[pl.ds(y_row, 1), :], (8, 128))
            yp = jnp.where(y_high_lanes, jnp.where(sub_last, ghost, roll(up, -1, 0)), up)
            return xm, xp, ym, yp

        def coef(at):
            return coef_ref[pl.ds(pl.multiple_of(at * 8, 8), 8), :]

        y_row = n * (COMPS + 1) * BZ + z
        center = coef(index)
        sides = beside(center, gx_ref[0], gx_ref[1], y_row + COMPS * BZ)
        weights = [0.5 * (center + side) for side in sides + (coef(index_m), coef(index_p))]
        total = functools.reduce(lambda a, b: a + b, weights)
        row = pl.multiple_of(index * LROWS, 8)
        row_m = pl.multiple_of(index_m * LROWS, 8)
        row_p = pl.multiple_of(index_p * LROWS, 8)
        rate = (
            pre_ref[0]
            * state_ref[pl.ds(row, 8), :]
            * state_ref[pl.ds(row + 8, 8), :]
            * jnp.exp(-act_ref[0] / state_ref[pl.ds(row + TEMP * 8, 8), :])
        )
        for c in range(COMPS):
            rows = slice(c * 8, c * 8 + 8)
            value = state_ref[pl.ds(row + c * 8, 8), :]
            sides = beside(value, bx_ref[rows, :], ax_ref[rows, :], y_row + c * BZ)
            sides = sides + (state_ref[pl.ds(row_m + c * 8, 8), :], state_ref[pl.ds(row_p + c * 8, 8), :])
            change = -total * value
            for weight, side in zip(weights, sides):
                change = change + weight * side
            value = value + diff_ref[c] * change
            if c < NSPEC:
                value = value + stoi_ref[c] * rate
            elif c == TEMP:
                value = value + heat_ref[0] * rate
            new_ref[pl.ds(row + c * 8, 8), :] = value
            if not last:
                put_x_faces(index, c, value, xl_ref, xh_ref)
        if last:
            for t in range(8):
                cells = pl.ds(pl.multiple_of(z * 1024 + t * 128, 128), 128)
                out_ref[n, :, cells] = new_ref[pl.ds(row + t, COMPS, stride=8), :]
        return carry

    lax.fori_loop(0, LAYERS, layer, 0)
    if not last:
        put_y_faces(new_ref, yl_ref, yh_ref)


def spec(space):
    return pl.BlockSpec(memory_space=space)


def struct(*shape, dtype=F32):
    return jax.ShapeDtypeStruct(shape, dtype)


PLANES = [struct(LROWS, 128)] * 4


def step(last, near, constants, state, planes):
    scratch = [
        VMEM((LAYERS * 8, 128), F32),
        VMEM((2, 8, 128), F32),
        VMEM((SLOTS * (COMPS + 1) * BZ, 128), F32),
        VMEM((SLOTS * (COMPS + 1) * BZ, 128), F32),
    ]
    if last:
        out_shape = struct(SLOTS, COMPS, BZ * BX * BX)
        out_specs = spec(VMEM)
        scratch.append(VMEM((ROWS, 128), F32))
    else:
        out_shape = [struct(ROWS, 128)] + PLANES
        out_specs = [spec(VMEM)] * 5
    return pl.pallas_call(
        functools.partial(step_kernel, last),
        out_shape=out_shape,
        in_specs=[spec(SMEM)] * 6 + [spec(VMEM)] * 5,
        out_specs=out_specs,
        scratch_shapes=scratch,
        compiler_params=PARAMS,
        cost_estimate=pl.CostEstimate(flops=20_000_000, bytes_accessed=4_000_000, transcendentals=0),
        name="step_last" if last else "step",
    )(near, *constants, state, *planes)


def shards(
    old_state,
    new_owner,
    new_slot,
    neighbours,
    diffusivity,
    stoichiometry,
    heat_release,
    prefactor,
    activation,
):
    count_x = lax.axis_size("gx")
    count_y = lax.axis_size("gy")
    boxes, outbox_x, outbox_y = pl.pallas_call(
        functools.partial(pack_kernel, count_y),
        out_shape=[struct(ROWS, 128), struct(BZ, PIECE, 128), struct(1, YBOX, 128)],
        in_specs=[spec(SMEM)] * 2 + [spec(VMEM)],
        out_specs=[spec(VMEM)] * 3,
        compiler_params=PARAMS,
        name="pack",
    )(new_owner, new_slot, old_state)
    all_y = lax.all_gather(outbox_y, "gy", axis=0, tiled=True)
    pieces = lax.all_to_all(outbox_x, "gx", 0, 0, tiled=True)
    first, second, more = pl.pallas_call(
        sort_kernel,
        out_shape=[struct(count_x, PIECE, 128)] * 2 + [struct(1, dtype=jnp.int32)],
        in_specs=[spec(VMEM)],
        out_specs=[spec(VMEM)] * 2 + [spec(SMEM)],
        scratch_shapes=[SMEM((count_x,), jnp.int32)],
        compiler_params=PARAMS,
        name="sort",
    )(pieces)
    first = lax.all_to_all(first, "gx", 0, 0, tiled=True)
    second = lax.cond(
        more[0] > 0,
        lambda value: lax.all_to_all(value, "gx", 0, 0, tiled=True),
        lambda value: value,
        second,
    )
    state, *planes = pl.pallas_call(
        functools.partial(place_kernel, count_y),
        out_shape=[struct(ROWS, 128)] + PLANES,
        in_specs=[spec(SMEM)] * 2 + [spec(pl.ANY)] * 4,
        out_specs=[spec(VMEM)] * 5,
        scratch_shapes=[
            VMEM((2, TAG, 128), F32),
            VMEM((count_y, TAG, 128), F32),
            pltpu.SemaphoreType.DMA((3,)),
            pltpu.SemaphoreType.DMA((SLOTS,)),
        ],
        compiler_params=PARAMS,
        name="place",
    )(new_owner, new_slot, boxes, first, second, all_y)
    constants = (diffusivity, stoichiometry, heat_release, prefactor, activation)
    for step_index in range(STEPS):
        x_low, x_high, y_low, y_high = planes
        received = (
            shifted(x_high, "gx", 1),
            shifted(x_low, "gx", -1),
            shifted(y_high, "gy", 1),
            shifted(y_low, "gy", -1),
        )
        if step_index < STEPS - 1:
            state, *planes = step(False, neighbours, constants, state, received)
        else:
            state = step(True, neighbours, constants, state, received)
    return state


def solution(mesh):
    return jax.shard_map(
        shards,
        mesh=mesh,
        in_specs=(
            P(("gx", "gy"), None, None),
            P(("gx", "gy")),
            P(("gx", "gy")),
            P(("gx", "gy"), None),
            P(),
            P(),
            P(),
            P(),
            P(),
        ),
        out_specs=P(("gx", "gy"), None, None),
        check_vma=False,
    )
```

time: 747 us -> 131 us (0.18); the launches traced: 739 us -> 131 us
  local copies, waits for them, and re-layouts: 386 us -> 4.98 us
  other arithmetic: 124 us -> 0 us
  waiting for transfers between devices: 69.9 us -> 6.63 us
  matrix products: 57.7 us -> 0 us
  Pallas kernels: 0 us -> 36.8 us
  blocking collectives: 58.4 us -> 41.1 us
    another operation x25 -> x0, local copies, waits for them, and re-layouts: 106 us -> none  [the longest x12 53.7 us: advance(): jnp.tile(ghost_ym, (1, 1, 1, BX))]
    reshape x32 -> x0, local copies, waits for them, and re-layouts: 105 us -> none  [the longest x6 39.4 us: advance(): jnp.repeat(ghost_xm, BX, axis=3)]
    slice x40 -> x0, local copies, waits for them, and re-layouts: 91.4 us -> none  [the longest x5 24.1 us: advance(): x_low = current[..., 0::BX].reshape(face_shape)]
    all_gather x2 -> x1, waiting for transfers between devices: 69.8 us -> 2.68 us  [shards(): all_y = lax.all_gather(outbox_y, 'gy', axis=0, tiled=True)]
    add x3 -> x0, other arithmetic: 62.3 us -> none  [advance(): current + change + source[None, :, None, None] * reaction_rate[:, None]]
    unnamed x2 -> x0, blocking collectives: 58.4 us -> none
    dot_general x25 -> x0, matrix products: 57.7 us -> none  [the longest x2 28.5 us: place(): return jnp.einsum('pt,pck->tck', selector, arrived, precision=PRECISE)]
    unnamed x17 -> x0, other arithmetic: 48.6 us -> none
  transfers between devices with their start and end apart: 14 -> 13, of which waited for: 2 -> 3; matrix products, arithmetic and copies ran while one was open for 37% -> 0% of each run, Pallas kernels for 0% -> 1%
where the time goes in v1:
time: 131 us
  blocking collectives  41.1 us (31%)
  Pallas kernels  36.8 us (28%)
  starting transfers between devices  25.1 us (19%)
  between operations  16.1 us (12%)
  waiting for transfers between devices  6.63 us (5%)
  local copies, waits for them, and re-layouts  4.98 us (4%)
    pallas_call x3, Pallas kernels, step(): pl.pallas_call(functools.partial(step_kernel, last), out_shape=out_shape,...  26 us
    ppermute x12, starting transfers between devices, shifted(): return lax.ppermute(value, axis, pairs)  25.1 us
    all_to_all x1, blocking collectives, shards(): pieces = lax.all_to_all(outbox_x, 'gx', 0, 0, tiled=True)  23.2 us
    all_to_all x1, blocking collectives, shards(): first = lax.all_to_all(first, 'gx', 0, 0, tiled=True)  17.9 us
    pallas_call x1, Pallas kernels, shards(): pl.pallas_call(functools.partial(place_kernel, count_y), out_shape=[struc...  7.24 us
    ppermute x12, waiting for transfers between devices, shifted(): return lax.ppermute(value, axis, pairs)  3.93 us
    all_gather x1, waiting for transfers between devices, shards(): all_y = lax.all_gather(outbox_y, 'gy', axis=0, tiled=True)  2.68 us
  transfers between devices with their start and end apart: 13, of which 3 were waited for; matrix products, arithmetic and copies ran while one was open for 0% of the time, Pallas kernels for 1%

profile of v1, /device:TPU:0, one launch (start us, length us, event | category | flops | bytes accessed | tf_op | source)
XLA Modules:
  0.0 130.7 jit_solution(2015174846629625510)
XLA Ops:
  6.5 0.0 copy-start.3
  6.5 0.0 copy-start.4
  6.5 0.0 all-gather.2.cloned.1.call-start
  6.5 2.5 %copy.12.old_ref = f32[2,13,16384]{2,1,0:T(8,128)S(1)} copy(f32[2,13,16384]{2,0,1:T(2,128)} %param.11) | data formatting | bytes 3407872 | tf_op args[0]
  9.0 0.0 copy-done.3
  9.0 0.0 copy-done.4
  9.0 2.1 %pack.1 = (f32[3328,128]{1,0:T(8,128)S(1)}, f32[16,112,128]{2,1,0:T(8,128)S(1)}, f32[1,1672,128]{2,1,0:T(8,128)}) custom-call(s32[2]{0:T(128)S(1)} %copy-done.3, s32[2]{0:T(128)S(1)} %copy-done.4, f32[2,13,16384]{2,1,0:T(8,128)S(1)} %copy.12.old_ref), custom_call_target="tpu_custom_call" | custom-call | tf_op jit(solution)/shard_map/pack/pallas_call | solution.py:378
  11.1 0.0 all-gather.2.cloned.1.call-update
  11.1 23.2 %all_to_all.15.pieces_ref = f32[16,112,128]{2,1,0:T(8,128)S(1)} all-to-all(f32[16,112,128]{2,1,0:T(8,128)S(1)} %get-tuple-element.32), channel_id=1, replica_groups=mesh['gx'=16,'gy'=8] {'gx'}, dimensions={0} | all-to-all | bytes 1835008 | tf_op jit(solution)/shard_map/all_to_all | solution.py:387
  34.4 1.4 %sort.1 = (f32[16,112,128]{2,1,0:T(8,128)S(1)}, f32[16,112,128]{2,1,0:T(8,128)}, s32[1]{0:T(128)}) custom-call(f32[16,112,128]{2,1,0:T(8,128)S(1)} %all_to_all.15.pieces_ref), custom_call_target="tpu_custom_call" | custom-call | tf_op jit(solution)/shard_map/sort/pallas_call | solution.py:388
  36.4 17.9 %all_to_all.16.first_ref = f32[16,112,128]{2,1,0:T(8,128)S(1)} all-to-all(f32[16,112,128]{2,1,0:T(8,128)S(1)} %get-tuple-element.33), channel_id=1, replica_groups=mesh['gx'=16,'gy'=8] {'gx'}, dimensions={0} | all-to-all | bytes 1835008 | tf_op jit(solution)/shard_map/all_to_all | solution.py:397
  54.3 2.7 %all-gather.2.cloned.1.call-done.ally_ref = f32[8,1672,128]{2,1,0:T(8,128)} async-done(((f32[1,1672,128]{2,1,0:T(8,128)}), f32[8,1672,128]{2,1,0:T(8,128)}) %all-gather.2.cloned.1.call-update) | async-done | bytes 6848528 | tf_op jit(solution)/shard_map/all_gather | solution.py:386
  57.0 0.0 copy-start
  57.0 0.0 copy-start.1
  57.0 0.0 copy-start.2
  57.0 7.2 %place.1 = (f32[3328,128]{1,0:T(8,128)S(1)}, f32[104,128]{1,0:T(8,128)S(1)}, f32[104,128]{1,0:T(8,128)S(1)}, f32[104,128]{1,0:T(8,128)S(1)}, f32[104,128]{1,0:T(8,128)S(1)}) custom-call(s32[2]{0:T(128)S(1)} %copy-done.3, s32[2]{0:T(128)S(1)} %copy-done.4, f32[3328,128]{1,0:T(8,128)S(1)} %get-tuple-element.31.box_ref, ...), custom_call_target="tpu_custom_call" | custom-call | tf_op jit(solution)/shard_map/place/pallas_call | solution.py:404
  64.3 1.6 %collective-permute-start = (f32[104,128]{1,0:T(8,128)S(1)}, f32[104,128]{1,0:T(8,128)S(1)}, u32[]{:S(2)}, u32[]{:S(2)}) collective-permute-start(f32[104,128]{1,0:T(8,128)S(1)} %get-tuple-element.38), channel_id=1, source_target_pairs={{0,8},{8,16},{16,24},{24,32},{32,40},{40,48},{48,56},{56,64},{64,7... | collective-permute-start | bytes 159752 | tf_op jit(solution)/shard_map/ppermute | solution.py:34
  65.9 3.8 %collective-permute-start.1 = (f32[104,128]{1,0:T(8,128)S(1)}, f32[104,128]{1,0:T(8,128)S(1)}, u32[]{:S(2)}, u32[]{:S(2)}) collective-permute-start(f32[104,128]{1,0:T(8,128)S(1)} %get-tuple-element.39), channel_id=1, source_target_pairs={{0,120},{8,0},{16,8},{24,16},{32,24},{40,32},{48,40},{56,48},{64,5... | collective-permute-start | bytes 159752 | tf_op jit(solution)/shard_map/ppermute | solution.py:34
  69.7 0.0 collective-permute-start.2
  69.7 3.0 %collective-permute-start.3 = (f32[104,128]{1,0:T(8,128)S(1)}, f32[104,128]{1,0:T(8,128)S(1)}, u32[]{:S(2)}, u32[]{:S(2)}) collective-permute-start(f32[104,128]{1,0:T(8,128)S(1)} %get-tuple-element.41), channel_id=1, source_target_pairs={{0,7},{1,0},{2,1},{3,2},{4,3},{5,4},{6,5},{7,6},{8,15},{9,8},{10,9... | collective-permute-start | bytes 159752 | tf_op jit(solution)/shard_map/ppermute | solution.py:34
  74.6 0.0 collective-permute-done.bx_ref
  74.6 0.0 collective-permute-done.1.ax_ref
  74.6 0.0 collective-permute-done.2.by_ref
  74.6 0.0 collective-permute-done.3.ay_ref
  74.6 0.0 copy-done
  74.6 0.0 copy-done.1
  74.7 0.0 copy-done.2
  74.7 9.3 %step.2 = (f32[3328,128]{1,0:T(8,128)S(1)}, f32[104,128]{1,0:T(8,128)S(1)}, f32[104,128]{1,0:T(8,128)S(1)}, f32[104,128]{1,0:T(8,128)S(1)}, f32[104,128]{1,0:T(8,128)S(1)}) custom-call(s32[2,6]{1,0:T(2,128)S(1)} %copy-done, f32[13]{0:T(128)S(1)} %copy-done.1, f32[9]{0:T(128)S(1)} %copy-done.2, f32[1]{0:T(128)S(6)} %copy.16.heat_ref, f32[1]{0:T(128)S(6)} %copy.17.pre_ref, ...), custom_call_target="tpu_custom_call" | custom-call | flops 20000000 | bytes 4000000 | tf_op jit(solution)/shard_map/step/pallas_call | solution.py:353
  84.0 0.1 collective-permute-start.4
  84.0 5.3 %collective-permute-start.5 = (f32[104,128]{1,0:T(8,128)S(1)}, f32[104,128]{1,0:T(8,128)S(1)}, u32[]{:S(2)}, u32[]{:S(2)}) collective-permute-start(f32[104,128]{1,0:T(8,128)S(1)} %get-tuple-element.44), channel_id=1, source_target_pairs={{0,120},{8,0},{16,8},{24,16},{32,24},{40,32},{48,40},{56,48},{64,5... | collective-permute-start | bytes 159752 | tf_op jit(solution)/shard_map/ppermute | solution.py:34
  89.4 0.0 collective-permute-start.6
  89.4 3.0 %collective-permute-start.7 = (f32[104,128]{1,0:T(8,128)S(1)}, f32[104,128]{1,0:T(8,128)S(1)}, u32[]{:S(2)}, u32[]{:S(2)}) collective-permute-start(f32[104,128]{1,0:T(8,128)S(1)} %get-tuple-element.46), channel_id=1, source_target_pairs={{0,7},{1,0},{2,1},{3,2},{4,3},{5,4},{6,5},{7,6},{8,15},{9,8},{10,9... | collective-permute-start | bytes 159752 | tf_op jit(solution)/shard_map/ppermute | solution.py:34
  92.3 0.0 collective-permute-done.4.bx_ref
  92.3 0.0 collective-permute-done.5.ax_ref
  92.3 1.8 %collective-permute-done.6.by_ref = f32[104,128]{1,0:T(8,128)S(1)} collective-permute-done((f32[104,128]{1,0:T(8,128)S(1)}, f32[104,128]{1,0:T(8,128)S(1)}, u32[]{:S(2)}, u32[]{:S(2)}) %collective-permute-start.6) | collective-permute-done | bytes 53280 | tf_op jit(solution)/shard_map/ppermute | solution.py:34
  94.1 0.0 collective-permute-done.7.ay_ref
  94.2 9.3 %step.3 = (f32[3328,128]{1,0:T(8,128)S(1)}, f32[104,128]{1,0:T(8,128)S(1)}, f32[104,128]{1,0:T(8,128)S(1)}, f32[104,128]{1,0:T(8,128)S(1)}, f32[104,128]{1,0:T(8,128)S(1)}) custom-call(s32[2,6]{1,0:T(2,128)S(1)} %copy-done, f32[13]{0:T(128)S(1)} %copy-done.1, f32[9]{0:T(128)S(1)} %copy-done.2, f32[1]{0:T(128)S(6)} %copy.16.heat_ref, f32[1]{0:T(128)S(6)} %copy.17.pre_ref, ...), custom_call_target="tpu_custom_call" | custom-call | flops 20000000 | bytes 4000000 | tf_op jit(solution)/shard_map/step/pallas_call | solution.py:353
  103.4 0.0 collective-permute-start.10
  103.5 3.0 %collective-permute-start.11 = (f32[104,128]{1,0:T(8,128)S(1)}, f32[104,128]{1,0:T(8,128)S(1)}, u32[]{:S(2)}, u32[]{:S(2)}) collective-permute-start(f32[104,128]{1,0:T(8,128)S(1)} %get-tuple-element.51), channel_id=1, source_target_pairs={{0,7},{1,0},{2,1},{3,2},{4,3},{5,4},{6,5},{7,6},{8,15},{9,8},{10,9... | collective-permute-start | bytes 159752 | tf_op jit(solution)/shard_map/ppermute | solution.py:34
  106.4 0.0 collective-permute-start.8
  106.4 5.3 %collective-permute-start.9 = (f32[104,128]{1,0:T(8,128)S(1)}, f32[104,128]{1,0:T(8,128)S(1)}, u32[]{:S(2)}, u32[]{:S(2)}) collective-permute-start(f32[104,128]{1,0:T(8,128)S(1)} %get-tuple-element.49), channel_id=1, source_target_pairs={{0,120},{8,0},{16,8},{24,16},{32,24},{40,32},{48,40},{56,48},{64,5... | collective-permute-start | bytes 159752 | tf_op jit(solution)/shard_map/ppermute | solution.py:34
  111.8 0.0 collective-permute-done.10.by_ref
  111.8 0.0 collective-permute-done.11.ay_ref
  111.8 2.1 %collective-permute-done.8.bx_ref = f32[104,128]{1,0:T(8,128)S(1)} collective-permute-done((f32[104,128]{1,0:T(8,128)S(1)}, f32[104,128]{1,0:T(8,128)S(1)}, u32[]{:S(2)}, u32[]{:S(2)}) %collective-permute-start.8) | collective-permute-done | bytes 53280 | tf_op jit(solution)/shard_map/ppermute | solution.py:34
  113.9 0.0 collective-permute-done.9.ax_ref
  113.9 7.5 %step_last.1 = f32[2,13,16384]{2,1,0:T(8,128)S(1)} custom-call(s32[2,6]{1,0:T(2,128)S(1)} %copy-done, f32[13]{0:T(128)S(1)} %copy-done.1, f32[9]{0:T(128)S(1)} %copy-done.2, f32[1]{0:T(128)S(6)} %copy.16.heat_ref, f32[1]{0:T(128)S(6)} %copy.17.pre_ref, f32[1]{0:T(128)S(6)} %copy.18.act_ref, f32[3328,128]{1,0:T(8,128)S(1)} %get-tuple-element.47.state_ref, ...), custom_call_target="tpu_custom_call" | custom-call | flops 20000000 | bytes 4000000 | tf_op jit(solution)/shard_map/step_last/pallas_call | solution.py:353
  121.4 2.5 %copy.13 = f32[2,13,16384]{2,0,1:T(2,128)} copy(f32[2,13,16384]{2,1,0:T(8,128)S(1)} %step_last.1) | data formatting | bytes 3407872 | tf_op jit(solution)/shard_map/step_last/pallas_call | solution.py:353
  (1 shorter events, 0.0 us)
Async XLA Ops:
  6.5 2.5 %copy-start.3 = (s32[2]{0:T(128)S(1)}, s32[2]{0:T(128)}, u32[]{:S(2)}) copy-start(s32[2]{0:T(128)} %owner_ref.3) | copy-start | bytes 28
  6.5 2.5 %copy-start.4 = (s32[2]{0:T(128)S(1)}, s32[2]{0:T(128)}, u32[]{:S(2)}) copy-start(s32[2]{0:T(128)} %slot_ref.3) | copy-start | bytes 28
  6.5 50.5 %all-gather.2.cloned.1.call-start = ((), (), s32[]{:S(2)}) async-start(), calls=%async_computation.3 | async-start | bytes 7704576 | tf_op jit(solution)/shard_map/all_gather | solution.py:386
  57.0 17.6 %copy-start = (s32[2,6]{1,0:T(2,128)S(1)}, s32[2,6]{1,0:T(2,128)}, u32[]{:S(2)}) copy-start(s32[2,6]{1,0:T(2,128)} %near_ref.5) | copy-start | bytes 148
  57.0 17.6 %copy-start.1 = (f32[13]{0:T(128)S(1)}, f32[13]{0:T(128)}, u32[]{:S(2)}) copy-start(f32[13]{0:T(128)} %diff_ref.5) | copy-start | bytes 160
  57.0 17.6 %copy-start.2 = (f32[9]{0:T(128)S(1)}, f32[9]{0:T(128)}, u32[]{:S(2)}) copy-start(f32[9]{0:T(128)} %stoi_ref.5) | copy-start | bytes 112
  64.3 10.3 %collective-permute-start = (f32[104,128]{1,0:T(8,128)S(1)}, f32[104,128]{1,0:T(8,128)S(1)}, u32[]{:S(2)}, u32[]{:S(2)}) collective-permute-start(f32[104,128]{1,0:T(8,128)S(1)} %get-tuple-element.38), channel_id=1, source_target_pairs={{0,8},{8,16},{16,24},{24,32},{32,40},{40,48},{48,56},{56,64},{64,7... | collective-permute-start | bytes 159752 | tf_op jit(solution)/shard_map/ppermute | solution.py:34
  65.9 8.7 %collective-permute-start.1 = (f32[104,128]{1,0:T(8,128)S(1)}, f32[104,128]{1,0:T(8,128)S(1)}, u32[]{:S(2)}, u32[]{:S(2)}) collective-permute-start(f32[104,128]{1,0:T(8,128)S(1)} %get-tuple-element.39), channel_id=1, source_target_pairs={{0,120},{8,0},{16,8},{24,16},{32,24},{40,32},{48,40},{56,48},{64,5... | collective-permute-start | bytes 159752 | tf_op jit(solution)/shard_map/ppermute | solution.py:34
  69.7 4.9 %collective-permute-start.2 = (f32[104,128]{1,0:T(8,128)S(1)}, f32[104,128]{1,0:T(8,128)S(1)}, u32[]{:S(2)}, u32[]{:S(2)}) collective-permute-start(f32[104,128]{1,0:T(8,128)S(1)} %get-tuple-element.40), channel_id=1, source_target_pairs={{0,1},{1,2},{2,3},{3,4},{4,5},{5,6},{6,7},{7,0},{8,9},{9,10},{10,1... | collective-permute-start | bytes 159752 | tf_op jit(solution)/shard_map/ppermute | solution.py:34
  69.7 4.9 %collective-permute-start.3 = (f32[104,128]{1,0:T(8,128)S(1)}, f32[104,128]{1,0:T(8,128)S(1)}, u32[]{:S(2)}, u32[]{:S(2)}) collective-permute-start(f32[104,128]{1,0:T(8,128)S(1)} %get-tuple-element.41), channel_id=1, source_target_pairs={{0,7},{1,0},{2,1},{3,2},{4,3},{5,4},{6,5},{7,6},{8,15},{9,8},{10,9... | collective-permute-start | bytes 159752 | tf_op jit(solution)/shard_map/ppermute | solution.py:34
  84.0 8.4 %collective-permute-start.4 = (f32[104,128]{1,0:T(8,128)S(1)}, f32[104,128]{1,0:T(8,128)S(1)}, u32[]{:S(2)}, u32[]{:S(2)}) collective-permute-start(f32[104,128]{1,0:T(8,128)S(1)} %get-tuple-element.43), channel_id=1, source_target_pairs={{0,8},{8,16},{16,24},{24,32},{32,40},{40,48},{48,56},{56,64},{64,7... | collective-permute-start | bytes 159752 | tf_op jit(solution)/shard_map/ppermute | solution.py:34
  84.0 8.3 %collective-permute-start.5 = (f32[104,128]{1,0:T(8,128)S(1)}, f32[104,128]{1,0:T(8,128)S(1)}, u32[]{:S(2)}, u32[]{:S(2)}) collective-permute-start(f32[104,128]{1,0:T(8,128)S(1)} %get-tuple-element.44), channel_id=1, source_target_pairs={{0,120},{8,0},{16,8},{24,16},{32,24},{40,32},{48,40},{56,48},{64,5... | collective-permute-start | bytes 159752 | tf_op jit(solution)/shard_map/ppermute | solution.py:34
  89.4 4.8 %collective-permute-start.6 = (f32[104,128]{1,0:T(8,128)S(1)}, f32[104,128]{1,0:T(8,128)S(1)}, u32[]{:S(2)}, u32[]{:S(2)}) collective-permute-start(f32[104,128]{1,0:T(8,128)S(1)} %get-tuple-element.45), channel_id=1, source_target_pairs={{0,1},{1,2},{2,3},{3,4},{4,5},{5,6},{6,7},{7,0},{8,9},{9,10},{10,1... | collective-permute-start | bytes 159752 | tf_op jit(solution)/shard_map/ppermute | solution.py:34
  89.4 4.8 %collective-permute-start.7 = (f32[104,128]{1,0:T(8,128)S(1)}, f32[104,128]{1,0:T(8,128)S(1)}, u32[]{:S(2)}, u32[]{:S(2)}) collective-permute-start(f32[104,128]{1,0:T(8,128)S(1)} %get-tuple-element.46), channel_id=1, source_target_pairs={{0,7},{1,0},{2,1},{3,2},{4,3},{5,4},{6,5},{7,6},{8,15},{9,8},{10,9... | collective-permute-start | bytes 159752 | tf_op jit(solution)/shard_map/ppermute | solution.py:34
  103.4 8.3 %collective-permute-start.10 = (f32[104,128]{1,0:T(8,128)S(1)}, f32[104,128]{1,0:T(8,128)S(1)}, u32[]{:S(2)}, u32[]{:S(2)}) collective-permute-start(f32[104,128]{1,0:T(8,128)S(1)} %get-tuple-element.50), channel_id=1, source_target_pairs={{0,1},{1,2},{2,3},{3,4},{4,5},{5,6},{6,7},{7,0},{8,9},{9,10},{10,1... | collective-permute-start | bytes 159752 | tf_op jit(solution)/shard_map/ppermute | solution.py:34
  103.5 8.3 %collective-permute-start.11 = (f32[104,128]{1,0:T(8,128)S(1)}, f32[104,128]{1,0:T(8,128)S(1)}, u32[]{:S(2)}, u32[]{:S(2)}) collective-permute-start(f32[104,128]{1,0:T(8,128)S(1)} %get-tuple-element.51), channel_id=1, source_target_pairs={{0,7},{1,0},{2,1},{3,2},{4,3},{5,4},{6,5},{7,6},{8,15},{9,8},{10,9... | collective-permute-start | bytes 159752 | tf_op jit(solution)/shard_map/ppermute | solution.py:34
  106.4 7.5 %collective-permute-start.8 = (f32[104,128]{1,0:T(8,128)S(1)}, f32[104,128]{1,0:T(8,128)S(1)}, u32[]{:S(2)}, u32[]{:S(2)}) collective-permute-start(f32[104,128]{1,0:T(8,128)S(1)} %get-tuple-element.48), channel_id=1, source_target_pairs={{0,8},{8,16},{16,24},{24,32},{32,40},{40,48},{48,56},{56,64},{64,7... | collective-permute-start | bytes 159752 | tf_op jit(solution)/shard_map/ppermute | solution.py:34
  106.4 7.5 %collective-permute-start.9 = (f32[104,128]{1,0:T(8,128)S(1)}, f32[104,128]{1,0:T(8,128)S(1)}, u32[]{:S(2)}, u32[]{:S(2)}) collective-permute-start(f32[104,128]{1,0:T(8,128)S(1)} %get-tuple-element.49), channel_id=1, source_target_pairs={{0,120},{8,0},{16,8},{24,16},{32,24},{40,32},{48,40},{56,48},{64,5... | collective-permute-start | bytes 159752 | tf_op jit(solution)/shard_map/ppermute | solution.py:34
Sparse Core Ops, SparseCore 0:
  11.3 45.7 all-gather.1

commit v2 on v1

--- a/solution.py
+++ b/solution.py
@@ -28,9 +28,11 @@
 PARAMS = pltpu.CompilerParams(vmem_limit_bytes=48 * 1024 * 1024)
 
 
-def shifted(value, axis, steps):
+def swapped(value, axis, first):
     count = lax.axis_size(axis)
-    pairs = [(source, (source + steps) % count) for source in range(count)]
+    pairs = []
+    for low in range(first, count + first, 2):
+        pairs += [(low % count, (low + 1) % count), ((low + 1) % count, low % count)]
     return lax.ppermute(value, axis, pairs)
 
 
@@ -43,19 +45,13 @@
     return dest_x, dest_y, goes_x, goes_y
 
 
+def source_rows(n, z, c):
+    return pl.ds(c * 256 + z * 16 + n, 8, stride=2)
+
+
 def pack_kernel(count_y, owner_ref, slot_ref, old_ref, box_ref, outx_ref, outy_ref):
     index_x = lax.axis_index("gx")
     index_y = lax.axis_index("gy")
-
-    def layer(z, carry):
-        for n in range(SLOTS):
-            row = pl.multiple_of(n * BROWS + z * LROWS, 8)
-            for t in range(8):
-                cells = pl.ds(pl.multiple_of(z * 1024 + t * 128, 128), 128)
-                box_ref[pl.ds(row + t, COMPS, stride=8), :] = old_ref[n, :, cells]
-        return carry
-
-    lax.fori_loop(0, BZ, layer, 0)
     row_x = jnp.int32(0)
     row_y = jnp.int32(0)
     tag_x = jnp.int32(-1)
@@ -67,15 +63,17 @@
         tag_x = jnp.where(goes_x, dest_x * SLOTS + slot_ref[n], tag_x)
         tag_y = jnp.where(goes_y, dest_y * SLOTS + slot_ref[n], tag_y)
 
-    def copy(z, carry):
-        source_x = pl.ds(pl.multiple_of(row_x * BROWS + z * LROWS, 8), LROWS)
-        source_y = pl.ds(pl.multiple_of(row_y * BROWS + z * LROWS, 8), LROWS)
-        outx_ref[z, :LROWS, :] = box_ref[source_x, :]
+    def layer(z, carry):
+        row = pl.multiple_of(z * LROWS, 8)
+        for c in range(COMPS):
+            for n in range(SLOTS):
+                box_ref[pl.ds(n * BROWS + row + c * 8, 8), :] = old_ref[source_rows(n, z, c), :]
+            outx_ref[z, c * 8 : c * 8 + 8, :] = old_ref[source_rows(row_x, z, c), :]
+            outy_ref[0, pl.ds(row + c * 8, 8), :] = old_ref[source_rows(row_y, z, c), :]
         outx_ref[z, LROWS:, :] = jnp.full((TAG, 128), tag_x, jnp.int32).astype(F32)
-        outy_ref[0, pl.ds(pl.multiple_of(z * LROWS, 8), LROWS), :] = box_ref[source_y, :]
         return carry
 
-    lax.fori_loop(0, BZ, copy, 0)
+    lax.fori_loop(0, BZ, layer, 0)
     outy_ref[0, BROWS:, :] = jnp.full((TAG, 128), tag_y, jnp.int32).astype(F32)
 
 
@@ -126,34 +124,56 @@
     return lax.broadcasted_iota(jnp.int32, (8, 128), 0)
 
 
-def put_x_faces(layer_index, c, value, low_ref, high_ref):
-    here = (lanes() & 31) == layer_index
-    rows = pl.ds(c * 8, 8)
-    low_ref[rows, :] = jnp.where(here, roll(value, layer_index, 1), low_ref[rows, :])
-    high_ref[rows, :] = jnp.where(here, roll(value, layer_index - 31, 1), high_ref[rows, :])
-
-
-def put_y_faces(state_ref, low_ref, high_ref):
-    group = lanes() >> 5
-
-    for c in range(COMPS):
+def tile(row):
+    return pl.ds(pl.multiple_of(row, 8), 8)
+
+
+def put_faces(state_ref, out_refs):
+    lane = lanes()
+    ends = ((lane & 31) == 0) | ((lane & 31) == 31)
+    even = (lane & 1) == 0
+    group = lane >> 5
+    even_x = lax.rem(lax.axis_index("gx"), 2) == 0
+    even_y = lax.rem(lax.axis_index("gy"), 2) == 0
+    xa_ref, xb_ref, ya_ref, yb_ref = out_refs
+
+    def plane(c, carry):
+        first = pl.multiple_of(c * 8, 8)
+        rows = pl.ds(first, 8)
+        both = []
+        for n in range(SLOTS):
+            parts = [
+                roll(jnp.where(ends, state_ref[tile(first + (n * BZ + z) * LROWS), :], 0.0), 2 * z, 1)
+                for z in range(BZ)
+            ]
+            while len(parts) > 1:
+                parts = [a + b for a, b in zip(parts[::2], parts[1::2])]
+            both.append(parts[0])
+        other = roll(both[1], 1, 1)
+        low = jnp.where(even, both[0], other)
+        high = jnp.where(even, other, both[0])
+        xa_ref[rows, :] = jnp.where(even_x, high, low)
+        xb_ref[rows, :] = jnp.where(even_x, low, high)
         low = jnp.zeros((8, 128), F32)
         high = jnp.zeros((8, 128), F32)
         for n in range(SLOTS):
             for half in range(2):
                 where = 2 * n + half
-                base = n * BROWS + half * 8 * LROWS + c * 8
+                base = n * BROWS + half * 8 * LROWS + first
                 bottom = state_ref[pl.ds(base, 8, stride=LROWS), :]
                 top = state_ref[pl.ds(base + 7, 8, stride=LROWS), :]
                 low = jnp.where(group == where, roll(bottom, 32 * where, 1), low)
                 high = jnp.where(group == where, roll(top, 32 * where - 96, 1), high)
-        low_ref[c * 8 : c * 8 + 8, :] = low
-        high_ref[c * 8 : c * 8 + 8, :] = high
+        ya_ref[rows, :] = jnp.where(even_y, high, low)
+        yb_ref[rows, :] = jnp.where(even_y, low, high)
+        return carry
+
+    lax.fori_loop(0, COMPS, plane, 0)
 
 
 def place_kernel(
     count_y, owner_ref, slot_ref, box_ref, first_ref, second_ref, ally_ref,
-    state_ref, xl_ref, xh_ref, yl_ref, yh_ref, tagx_ref, tagy_ref, tag_sem, sems,
+    state_ref, xa_ref, xb_ref, ya_ref, yb_ref, tagx_ref, tagy_ref, tag_sem, sems,
 ):
     index_x = lax.axis_index("gx")
     index_y = lax.axis_index("gy")
@@ -201,78 +221,82 @@
     for slot in range(SLOTS):
         pltpu.make_async_copy(box_ref.at[pl.ds(0, BROWS), :], into(slot), sems.at[slot]).wait()
 
-    def layer(index, carry):
-        row = pl.multiple_of(index * LROWS, 8)
-        for c in range(COMPS):
-            put_x_faces(index, c, state_ref[pl.ds(row + c * 8, 8), :], xl_ref, xh_ref)
-        return carry
-
-    xl_ref[...] = jnp.zeros_like(xl_ref)
-    xh_ref[...] = jnp.zeros_like(xh_ref)
-    lax.fori_loop(0, LAYERS, layer, 0)
-    put_y_faces(state_ref, yl_ref, yh_ref)
+    put_faces(state_ref, (xa_ref, xb_ref, ya_ref, yb_ref))
 
 
 def power(value):
     return jnp.exp(0.7 * jnp.log(value))
 
 
+UNROLL = 4
+
+
 def step_kernel(
     last, near_ref, diff_ref, stoi_ref, heat_ref, pre_ref, act_ref,
-    state_ref, bx_ref, ax_ref, by_ref, ay_ref, *rest,
+    state_ref, xa_ref, xb_ref, ya_ref, yb_ref, *rest,
 ):
     if last:
-        out_ref, coef_ref, gx_ref, ym_ref, yp_ref, new_ref = rest
+        new_ref, coef_ref, gx_ref, ym_ref, yp_ref = rest
     else:
-        new_ref, xl_ref, xh_ref, yl_ref, yh_ref, coef_ref, gx_ref, ym_ref, yp_ref = rest
+        new_ref, *out_refs, coef_ref, gx_ref, ym_ref, yp_ref = rest
     lane = lanes()
     sub = sublanes()
+    even = (lane & 1) == 0
     x_first = (lane & 31) == 0
     x_last = (lane & 31) == 31
     y_low_lanes = lane < 32
     y_high_lanes = lane >= 96
     sub_first = sub == 0
     sub_last = sub == 7
-
-    def power_layer(index, carry):
-        row = pl.multiple_of(index * LROWS, 8)
-        coef_ref[pl.ds(pl.multiple_of(index * 8, 8), 8), :] = power(state_ref[pl.ds(row + TEMP * 8, 8), :])
+    even_x = lax.rem(lax.axis_index("gx"), 2) == 0
+    even_y = lax.rem(lax.axis_index("gy"), 2) == 0
+
+    def power_layer(block, carry):
+        for u in range(8):
+            index = block * 8 + u
+            coef_ref[tile(index * 8), :] = power(state_ref[tile(index * LROWS + TEMP * 8), :])
         return carry
 
-    lax.fori_loop(0, LAYERS, power_layer, 0)
-    gx_ref[0] = power(bx_ref[TEMP * 8 :, :])
-    gx_ref[1] = power(ax_ref[TEMP * 8 :, :])
-    for c in range(COMPS + 1):
-        if c < COMPS:
-            below = by_ref[c * 8 : c * 8 + 8, :]
-            above = ay_ref[c * 8 : c * 8 + 8, :]
-        else:
-            below = power(by_ref[TEMP * 8 :, :])
-            above = power(ay_ref[TEMP * 8 :, :])
+    lax.fori_loop(0, LAYERS // 8, power_layer, 0)
+    for c in range(COMPS):
+        rows = slice(c * 8, c * 8 + 8)
+        pair_a, pair_b = xa_ref[rows, :], xb_ref[rows, :]
+        below = jnp.where(even_x, pair_b, pair_a)
+        above = jnp.where(even_x, pair_a, pair_b)
         for n in range(SLOTS):
-            from_below = near_ref[n, 2]
-            from_above = near_ref[n, 3]
+            ghost = jnp.where(
+                even, roll(below, -31 - near_ref[n, 0], 1), roll(above, 31 - near_ref[n, 1], 1)
+            )
+            gx_ref[n * (COMPS + 1) + c] = ghost
+            if c == TEMP:
+                gx_ref[n * (COMPS + 1) + COMPS] = power(ghost)
+        pair_a, pair_b = ya_ref[rows, :], yb_ref[rows, :]
+        below = jnp.where(even_y, pair_b, pair_a)
+        above = jnp.where(even_y, pair_a, pair_b)
+        for n in range(SLOTS):
             for half in range(2):
-                rows = pl.ds((n * (COMPS + 1) + c) * BZ + half * 8, 8)
-                ym_ref[rows, :] = roll(below, -32 * (2 * from_below + half), 1)
-                yp_ref[rows, :] = roll(above, 96 - 32 * (2 * from_above + half), 1)
-    if not last:
-        xl_ref[...] = jnp.zeros_like(xl_ref)
-        xh_ref[...] = jnp.zeros_like(xh_ref)
-
-    def layer(index, carry):
-        n = index // BZ
-        z = index - n * BZ
+                ghost_m = roll(below, -32 * (2 * near_ref[n, 2] + half), 1)
+                ghost_p = roll(above, 96 - 32 * (2 * near_ref[n, 3] + half), 1)
+                at = (n * (COMPS + 1) + c) * BZ + half * 8
+                ym_ref[pl.ds(at, 8), :] = ghost_m
+                yp_ref[pl.ds(at, 8), :] = ghost_p
+                if c == TEMP:
+                    ym_ref[pl.ds(at + BZ, 8), :] = power(ghost_m)
+                    yp_ref[pl.ds(at + BZ, 8), :] = power(ghost_p)
+
+    def layer(n, z):
+        index = n * BZ + z
         near_zm = near_ref[n, 4]
         near_zp = near_ref[n, 5]
         index_m = jnp.where(z == 0, jnp.where(near_zm < 0, index, near_zm * BZ + BZ - 1), index - 1)
         index_p = jnp.where(z == BZ - 1, jnp.where(near_zp < 0, index, near_zp * BZ), index + 1)
-        shift_m = 128 - (near_ref[n, 0] * BZ + z)
-        shift_p = 128 + 31 - (near_ref[n, 1] * BZ + z)
-
-        def beside(value, face_m, face_p, y_row):
-            xm = jnp.where(x_first, roll(face_m, shift_m, 1), roll(value, 1, 1))
-            xp = jnp.where(x_last, roll(face_p, shift_p, 1), roll(value, -1, 1))
+        shift = 128 - 2 * z
+
+        def beside(value, c):
+            ghost = roll(gx_ref[n * (COMPS + 1) + c], shift, 1)
+            xm = jnp.where(x_first, ghost, roll(value, 1, 1))
+            xp = jnp.where(x_last, ghost, roll(value, -1, 1))
+            y_row = (n * (COMPS + 1) + c) * BZ + z
             down = roll(value, 32, 1)
             ghost = jnp.broadcast_to(ym_ref[pl.ds(y_row, 1), :], (8, 128))
             ym = jnp.where(y_low_lanes, jnp.where(sub_first, ghost, roll(down, 1, 0)), down)
@@ -281,13 +305,9 @@
             yp = jnp.where(y_high_lanes, jnp.where(sub_last, ghost, roll(up, -1, 0)), up)
             return xm, xp, ym, yp
 
-        def coef(at):
-            return coef_ref[pl.ds(pl.multiple_of(at * 8, 8), 8), :]
-
-        y_row = n * (COMPS + 1) * BZ + z
-        center = coef(index)
-        sides = beside(center, gx_ref[0], gx_ref[1], y_row + COMPS * BZ)
-        weights = [0.5 * (center + side) for side in sides + (coef(index_m), coef(index_p))]
+        center = coef_ref[tile(index * 8), :]
+        sides = beside(center, COMPS) + (coef_ref[tile(index_m * 8), :], coef_ref[tile(index_p * 8), :])
+        weights = [0.5 * (center + side) for side in sides]
         total = functools.reduce(lambda a, b: a + b, weights)
         row = pl.multiple_of(index * LROWS, 8)
         row_m = pl.multiple_of(index_m * LROWS, 8)
@@ -299,9 +319,8 @@
             * jnp.exp(-act_ref[0] / state_ref[pl.ds(row + TEMP * 8, 8), :])
         )
         for c in range(COMPS):
-            rows = slice(c * 8, c * 8 + 8)
             value = state_ref[pl.ds(row + c * 8, 8), :]
-            sides = beside(value, bx_ref[rows, :], ax_ref[rows, :], y_row + c * BZ)
+            sides = beside(value, c)
             sides = sides + (state_ref[pl.ds(row_m + c * 8, 8), :], state_ref[pl.ds(row_p + c * 8, 8), :])
             change = -total * value
             for weight, side in zip(weights, sides):
@@ -311,18 +330,21 @@
                 value = value + stoi_ref[c] * rate
             elif c == TEMP:
                 value = value + heat_ref[0] * rate
-            new_ref[pl.ds(row + c * 8, 8), :] = value
-            if not last:
-                put_x_faces(index, c, value, xl_ref, xh_ref)
-        if last:
-            for t in range(8):
-                cells = pl.ds(pl.multiple_of(z * 1024 + t * 128, 128), 128)
-                out_ref[n, :, cells] = new_ref[pl.ds(row + t, COMPS, stride=8), :]
+            if last:
+                new_ref[source_rows(n, z, c), :] = value
+            else:
+                new_ref[pl.ds(row + c * 8, 8), :] = value
+
+    def layers(block, carry):
+        n = block // (BZ // UNROLL)
+        z = (block - n * (BZ // UNROLL)) * UNROLL
+        for u in range(UNROLL):
+            layer(n, z + u)
         return carry
 
-    lax.fori_loop(0, LAYERS, layer, 0)
+    lax.fori_loop(0, LAYERS // UNROLL, layers, 0)
     if not last:
-        put_y_faces(new_ref, yl_ref, yh_ref)
+        put_faces(new_ref, out_refs)
 
 
 def spec(space):
@@ -337,16 +359,9 @@
 
 
 def step(last, near, constants, state, planes):
-    scratch = [
-        VMEM((LAYERS * 8, 128), F32),
-        VMEM((2, 8, 128), F32),
-        VMEM((SLOTS * (COMPS + 1) * BZ, 128), F32),
-        VMEM((SLOTS * (COMPS + 1) * BZ, 128), F32),
-    ]
     if last:
-        out_shape = struct(SLOTS, COMPS, BZ * BX * BX)
+        out_shape = struct(ROWS, 128)
         out_specs = spec(VMEM)
-        scratch.append(VMEM((ROWS, 128), F32))
     else:
         out_shape = [struct(ROWS, 128)] + PLANES
         out_specs = [spec(VMEM)] * 5
@@ -355,7 +370,12 @@
         out_shape=out_shape,
         in_specs=[spec(SMEM)] * 6 + [spec(VMEM)] * 5,
         out_specs=out_specs,
-        scratch_shapes=scratch,
+        scratch_shapes=[
+            VMEM((LAYERS * 8, 128), F32),
+            VMEM((SLOTS * (COMPS + 1), 8, 128), F32),
+            VMEM((SLOTS * (COMPS + 1) * BZ, 128), F32),
+            VMEM((SLOTS * (COMPS + 1) * BZ, 128), F32),
+        ],
         compiler_params=PARAMS,
         cost_estimate=pl.CostEstimate(flops=20_000_000, bytes_accessed=4_000_000, transcendentals=0),
         name="step_last" if last else "step",
@@ -375,6 +395,7 @@
 ):
     count_x = lax.axis_size("gx")
     count_y = lax.axis_size("gy")
+    old_rows = old_state.reshape(SLOTS, COMPS, 128, 128).transpose(1, 2, 0, 3).reshape(ROWS, 128)
     boxes, outbox_x, outbox_y = pl.pallas_call(
         functools.partial(pack_kernel, count_y),
         out_shape=[struct(ROWS, 128), struct(BZ, PIECE, 128), struct(1, YBOX, 128)],
@@ -382,7 +403,7 @@
         out_specs=[spec(VMEM)] * 3,
         compiler_params=PARAMS,
         name="pack",
-    )(new_owner, new_slot, old_state)
+    )(new_owner, new_slot, old_rows)
     all_y = lax.all_gather(outbox_y, "gy", axis=0, tiled=True)
     pieces = lax.all_to_all(outbox_x, "gx", 0, 0, tiled=True)
     first, second, more = pl.pallas_call(
@@ -417,18 +438,13 @@
     )(new_owner, new_slot, boxes, first, second, all_y)
     constants = (diffusivity, stoichiometry, heat_release, prefactor, activation)
     for step_index in range(STEPS):
-        x_low, x_high, y_low, y_high = planes
-        received = (
-            shifted(x_high, "gx", 1),
-            shifted(x_low, "gx", -1),
-            shifted(y_high, "gy", 1),
-            shifted(y_low, "gy", -1),
-        )
+        x_a, x_b, y_a, y_b = planes
+        received = (swapped(x_a, "gx", 0), swapped(x_b, "gx", 1), swapped(y_a, "gy", 0), swapped(y_b, "gy", 1))
         if step_index < STEPS - 1:
             state, *planes = step(False, neighbours, constants, state, received)
         else:
             state = step(True, neighbours, constants, state, received)
-    return state
+    return state.reshape(COMPS, 128, SLOTS, 128).transpose(2, 0, 1, 3).reshape(SLOTS, COMPS, BZ * BX * BX)
 
 
 def solution(mesh):

time: 131 us -> 113 us (0.86)
  starting transfers between devices: 25.1 us -> 11.1 us
  Pallas kernels: 36.8 us -> 26.5 us
  waiting for transfers between devices: 6.63 us -> 15 us
  local copies, waits for them, and re-layouts: 4.98 us -> 2.79 us
    ppermute x12, starting transfers between devices: 25.1 us -> 11.1 us  [swapped(): return lax.ppermute(value, axis, pairs)]
    pallas_call x3, Pallas kernels: 26 us -> 17.2 us  [step(): pl.pallas_call(functools.partial(step_kernel, last), out_shape=out_shape,...]
    ppermute x12, waiting for transfers between devices: 3.93 us -> 12.3 us  [swapped(): return lax.ppermute(value, axis, pairs)]
    pallas_call x1 -> x0, local copies, waits for them, and re-layouts: 2.5 us -> none  [step(): pl.pallas_call(functools.partial(step_kernel, last), out_shape=out_shape,...]
    unnamed x11 -> x16, local copies, waits for them, and re-layouts: 2.48 us -> 2.79 us
  transfers between devices with their start and end apart: 13 -> 13, of which waited for: 3 -> 7; matrix products, arithmetic and copies ran while one was open for 0% -> 0% of each run, Pallas kernels for 1% -> 1%
where the time goes in v2:
time: 113 us
  blocking collectives  41.2 us (36%)
  Pallas kernels  26.5 us (23%)
  between operations  16 us (14%)
  waiting for transfers between devices  15 us (13%)
  starting transfers between devices  11.1 us (10%)
  local copies, waits for them, and re-layouts  2.79 us (2%)
    all_to_all x1, blocking collectives, shards(): pieces = lax.all_to_all(outbox_x, 'gx', 0, 0, tiled=True)  23.2 us
    all_to_all x1, blocking collectives, shards(): first = lax.all_to_all(first, 'gx', 0, 0, tiled=True)  18 us
    pallas_call x3, Pallas kernels, step(): pl.pallas_call(functools.partial(step_kernel, last), out_shape=out_shape,...  17.2 us
    ppermute x12, waiting for transfers between devices, swapped(): return lax.ppermute(value, axis, pairs)  12.3 us
    ppermute x12, starting transfers between devices, swapped(): return lax.ppermute(value, axis, pairs)  11.1 us
    pallas_call x1, Pallas kernels, shards(): pl.pallas_call(functools.partial(place_kernel, count_y), out_shape=[struc...  5.96 us
    unnamed x16, local copies, waits for them, and re-layouts  2.79 us
    all_gather x1, waiting for transfers between devices, shards(): all_y = lax.all_gather(outbox_y, 'gy', axis=0, tiled=True)  2.69 us
  transfers between devices with their start and end apart: 13, of which 7 were waited for; matrix products, arithmetic and copies ran while one was open for 0% of the time, Pallas kernels for 1%

profile of v2, /device:TPU:0, one launch (start us, length us, event | category | flops | bytes accessed | tf_op | source)
XLA Modules:
  0.0 112.6 jit_solution(3020715806168688605)
XLA Ops:
  6.5 0.0 all-gather.2.cloned.1.call-start
  6.5 0.0 copy-start
  6.5 1.5 %copy-done = f32[2,13,16384]{2,0,1:T(2,128)S(1)} copy-done((f32[2,13,16384]{2,0,1:T(2,128)S(1)}, f32[2,13,16384]{2,0,1:T(2,128)}, u32[]{:S(2)}) %copy-start) | copy-done | bytes 1703960
  8.0 0.0 copy-start.4
  8.0 0.7 copy-done.4
  8.6 0.0 copy-start.6
  8.6 0.7 copy-done.6
  9.3 1.9 %pack.1 = (f32[3328,128]{1,0:T(8,128)S(1)}, f32[16,112,128]{2,1,0:T(8,128)S(1)}, f32[1,1672,128]{2,1,0:T(8,128)}) custom-call(s32[2]{0:T(128)S(1)} %copy-done.4, s32[2]{0:T(128)S(1)} %copy-done.6, f32[3328,128]{1,0:T(8,128)S(1)} %bitcast.11), custom_call_target="tpu_custom_call" | custom-call | tf_op jit(solution)/shard_map/pack/pallas_call | solution.py:399
  11.2 0.0 all-gather.2.cloned.1.call-update
  11.2 23.2 %all_to_all.15.pieces_ref = f32[16,112,128]{2,1,0:T(8,128)S(1)} all-to-all(f32[16,112,128]{2,1,0:T(8,128)S(1)} %get-tuple-element.32), channel_id=1, replica_groups=mesh['gx'=16,'gy'=8] {'gx'}, dimensions={0} | all-to-all | bytes 1835008 | tf_op jit(solution)/shard_map/all_to_all | solution.py:408
  34.4 1.4 %sort.1 = (f32[16,112,128]{2,1,0:T(8,128)S(1)}, f32[16,112,128]{2,1,0:T(8,128)}, s32[1]{0:T(128)}) custom-call(f32[16,112,128]{2,1,0:T(8,128)S(1)} %all_to_all.15.pieces_ref), custom_call_target="tpu_custom_call" | custom-call | tf_op jit(solution)/shard_map/sort/pallas_call | solution.py:409
  36.4 0.0 copy-start.5
  36.4 0.0 copy-start.7
  36.4 18.0 %all_to_all.16.first_ref = f32[16,112,128]{2,1,0:T(8,128)S(1)} all-to-all(f32[16,112,128]{2,1,0:T(8,128)S(1)} %get-tuple-element.33), channel_id=1, replica_groups=mesh['gx'=16,'gy'=8] {'gx'}, dimensions={0} | all-to-all | bytes 1835008 | tf_op jit(solution)/shard_map/all_to_all | solution.py:418
  54.4 2.7 %all-gather.2.cloned.1.call-done.ally_ref = f32[8,1672,128]{2,1,0:T(8,128)} async-done(((f32[1,1672,128]{2,1,0:T(8,128)}), f32[8,1672,128]{2,1,0:T(8,128)}) %all-gather.2.cloned.1.call-update) | async-done | bytes 6848528 | tf_op jit(solution)/shard_map/all_gather | solution.py:407
  57.1 0.0 copy-done.5
  57.1 0.0 copy-done.7
  57.1 0.0 copy-start.1
  57.1 0.0 copy-start.2
  57.1 0.0 copy-start.3
  57.1 6.0 %place.1 = (f32[3328,128]{1,0:T(8,128)S(1)}, f32[104,128]{1,0:T(8,128)S(1)}, f32[104,128]{1,0:T(8,128)S(1)}, f32[104,128]{1,0:T(8,128)S(1)}, f32[104,128]{1,0:T(8,128)S(1)}) custom-call(s32[2]{0:T(128)S(1)} %copy-done.5, s32[2]{0:T(128)S(1)} %copy-done.7, f32[3328,128]{1,0:T(8,128)S(1)} %get-tuple-element.31.box_ref, ...), custom_call_target="tpu_custom_call" | custom-call | tf_op jit(solution)/shard_map/place/pallas_call | solution.py:425
  63.1 0.7 collective-permute-start
  63.7 4.6 %collective-permute-start.1 = (f32[104,128]{1,0:T(8,128)S(1)}, f32[104,128]{1,0:T(8,128)S(1)}, u32[]{:S(2)}, u32[]{:S(2)}) collective-permute-start(f32[104,128]{1,0:T(8,128)S(1)} %get-tuple-element.39), channel_id=1, source_target_pairs={{8,16},{16,8},{24,32},{32,24},{40,48},{48,40},{56,64},{64,56},{72,... | collective-permute-start | bytes 159752 | tf_op jit(solution)/shard_map/ppermute | solution.py:36
  68.3 0.0 collective-permute-start.2
  68.3 0.0 collective-permute-start.3
  70.3 0.0 collective-permute-done.xa_ref
  70.3 0.9 collective-permute-done.1.xb_ref
  71.2 0.0 collective-permute-done.2.ya_ref
  71.2 1.9 %collective-permute-done.3.yb_ref = f32[104,128]{1,0:T(8,128)S(1)} collective-permute-done((f32[104,128]{1,0:T(8,128)S(1)}, f32[104,128]{1,0:T(8,128)S(1)}, u32[]{:S(2)}, u32[]{:S(2)}) %collective-permute-start.3) | collective-permute-done | bytes 53280 | tf_op jit(solution)/shard_map/ppermute | solution.py:36
  73.1 0.0 copy-done.1
  73.1 0.0 copy-done.2
  73.1 0.0 copy-done.3
  73.1 6.0 %step.2 = (f32[3328,128]{1,0:T(8,128)S(1)}, f32[104,128]{1,0:T(8,128)S(1)}, f32[104,128]{1,0:T(8,128)S(1)}, f32[104,128]{1,0:T(8,128)S(1)}, f32[104,128]{1,0:T(8,128)S(1)}) custom-call(s32[2,6]{1,0:T(2,128)S(1)} %copy-done.1, f32[13]{0:T(128)S(1)} %copy-done.2, f32[9]{0:T(128)S(1)} %copy-done.3, f32[1]{0:T(128)S(6)} %copy.16.heat_ref, f32[1]{0:T(128)S(6)} %copy.17.pre_ref, ...), custom_call_target="tpu_custom_call" | custom-call | flops 20000000 | bytes 4000000 | tf_op jit(solution)/shard_map/step/pallas_call | solution.py:368
  79.1 0.0 collective-permute-start.4
  79.2 2.8 %collective-permute-start.5 = (f32[104,128]{1,0:T(8,128)S(1)}, f32[104,128]{1,0:T(8,128)S(1)}, u32[]{:S(2)}, u32[]{:S(2)}) collective-permute-start(f32[104,128]{1,0:T(8,128)S(1)} %get-tuple-element.44), channel_id=1, source_target_pairs={{8,16},{16,8},{24,32},{32,24},{40,48},{48,40},{56,64},{64,56},{72,... | collective-permute-start | bytes 159752 | tf_op jit(solution)/shard_map/ppermute | solution.py:36
  82.0 0.0 collective-permute-start.6
  82.0 0.0 collective-permute-start.7
  82.0 1.3 %collective-permute-done.4.xa_ref = f32[104,128]{1,0:T(8,128)S(1)} collective-permute-done((f32[104,128]{1,0:T(8,128)S(1)}, f32[104,128]{1,0:T(8,128)S(1)}, u32[]{:S(2)}, u32[]{:S(2)}) %collective-permute-start.4) | collective-permute-done | bytes 53280 | tf_op jit(solution)/shard_map/ppermute | solution.py:36
  83.3 3.4 %collective-permute-done.5.xb_ref = f32[104,128]{1,0:T(8,128)S(1)} collective-permute-done((f32[104,128]{1,0:T(8,128)S(1)}, f32[104,128]{1,0:T(8,128)S(1)}, u32[]{:S(2)}, u32[]{:S(2)}) %collective-permute-start.5) | collective-permute-done | bytes 53280 | tf_op jit(solution)/shard_map/ppermute | solution.py:36
  86.7 0.0 collective-permute-done.6.ya_ref
  86.7 0.0 collective-permute-done.7.yb_ref
  86.7 6.0 %step.3 = (f32[3328,128]{1,0:T(8,128)S(1)}, f32[104,128]{1,0:T(8,128)S(1)}, f32[104,128]{1,0:T(8,128)S(1)}, f32[104,128]{1,0:T(8,128)S(1)}, f32[104,128]{1,0:T(8,128)S(1)}) custom-call(s32[2,6]{1,0:T(2,128)S(1)} %copy-done.1, f32[13]{0:T(128)S(1)} %copy-done.2, f32[9]{0:T(128)S(1)} %copy-done.3, f32[1]{0:T(128)S(6)} %copy.16.heat_ref, f32[1]{0:T(128)S(6)} %copy.17.pre_ref, ...), custom_call_target="tpu_custom_call" | custom-call | flops 20000000 | bytes 4000000 | tf_op jit(solution)/shard_map/step/pallas_call | solution.py:368
  92.8 0.0 collective-permute-start.10
  92.8 0.3 collective-permute-start.11
  93.1 0.0 collective-permute-start.8
  93.1 2.7 %collective-permute-start.9 = (f32[104,128]{1,0:T(8,128)S(1)}, f32[104,128]{1,0:T(8,128)S(1)}, u32[]{:S(2)}, u32[]{:S(2)}) collective-permute-start(f32[104,128]{1,0:T(8,128)S(1)} %get-tuple-element.49), channel_id=1, source_target_pairs={{8,16},{16,8},{24,32},{32,24},{40,48},{48,40},{56,64},{64,56},{72,... | collective-permute-start | bytes 159752 | tf_op jit(solution)/shard_map/ppermute | solution.py:36
  95.8 0.0 collective-permute-done.10.ya_ref
  95.8 1.8 %collective-permute-done.11.yb_ref = f32[104,128]{1,0:T(8,128)S(1)} collective-permute-done((f32[104,128]{1,0:T(8,128)S(1)}, f32[104,128]{1,0:T(8,128)S(1)}, u32[]{:S(2)}, u32[]{:S(2)}) %collective-permute-start.11) | collective-permute-done | bytes 53280 | tf_op jit(solution)/shard_map/ppermute | solution.py:36
  97.7 0.0 collective-permute-done.8.xa_ref
  97.7 2.9 %collective-permute-done.9.xb_ref = f32[104,128]{1,0:T(8,128)S(1)} collective-permute-done((f32[104,128]{1,0:T(8,128)S(1)}, f32[104,128]{1,0:T(8,128)S(1)}, u32[]{:S(2)}, u32[]{:S(2)}) %collective-permute-start.9) | collective-permute-done | bytes 53280 | tf_op jit(solution)/shard_map/ppermute | solution.py:36
  100.6 5.2 %step_last.1 = f32[3328,128]{1,0:T(8,128)} custom-call(s32[2,6]{1,0:T(2,128)S(1)} %copy-done.1, f32[13]{0:T(128)S(1)} %copy-done.2, f32[9]{0:T(128)S(1)} %copy-done.3, f32[1]{0:T(128)S(6)} %copy.16.heat_ref, f32[1]{0:T(128)S(6)} %copy.17.pre_ref, f32[1]{0:T(128)S(6)} %copy.18.act_ref, f32[3328,128]{1,0:T(8,128)S(1)} %get-tuple-element.47.state_ref, ...), custom_call_target="tpu_custom_call" | custom-call | flops 20000000 | bytes 4000000 | tf_op jit(solution)/shard_map/step_last/pallas_call | solution.py:368
  (1 shorter events, 0.0 us)
Async XLA Ops:
  6.5 50.5 %all-gather.2.cloned.1.call-start = ((), (), s32[]{:S(2)}) async-start(), calls=%async_computation.3 | async-start | bytes 7704576 | tf_op jit(solution)/shard_map/all_gather | solution.py:407
  6.5 1.5 %copy-start = (f32[2,13,16384]{2,0,1:T(2,128)S(1)}, f32[2,13,16384]{2,0,1:T(2,128)}, u32[]{:S(2)}) copy-start(f32[2,13,16384]{2,0,1:T(2,128)} %param.11) | copy-start | bytes 5111812
  8.0 0.7 copy-start.4
  8.6 0.7 copy-start.6
  36.4 20.7 %copy-start.5 = (s32[2]{0:T(128)S(1)}, s32[2]{0:T(128)}, u32[]{:S(2)}) copy-start(s32[2]{0:T(128)} %owner_ref.3) | copy-start | bytes 28
  36.4 20.7 %copy-start.7 = (s32[2]{0:T(128)S(1)}, s32[2]{0:T(128)}, u32[]{:S(2)}) copy-start(s32[2]{0:T(128)} %slot_ref.3) | copy-start | bytes 28
  57.1 16.0 %copy-start.1 = (s32[2,6]{1,0:T(2,128)S(1)}, s32[2,6]{1,0:T(2,128)}, u32[]{:S(2)}) copy-start(s32[2,6]{1,0:T(2,128)} %near_ref.5) | copy-start | bytes 148
  57.1 16.0 %copy-start.2 = (f32[13]{0:T(128)S(1)}, f32[13]{0:T(128)}, u32[]{:S(2)}) copy-start(f32[13]{0:T(128)} %diff_ref.5) | copy-start | bytes 160
  57.1 16.0 %copy-start.3 = (f32[9]{0:T(128)S(1)}, f32[9]{0:T(128)}, u32[]{:S(2)}) copy-start(f32[9]{0:T(128)} %stoi_ref.5) | copy-start | bytes 112
  63.1 7.2 %collective-permute-start = (f32[104,128]{1,0:T(8,128)S(1)}, f32[104,128]{1,0:T(8,128)S(1)}, u32[]{:S(2)}, u32[]{:S(2)}) collective-permute-start(f32[104,128]{1,0:T(8,128)S(1)} %get-tuple-element.38), channel_id=1, source_target_pairs={{0,8},{8,0},{16,24},{24,16},{32,40},{40,32},{48,56},{56,48},{64,72... | collective-permute-start | bytes 159752 | tf_op jit(solution)/shard_map/ppermute | solution.py:36
  63.7 7.5 %collective-permute-start.1 = (f32[104,128]{1,0:T(8,128)S(1)}, f32[104,128]{1,0:T(8,128)S(1)}, u32[]{:S(2)}, u32[]{:S(2)}) collective-permute-start(f32[104,128]{1,0:T(8,128)S(1)} %get-tuple-element.39), channel_id=1, source_target_pairs={{8,16},{16,8},{24,32},{32,24},{40,48},{48,40},{56,64},{64,56},{72,... | collective-permute-start | bytes 159752 | tf_op jit(solution)/shard_map/ppermute | solution.py:36
  68.3 2.9 %collective-permute-start.2 = (f32[104,128]{1,0:T(8,128)S(1)}, f32[104,128]{1,0:T(8,128)S(1)}, u32[]{:S(2)}, u32[]{:S(2)}) collective-permute-start(f32[104,128]{1,0:T(8,128)S(1)} %get-tuple-element.40), channel_id=1, source_target_pairs={{0,1},{1,0},{2,3},{3,2},{4,5},{5,4},{6,7},{7,6},{8,9},{9,8},{10,11... | collective-permute-start | bytes 159752 | tf_op jit(solution)/shard_map/ppermute | solution.py:36
  68.3 4.8 %collective-permute-start.3 = (f32[104,128]{1,0:T(8,128)S(1)}, f32[104,128]{1,0:T(8,128)S(1)}, u32[]{:S(2)}, u32[]{:S(2)}) collective-permute-start(f32[104,128]{1,0:T(8,128)S(1)} %get-tuple-element.41), channel_id=1, source_target_pairs={{1,2},{2,1},{3,4},{4,3},{5,6},{6,5},{7,0},{0,7},{9,10},{10,9},{11,... | collective-permute-start | bytes 159752 | tf_op jit(solution)/shard_map/ppermute | solution.py:36
  79.1 4.2 %collective-permute-start.4 = (f32[104,128]{1,0:T(8,128)S(1)}, f32[104,128]{1,0:T(8,128)S(1)}, u32[]{:S(2)}, u32[]{:S(2)}) collective-permute-start(f32[104,128]{1,0:T(8,128)S(1)} %get-tuple-element.43), channel_id=1, source_target_pairs={{0,8},{8,0},{16,24},{24,16},{32,40},{40,32},{48,56},{56,48},{64,72... | collective-permute-start | bytes 159752 | tf_op jit(solution)/shard_map/ppermute | solution.py:36
  79.2 7.5 %collective-permute-start.5 = (f32[104,128]{1,0:T(8,128)S(1)}, f32[104,128]{1,0:T(8,128)S(1)}, u32[]{:S(2)}, u32[]{:S(2)}) collective-permute-start(f32[104,128]{1,0:T(8,128)S(1)} %get-tuple-element.44), channel_id=1, source_target_pairs={{8,16},{16,8},{24,32},{32,24},{40,48},{48,40},{56,64},{64,56},{72,... | collective-permute-start | bytes 159752 | tf_op jit(solution)/shard_map/ppermute | solution.py:36
  82.0 4.8 %collective-permute-start.6 = (f32[104,128]{1,0:T(8,128)S(1)}, f32[104,128]{1,0:T(8,128)S(1)}, u32[]{:S(2)}, u32[]{:S(2)}) collective-permute-start(f32[104,128]{1,0:T(8,128)S(1)} %get-tuple-element.45), channel_id=1, source_target_pairs={{0,1},{1,0},{2,3},{3,2},{4,5},{5,4},{6,7},{7,6},{8,9},{9,8},{10,11... | collective-permute-start | bytes 159752 | tf_op jit(solution)/shard_map/ppermute | solution.py:36
  82.0 4.8 %collective-permute-start.7 = (f32[104,128]{1,0:T(8,128)S(1)}, f32[104,128]{1,0:T(8,128)S(1)}, u32[]{:S(2)}, u32[]{:S(2)}) collective-permute-start(f32[104,128]{1,0:T(8,128)S(1)} %get-tuple-element.46), channel_id=1, source_target_pairs={{1,2},{2,1},{3,4},{4,3},{5,6},{6,5},{7,0},{0,7},{9,10},{10,9},{11,... | collective-permute-start | bytes 159752 | tf_op jit(solution)/shard_map/ppermute | solution.py:36
  92.8 3.1 %collective-permute-start.10 = (f32[104,128]{1,0:T(8,128)S(1)}, f32[104,128]{1,0:T(8,128)S(1)}, u32[]{:S(2)}, u32[]{:S(2)}) collective-permute-start(f32[104,128]{1,0:T(8,128)S(1)} %get-tuple-element.50), channel_id=1, source_target_pairs={{0,1},{1,0},{2,3},{3,2},{4,5},{5,4},{6,7},{7,6},{8,9},{9,8},{10,11... | collective-permute-start | bytes 159752 | tf_op jit(solution)/shard_map/ppermute | solution.py:36
  92.8 4.8 %collective-permute-start.11 = (f32[104,128]{1,0:T(8,128)S(1)}, f32[104,128]{1,0:T(8,128)S(1)}, u32[]{:S(2)}, u32[]{:S(2)}) collective-permute-start(f32[104,128]{1,0:T(8,128)S(1)} %get-tuple-element.51), channel_id=1, source_target_pairs={{1,2},{2,1},{3,4},{4,3},{5,6},{6,5},{7,0},{0,7},{9,10},{10,9},{11,... | collective-permute-start | bytes 159752 | tf_op jit(solution)/shard_map/ppermute | solution.py:36
  93.1 4.6 %collective-permute-start.8 = (f32[104,128]{1,0:T(8,128)S(1)}, f32[104,128]{1,0:T(8,128)S(1)}, u32[]{:S(2)}, u32[]{:S(2)}) collective-permute-start(f32[104,128]{1,0:T(8,128)S(1)} %get-tuple-element.48), channel_id=1, source_target_pairs={{0,8},{8,0},{16,24},{24,16},{32,40},{40,32},{48,56},{56,48},{64,72... | collective-permute-start | bytes 159752 | tf_op jit(solution)/shard_map/ppermute | solution.py:36
  93.1 7.5 %collective-permute-start.9 = (f32[104,128]{1,0:T(8,128)S(1)}, f32[104,128]{1,0:T(8,128)S(1)}, u32[]{:S(2)}, u32[]{:S(2)}) collective-permute-start(f32[104,128]{1,0:T(8,128)S(1)} %get-tuple-element.49), channel_id=1, source_target_pairs={{8,16},{16,8},{24,32},{32,24},{40,48},{48,40},{56,64},{64,56},{72,... | collective-permute-start | bytes 159752 | tf_op jit(solution)/shard_map/ppermute | solution.py:36
Sparse Core Ops, SparseCore 0:
  11.3 45.7 all-gather.1

commit v3 on v2

v3 whole, which is shorter than its diff:
```python
import functools

import jax
import jax.numpy as jnp
from jax import lax
from jax.experimental import pallas as pl
from jax.experimental.pallas import tpu as pltpu
from jax.sharding import PartitionSpec as P

NSPEC = 9
COMPS = 13
TEMP = 12
BX = 32
BZ = 16
SLOTS = 2
STEPS = 3
LAYERS = SLOTS * BZ
LROWS = COMPS * 8
BROWS = BZ * LROWS
ROWS = SLOTS * BROWS
TAG = 8
PIECE = LROWS + TAG
YBOX = BROWS + TAG
NONE = -1.0
SMEM = pltpu.SMEM
VMEM = pltpu.VMEM
F32 = jnp.float32
PARAMS = pltpu.CompilerParams(vmem_limit_bytes=48 * 1024 * 1024)


def swapped(value, axis, first):
    count = lax.axis_size(axis)
    pairs = []
    for low in range(first, count + first, 2):
        pairs += [(low % count, (low + 1) % count), ((low + 1) % count, low % count)]
    return lax.ppermute(value, axis, pairs)


def moves(target_ref, row, count_y, index_x, index_y):
    slot = lax.rem(target_ref[row], SLOTS)
    owner = target_ref[row] // SLOTS
    dest_x = owner // count_y
    dest_y = owner - dest_x * count_y
    goes_x = (dest_y == index_y) & (dest_x != index_x)
    goes_y = (dest_x == index_x) & (dest_y != index_y)
    return dest_x, dest_y, slot, goes_x, goes_y


def source_rows(n, z, c):
    return pl.ds(c * 256 + z * 16 + n, 8, stride=2)


def pack_kernel(count_y, target_ref, old_ref, box_ref, outx_ref, outy_ref):
    index_x = lax.axis_index("gx")
    index_y = lax.axis_index("gy")
    row_x = jnp.int32(0)
    row_y = jnp.int32(0)
    tag_x = jnp.int32(-1)
    tag_y = jnp.int32(-1)
    for n in range(SLOTS):
        dest_x, dest_y, slot, goes_x, goes_y = moves(target_ref, n, count_y, index_x, index_y)
        row_x = jnp.where(goes_x, n, row_x)
        row_y = jnp.where(goes_y, n, row_y)
        tag_x = jnp.where(goes_x, dest_x * SLOTS + slot, tag_x)
        tag_y = jnp.where(goes_y, dest_y * SLOTS + slot, tag_y)
    first_x = jnp.full((8, 128), row_x, jnp.int32) == 0
    first_y = jnp.full((8, 128), row_y, jnp.int32) == 0

    def layer(z, carry):
        row = pl.multiple_of(z * LROWS, 8)
        for c in range(COMPS):
            zero = old_ref[source_rows(0, z, c), :]
            one = old_ref[source_rows(1, z, c), :]
            box_ref[pl.ds(row + c * 8, 8), :] = zero
            box_ref[pl.ds(BROWS + row + c * 8, 8), :] = one
            outx_ref[z, c * 8 : c * 8 + 8, :] = jnp.where(first_x, zero, one)
            outy_ref[0, pl.ds(row + c * 8, 8), :] = jnp.where(first_y, zero, one)
        outx_ref[z, LROWS:, :] = jnp.full((TAG, 128), tag_x, jnp.int32).astype(F32)
        return carry

    lax.fori_loop(0, BZ, layer, 0)
    outy_ref[0, BROWS:, :] = jnp.full((TAG, 128), tag_y, jnp.int32).astype(F32)


def tag_of(tile):
    return jnp.max(tile).astype(jnp.int32)


def sort_kernel(pieces_ref, first_ref, second_ref, more_ref, used_ref):
    count = pieces_ref.shape[0]
    empty = jnp.full((TAG, 128), NONE, F32)
    more_ref[0] = 0
    tags = []
    for d in range(count):
        first_ref[d, LROWS:, :] = empty
        second_ref[d, LROWS:, :] = empty
        used_ref[d] = 0
        tags.append(tag_of(pieces_ref[d, LROWS:, :]))
    for s in range(count):
        tag = tags[s]
        there = jnp.maximum(tag, 0) // SLOTS
        used = used_ref[there]

        @pl.when((tag >= 0) & (used == 0))
        def _():
            first_ref[there, :, :] = pieces_ref[s]
            used_ref[there] = 1

        @pl.when((tag >= 0) & (used == 1))
        def _():
            second_ref[there, :, :] = pieces_ref[s]
            more_ref[0] = 1


def roll(value, shift, axis):
    if isinstance(shift, int):
        shift = shift % value.shape[axis]
        if shift == 0:
            return value
        return pltpu.roll(value, shift, axis)
    return pltpu.roll(value, lax.rem(shift + 256, 128), axis)


def lanes():
    return lax.broadcasted_iota(jnp.int32, (8, 128), 1)


def sublanes():
    return lax.broadcasted_iota(jnp.int32, (8, 128), 0)


def tile(row):
    return pl.ds(pl.multiple_of(row, 8), 8)


def put_faces(value_of, state_ref, out_refs):
    lane = lanes()
    ends = ((lane & 31) == 0) | ((lane & 31) == 31)
    even = (lane & 1) == 0
    group = lane >> 5
    even_x = lax.rem(lax.axis_index("gx"), 2) == 0
    even_y = lax.rem(lax.axis_index("gy"), 2) == 0
    xa_ref, xb_ref, ya_ref, yb_ref = out_refs

    for c in range(COMPS):
        rows = pl.ds(c * 8, 8)
        both = []
        for n in range(SLOTS):
            parts = [roll(jnp.where(ends, value_of(n, z, c), 0.0), 2 * z, 1) for z in range(BZ)]
            while len(parts) > 1:
                parts = [a + b for a, b in zip(parts[::2], parts[1::2])]
            both.append(parts[0])
        other = roll(both[1], 1, 1)
        low = jnp.where(even, both[0], other)
        high = jnp.where(even, other, both[0])
        xa_ref[rows, :] = jnp.where(even_x, high, low)
        xb_ref[rows, :] = jnp.where(even_x, low, high)
        low = jnp.zeros((8, 128), F32)
        high = jnp.zeros((8, 128), F32)
        for n in range(SLOTS):
            for half in range(2):
                where = 2 * n + half
                base = n * BROWS + half * 8 * LROWS + c * 8
                bottom = state_ref[pl.ds(base, 8, stride=LROWS), :]
                top = state_ref[pl.ds(base + 7, 8, stride=LROWS), :]
                low = jnp.where(group == where, roll(bottom, 32 * where, 1), low)
                high = jnp.where(group == where, roll(top, 32 * where - 96, 1), high)
        ya_ref[rows, :] = jnp.where(even_y, high, low)
        yb_ref[rows, :] = jnp.where(even_y, low, high)


def into(state_ref, slot):
    return state_ref.at[pl.ds(pl.multiple_of(slot * BROWS, 8), BROWS), :]


def place_kernel(count_y, target_ref, box_ref, first_ref, second_ref, state_ref, sems):
    index_x = lax.axis_index("gx")
    index_y = lax.axis_index("gy")
    for n in range(SLOTS):
        dest_x, dest_y, slot, goes_x, goes_y = moves(target_ref, n, count_y, index_x, index_y)

        @pl.when((dest_x == index_x) & (dest_y == index_y))
        def _():
            load = pltpu.make_async_copy(
                box_ref.at[pl.ds(n * BROWS, BROWS), :], into(state_ref, slot), sems.at[0]
            )
            load.start()
            load.wait()

    for source in (first_ref, second_ref):
        tag = tag_of(source[0, LROWS:, :])

        @pl.when(tag >= 0)
        def _():
            base = lax.rem(tag, SLOTS) * BROWS
            loads = [
                pltpu.make_async_copy(
                    source.at[z, pl.ds(0, LROWS), :],
                    state_ref.at[pl.ds(pl.multiple_of(base + z * LROWS, 8), LROWS), :],
                    sems.at[z],
                )
                for z in range(BZ)
            ]
            for load in loads:
                load.start()
            for load in loads:
                load.wait()


def place_y_kernel(_, ally_ref, state_ref, xa_ref, xb_ref, ya_ref, yb_ref, tag_ref, sem):
    index_y = lax.axis_index("gy")
    load = pltpu.make_async_copy(ally_ref.at[:, pl.ds(BROWS, TAG), :], tag_ref, sem)
    load.start()
    load.wait()
    for p in range(tag_ref.shape[0]):
        tag = tag_of(tag_ref[p])

        @pl.when((tag >= 0) & (tag // SLOTS == index_y))
        def _():
            box = pltpu.make_async_copy(
                ally_ref.at[p, pl.ds(0, BROWS), :], into(state_ref, lax.rem(tag, SLOTS)), sem
            )
            box.start()
            box.wait()

    put_faces(
        lambda n, z, c: state_ref[pl.ds((n * BZ + z) * LROWS + c * 8, 8), :],
        state_ref,
        (xa_ref, xb_ref, ya_ref, yb_ref),
    )


def power(value):
    return jnp.exp(0.7 * jnp.log(value))


UNROLL = 4


def inside_kernel(near_ref, diff_ref, stoi_ref, heat_ref, pre_ref, act_ref, state_ref, new_ref, coef_ref):
    lane = lanes()
    sub = sublanes()
    y_low_lanes = lane < 32
    y_high_lanes = lane >= 96
    inner = [
        (lane & 31) != 0,
        (lane & 31) != 31,
        ~(y_low_lanes & (sub == 0)),
        ~(y_high_lanes & (sub == 7)),
    ]

    def power_layer(block, carry):
        for u in range(8):
            index = block * 8 + u
            coef_ref[tile(index * 8), :] = power(state_ref[tile(index * LROWS + TEMP * 8), :])
        return carry

    lax.fori_loop(0, LAYERS // 8, power_layer, 0)

    def layer(n, z):
        index = n * BZ + z
        near_zm = near_ref[n, 4]
        near_zp = near_ref[n, 5]
        index_m = jnp.where(z == 0, jnp.where(near_zm < 0, index, near_zm * BZ + BZ - 1), index - 1)
        index_p = jnp.where(z == BZ - 1, jnp.where(near_zp < 0, index, near_zp * BZ), index + 1)

        def beside(value):
            down = roll(value, 32, 1)
            up = roll(value, -32, 1)
            return (
                roll(value, 1, 1),
                roll(value, -1, 1),
                jnp.where(y_low_lanes, roll(down, 1, 0), down),
                jnp.where(y_high_lanes, roll(up, -1, 0), up),
            )

        center = coef_ref[tile(index * 8), :]
        weights = [
            jnp.where(mask, 0.5 * (center + side), 0.0) for mask, side in zip(inner, beside(center))
        ]
        for at in (index_m, index_p):
            weights.append(0.5 * (center + coef_ref[tile(at * 8), :]))
        total = functools.reduce(lambda a, b: a + b, weights)
        row = pl.multiple_of(index * LROWS, 8)
        row_m = pl.multiple_of(index_m * LROWS, 8)
        row_p = pl.multiple_of(index_p * LROWS, 8)
        rate = (
            pre_ref[0]
            * state_ref[pl.ds(row, 8), :]
            * state_ref[pl.ds(row + 8, 8), :]
            * jnp.exp(-act_ref[0] / state_ref[pl.ds(row + TEMP * 8, 8), :])
        )
        for c in range(COMPS):
            value = state_ref[pl.ds(row + c * 8, 8), :]
            sides = beside(value)
            sides = sides + (state_ref[pl.ds(row_m + c * 8, 8), :], state_ref[pl.ds(row_p + c * 8, 8), :])
            change = -total * value
            for weight, side in zip(weights, sides):
                change = change + weight * side
            value = value + diff_ref[c] * change
            if c < NSPEC:
                value = value + stoi_ref[c] * rate
            elif c == TEMP:
                value = value + heat_ref[0] * rate
            new_ref[pl.ds(row + c * 8, 8), :] = value

    def layers(block, carry):
        n = block // (BZ // UNROLL)
        z = (block - n * (BZ // UNROLL)) * UNROLL
        for u in range(UNROLL):
            layer(n, z + u)
        return carry

    lax.fori_loop(0, LAYERS // UNROLL, layers, 0)


def ghost_kernel(last, near_ref, diff_ref, part_ref, *refs):
    own_refs, got_refs, (new_ref, *out_refs, ym_ref, yp_ref) = refs[:4], refs[4:8], refs[8:]
    lane = lanes()
    even = (lane & 1) == 0
    ends = ((lane & 31) == 0) | ((lane & 31) == 31)
    first_box = lane < 64
    y_first = (lane < 32) & (sublanes() == 0)
    y_last = (lane >= 96) & (sublanes() == 7)
    even_x = lax.rem(lax.axis_index("gx"), 2) == 0
    even_y = lax.rem(lax.axis_index("gy"), 2) == 0

    def plane_pairs(c):
        rows = slice(c * 8, c * 8 + 8)
        own_a, own_b, own_ya, own_yb = (ref[rows, :] for ref in own_refs)
        got_a, got_b, got_ya, got_yb = (ref[rows, :] for ref in got_refs)
        low = jnp.where(even_x, own_b, own_a)
        high = jnp.where(even_x, own_a, own_b)
        below = jnp.where(even_x, got_b, got_a)
        above = jnp.where(even_x, got_a, got_b)
        own = (jnp.where(even, low, high), roll(jnp.where(even, high, low), -1, 1))
        pairs = []
        for n in range(SLOTS):
            ghost = jnp.where(
                even, roll(below, -31 - near_ref[n, 0], 1), roll(above, 31 - near_ref[n, 1], 1)
            )
            pairs.append((own[n], ghost))
        low = jnp.where(even_y, own_yb, own_ya)
        high = jnp.where(even_y, own_ya, own_yb)
        below = jnp.where(even_y, got_yb, got_ya)
        above = jnp.where(even_y, got_ya, got_yb)
        for side, mine, theirs in ((2, low, below), (3, high, above)):
            other = roll(theirs, 64, 1)
            ghost = jnp.where(
                first_box,
                jnp.where(near_ref[0, side] == 0, theirs, other),
                jnp.where(near_ref[1, side] == 1, theirs, other),
            )
            pairs.append((mine, ghost))
        return pairs

    weights = [0.5 * (power(own) + power(ghost)) for own, ghost in plane_pairs(TEMP)]
    x_terms = []
    for c in range(COMPS):
        terms = [
            diff_ref[c] * (weight * (ghost - own)) for weight, (own, ghost) in zip(weights, plane_pairs(c))
        ]
        x_terms.append(terms[:SLOTS])
        for n in range(SLOTS):
            for half in range(2):
                where = 32 * (2 * n + half)
                rows = pl.ds((c * SLOTS + n) * BZ + half * 8, 8)
                ym_ref[rows, :] = roll(terms[2], -where, 1)
                yp_ref[rows, :] = roll(terms[3], 96 - where, 1)

    def value_of(n, z, c):
        row = (n * BZ + z) * LROWS + c * 8
        at = pl.ds((c * SLOTS + n) * BZ + z, 1)
        value = part_ref[pl.ds(row, 8), :] + jnp.where(ends, roll(x_terms[c][n], -2 * z, 1), 0.0)
        low = jnp.broadcast_to(ym_ref[at, :], (8, 128))
        high = jnp.broadcast_to(yp_ref[at, :], (8, 128))
        value = value + jnp.where(y_first, low, jnp.where(y_last, high, 0.0))
        if last:
            new_ref[source_rows(n, z, c), :] = value
        else:
            new_ref[pl.ds(row, 8), :] = value
        return value

    if last:
        for c in range(COMPS):
            for n in range(SLOTS):
                for z in range(BZ):
                    value_of(n, z, c)
    else:
        put_faces(value_of, new_ref, out_refs)


def spec(space):
    return pl.BlockSpec(memory_space=space)


def struct(*shape, dtype=F32):
    return jax.ShapeDtypeStruct(shape, dtype)


PLANES = [struct(LROWS, 128)] * 4


def inside(near, constants, state):
    return pl.pallas_call(
        inside_kernel,
        out_shape=struct(ROWS, 128),
        in_specs=[spec(SMEM)] * 6 + [spec(VMEM)],
        out_specs=spec(VMEM),
        scratch_shapes=[VMEM((LAYERS * 8, 128), F32)],
        compiler_params=PARAMS,
        cost_estimate=pl.CostEstimate(flops=20_000_000, bytes_accessed=4_000_000, transcendentals=0),
        name="inside",
    )(near, *constants, state)


def add_ghosts(last, near, diffusivity, part, sent, received):
    out_shape = struct(ROWS, 128) if last else [struct(ROWS, 128)] + PLANES
    out_specs = spec(VMEM) if last else [spec(VMEM)] * 5
    return pl.pallas_call(
        functools.partial(ghost_kernel, last),
        out_shape=out_shape,
        in_specs=[spec(SMEM)] * 2 + [spec(VMEM)] * 9,
        out_specs=out_specs,
        scratch_shapes=[VMEM((COMPS * SLOTS * BZ, 128), F32)] * 2,
        compiler_params=PARAMS,
        name="ghosts_last" if last else "ghosts",
    )(near, diffusivity, part, *sent, *received)


def shards(
    old_state,
    new_owner,
    new_slot,
    neighbours,
    diffusivity,
    stoichiometry,
    heat_release,
    prefactor,
    activation,
):
    count_x = lax.axis_size("gx")
    count_y = lax.axis_size("gy")
    target = new_owner * SLOTS + new_slot
    old_rows = old_state.reshape(SLOTS, COMPS, 128, 128).transpose(1, 2, 0, 3).reshape(ROWS, 128)
    boxes, outbox_x, outbox_y = pl.pallas_call(
        functools.partial(pack_kernel, count_y),
        out_shape=[struct(ROWS, 128), struct(BZ, PIECE, 128), struct(1, YBOX, 128)],
        in_specs=[spec(SMEM), spec(VMEM)],
        out_specs=[spec(VMEM)] * 3,
        compiler_params=PARAMS,
        name="pack",
    )(target, old_rows)
    all_y = lax.all_gather(outbox_y, "gy", axis=0, tiled=True)
    pieces = lax.all_to_all(outbox_x, "gx", 0, 0, tiled=True)
    first, second, more = pl.pallas_call(
        sort_kernel,
        out_shape=[struct(count_x, PIECE, 128)] * 2 + [struct(1, dtype=jnp.int32)],
        in_specs=[spec(VMEM)],
        out_specs=[spec(VMEM)] * 2 + [spec(SMEM)],
        scratch_shapes=[SMEM((count_x,), jnp.int32)],
        compiler_params=PARAMS,
        name="sort",
    )(pieces)
    first = lax.all_to_all(first, "gx", 0, 0, tiled=True)
    second = lax.cond(
        more[0] > 0,
        lambda value: lax.all_to_all(value, "gx", 0, 0, tiled=True),
        lambda value: value,
        second,
    )
    state = pl.pallas_call(
        functools.partial(place_kernel, count_y),
        out_shape=struct(ROWS, 128),
        in_specs=[spec(SMEM)] + [spec(VMEM)] * 3,
        out_specs=spec(VMEM),
        scratch_shapes=[pltpu.SemaphoreType.DMA((BZ,))],
        compiler_params=PARAMS,
        name="place",
    )(target, boxes, first, second)
    state, *planes = pl.pallas_call(
        place_y_kernel,
        out_shape=[struct(ROWS, 128)] + PLANES,
        in_specs=[spec(VMEM), spec(pl.ANY)],
        out_specs=[spec(VMEM)] * 5,
        input_output_aliases={0: 0},
        scratch_shapes=[VMEM((count_y, TAG, 128), F32), pltpu.SemaphoreType.DMA],
        compiler_params=PARAMS,
        name="place_y",
    )(state, all_y)
    constants = (diffusivity, stoichiometry, heat_release, prefactor, activation)
    for step_index in range(STEPS):
        x_a, x_b, y_a, y_b = planes
        received = (swapped(x_a, "gx", 0), swapped(x_b, "gx", 1), swapped(y_a, "gy", 0), swapped(y_b, "gy", 1))
        part = inside(neighbours, constants, state)
        if step_index < STEPS - 1:
            state, *planes = add_ghosts(False, neighbours, diffusivity, part, planes, received)
        else:
            state = add_ghosts(True, neighbours, diffusivity, part, planes, received)
    return state.reshape(COMPS, 128, SLOTS, 128).transpose(2, 0, 1, 3).reshape(SLOTS, COMPS, BZ * BX * BX)


def solution(mesh):
    return jax.shard_map(
        shards,
        mesh=mesh,
        in_specs=(
            P(("gx", "gy"), None, None),
            P(("gx", "gy")),
            P(("gx", "gy")),
            P(("gx", "gy"), None),
            P(),
            P(),
            P(),
            P(),
            P(),
        ),
        out_specs=P(("gx", "gy"), None, None),
        check_vma=False,
    )
```

time: 113 us -> 106 us (0.938)
  waiting for transfers between devices: 15 us -> 3.59 us
  starting transfers between devices: 11.1 us -> 14.4 us
  Pallas kernels: 26.5 us -> 28.5 us
  local copies, waits for them, and re-layouts: 2.79 us -> 1.48 us
    ppermute x12, waiting for transfers between devices: 12.3 us -> 3.33 us  [swapped(): return lax.ppermute(value, axis, pairs)]
    ppermute x12, starting transfers between devices: 11.1 us -> 14.3 us  [swapped(): return lax.ppermute(value, axis, pairs)]
    pallas_call x4 -> x8, Pallas kernels: 23.2 us -> 25.7 us  [the longest x3 9.57 us: inside(): pl.pallas_call(inside_kernel, out_shape=struct(ROWS, 128), in_specs=[spec...]
    all_gather x1, waiting for transfers between devices: 2.69 us -> 0.25 us  [shards(): all_y = lax.all_gather(outbox_y, 'gy', axis=0, tiled=True)]
    unnamed x16 -> x10, local copies, waits for them, and re-layouts: 2.79 us -> 1.48 us
  transfers between devices with their start and end apart: 13 -> 13, of which waited for: 7 -> 3; matrix products, arithmetic and copies ran while one was open for 0% -> 0% of each run, Pallas kernels for 1% -> 13%
where the time goes in v3:
time: 106 us
  blocking collectives  41.2 us (39%)
  Pallas kernels  28.5 us (27%)
  between operations  16.2 us (15%)
  starting transfers between devices  14.4 us (14%)
  waiting for transfers between devices  3.59 us (3%)
  local copies, waits for them, and re-layouts  1.48 us (1%)
    all_to_all x1, blocking collectives, shards(): pieces = lax.all_to_all(outbox_x, 'gx', 0, 0, tiled=True)  23.2 us
    all_to_all x1, blocking collectives, shards(): first = lax.all_to_all(first, 'gx', 0, 0, tiled=True)  17.9 us
    ppermute x12, starting transfers between devices, swapped(): return lax.ppermute(value, axis, pairs)  14.3 us
    pallas_call x3, Pallas kernels, inside(): pl.pallas_call(inside_kernel, out_shape=struct(ROWS, 128), in_specs=[spec...  9.57 us
    pallas_call x3, Pallas kernels, add_ghosts(): pl.pallas_call(functools.partial(ghost_kernel, last), out_shape=out_shape...  9.2 us
    pallas_call x1, Pallas kernels, shards(): pl.pallas_call(place_y_kernel, out_shape=[struct(ROWS, 128)] + PLANES, in...  4.23 us
    ppermute x12, waiting for transfers between devices, swapped(): return lax.ppermute(value, axis, pairs)  3.33 us
    pallas_call x1, Pallas kernels, shards(): pl.pallas_call(functools.partial(place_kernel, count_y), out_shape=struct...  2.75 us
  transfers between devices with their start and end apart: 13, of which 3 were waited for; matrix products, arithmetic and copies ran while one was open for 0% of the time, Pallas kernels for 13%

profile of v3, /device:TPU:0, one launch (start us, length us, event | category | flops | bytes accessed | tf_op | source)
XLA Modules:
  0.0 105.9 jit_solution(6544446839522476969)
XLA Ops:
  6.5 0.0 all-gather.2.cloned.1.call-start
  6.5 0.7 multiply_add_fusion.target_ref
  7.2 0.0 copy-start
  7.2 1.5 %copy-done = f32[2,13,16384]{2,0,1:T(2,128)S(1)} copy-done((f32[2,13,16384]{2,0,1:T(2,128)S(1)}, f32[2,13,16384]{2,0,1:T(2,128)}, u32[]{:S(2)}) %copy-start) | copy-done | bytes 1703960
  8.7 1.7 %pack.1 = (f32[3328,128]{1,0:T(8,128)S(1)}, f32[16,112,128]{2,1,0:T(8,128)S(1)}, f32[1,1672,128]{2,1,0:T(8,128)}) custom-call(s32[2]{0:T(128)S(1)} %multiply_add_fusion.target_ref, f32[3328,128]{1,0:T(8,128)S(1)} %bitcast.11), custom_call_target="tpu_custom_call" | custom-call | tf_op jit(solution)/shard_map/pack/pallas_call | solution.py:446
  10.4 0.0 all-gather.2.cloned.1.call-update
  10.4 23.2 %all_to_all.15.pieces_ref = f32[16,112,128]{2,1,0:T(8,128)S(1)} all-to-all(f32[16,112,128]{2,1,0:T(8,128)S(1)} %get-tuple-element.32), channel_id=1, replica_groups=mesh['gx'=16,'gy'=8] {'gx'}, dimensions={0} | all-to-all | bytes 1835008 | tf_op jit(solution)/shard_map/all_to_all | solution.py:455
  33.6 1.0 sort.1
  35.3 0.0 copy-start.4
  35.3 17.9 %all_to_all.16.first_ref = f32[16,112,128]{2,1,0:T(8,128)S(1)} all-to-all(f32[16,112,128]{2,1,0:T(8,128)S(1)} %get-tuple-element.33), channel_id=1, replica_groups=mesh['gx'=16,'gy'=8] {'gx'}, dimensions={0} | all-to-all | bytes 1835008 | tf_op jit(solution)/shard_map/all_to_all | solution.py:465
  53.3 0.0 copy-done.4
  53.3 2.8 %place.1._ = f32[3328,128]{1,0:T(8,128)S(1)} custom-call(s32[2]{0:T(128)S(1)} %multiply_add_fusion.target_ref, f32[3328,128]{1,0:T(8,128)S(1)} %get-tuple-element.31.box_ref, f32[16,112,128]{2,1,0:T(8,128)S(1)} %all_to_all.16.first_ref, f32[16,112,128]{2,1,0:T(8,128)} %copy-done.4), custom_call_target="tpu_custom_call" | custom-call | tf_op jit(solution)/shard_map/place/pallas_call | solution.py:472
  56.0 0.0 copy-start.1
  56.0 0.0 copy-start.2
  56.1 0.0 copy-start.3
  56.1 0.2 all-gather.2.cloned.1.call-done.ally_ref
  56.3 4.2 %place_y.1 = (f32[3328,128]{1,0:T(8,128)S(1)}, f32[104,128]{1,0:T(8,128)S(1)}, f32[104,128]{1,0:T(8,128)S(1)}, f32[104,128]{1,0:T(8,128)S(1)}, f32[104,128]{1,0:T(8,128)S(1)}) custom-call(f32[3328,128]{1,0:T(8,128)S(1)} %place.1._, f32[8,1672,128]{2,1,0:T(8,128)} %all-gather.2.cloned.1.call-done.ally_ref), custom_call_target="tpu_custom_call", output_to_operand_aliasing={{0}: (0, {})} | custom-call | tf_op jit(solution)/shard_map/place_y/pallas_call | solution.py:481
  60.5 1.6 %collective-permute-start = (f32[104,128]{1,0:T(8,128)S(1)}, f32[104,128]{1,0:T(8,128)S(1)}, u32[]{:S(2)}, u32[]{:S(2)}) collective-permute-start(f32[104,128]{1,0:T(8,128)S(1)} %get-tuple-element.38.refs_0_), channel_id=1, source_target_pairs={{0,8},{8,0},{16,24},{24,16},{32,40},{40,32},{48,56},{56,48},{64,72... | collective-permute-start | bytes 159752 | tf_op jit(solution)/shard_map/ppermute | solution.py:36
  62.2 4.3 %collective-permute-start.1 = (f32[104,128]{1,0:T(8,128)S(1)}, f32[104,128]{1,0:T(8,128)S(1)}, u32[]{:S(2)}, u32[]{:S(2)}) collective-permute-start(f32[104,128]{1,0:T(8,128)S(1)} %get-tuple-element.39.refs_1_), channel_id=1, source_target_pairs={{8,16},{16,8},{24,32},{32,24},{40,48},{48,40},{56,64},{64,56},{72,... | collective-permute-start | bytes 159752 | tf_op jit(solution)/shard_map/ppermute | solution.py:36
  66.5 0.0 collective-permute-start.2
  66.5 1.0 collective-permute-start.3
  69.4 0.0 copy-done.1
  69.4 0.0 copy-done.2
  69.4 0.0 copy-done.3
  69.4 3.2 %inside.3.part_ref = f32[3328,128]{1,0:T(8,128)S(1)} custom-call(s32[2,6]{1,0:T(2,128)S(1)} %copy-done.1, f32[13]{0:T(128)S(1)} %copy-done.2, f32[9]{0:T(128)S(1)} %copy-done.3, f32[1]{0:T(128)S(6)} %copy.18.heat_ref, f32[1]{0:T(128)S(6)} %copy.19.pre_ref, f32[1]{0:T(128)S(6)} %copy.20.act_ref, f32[3328,128]{1,0:T(8,128)S(1)} %get-tuple-element.37.state_ref), custom_call_target="tpu_custom_call" | custom-call | flops 20000000 | bytes 4000000 | tf_op jit(solution)/shard_map/inside/pallas_call | solution.py:405
  72.6 0.0 collective-permute-done.refs_4_
  72.6 0.0 collective-permute-done.1.refs_5_
  72.6 0.0 collective-permute-done.2.refs_6_
  72.7 0.0 collective-permute-done.3.refs_7_
  72.7 3.1 %ghosts.2 = (f32[3328,128]{1,0:T(8,128)S(1)}, f32[104,128]{1,0:T(8,128)S(1)}, f32[104,128]{1,0:T(8,128)S(1)}, f32[104,128]{1,0:T(8,128)S(1)}, f32[104,128]{1,0:T(8,128)S(1)}) custom-call(s32[2,6]{1,0:T(2,128)S(1)} %copy-done.1, f32[13]{0:T(128)S(1)} %copy-done.2, f32[3328,128]{1,0:T(8,128)S(1)} %inside.3.part_ref, f32[104,128]{1,0:T(8,128)S(1)} %get-tuple-element.38.refs_0_, ...), custom_call_target="tpu_custom_call" | custom-call | tf_op jit(solution)/shard_map/ghosts/pallas_call | solution.py:420
  75.8 0.1 collective-permute-start.4
  75.9 1.8 %collective-permute-start.5 = (f32[104,128]{1,0:T(8,128)S(1)}, f32[104,128]{1,0:T(8,128)S(1)}, u32[]{:S(2)}, u32[]{:S(2)}) collective-permute-start(f32[104,128]{1,0:T(8,128)S(1)} %get-tuple-element.44.refs_1_), channel_id=1, source_target_pairs={{8,16},{16,8},{24,32},{32,24},{40,48},{48,40},{56,64},{64,56},{72,... | collective-permute-start | bytes 159752 | tf_op jit(solution)/shard_map/ppermute | solution.py:36
  77.7 0.0 collective-permute-start.6
  77.7 1.1 %collective-permute-start.7 = (f32[104,128]{1,0:T(8,128)S(1)}, f32[104,128]{1,0:T(8,128)S(1)}, u32[]{:S(2)}, u32[]{:S(2)}) collective-permute-start(f32[104,128]{1,0:T(8,128)S(1)} %get-tuple-element.46.refs_3_), channel_id=1, source_target_pairs={{1,2},{2,1},{3,4},{4,3},{5,6},{6,5},{7,0},{0,7},{9,10},{10,9},{11,... | collective-permute-start | bytes 159752 | tf_op jit(solution)/shard_map/ppermute | solution.py:36
  78.8 3.2 %inside.4.part_ref = f32[3328,128]{1,0:T(8,128)S(1)} custom-call(s32[2,6]{1,0:T(2,128)S(1)} %copy-done.1, f32[13]{0:T(128)S(1)} %copy-done.2, f32[9]{0:T(128)S(1)} %copy-done.3, f32[1]{0:T(128)S(6)} %copy.18.heat_ref, f32[1]{0:T(128)S(6)} %copy.19.pre_ref, f32[1]{0:T(128)S(6)} %copy.20.act_ref, f32[3328,128]{1,0:T(8,128)S(1)} %get-tuple-element.42.state_ref), custom_call_target="tpu_custom_call" | custom-call | flops 20000000 | bytes 4000000 | tf_op jit(solution)/shard_map/inside/pallas_call | solution.py:405
  82.0 0.0 collective-permute-done.4.refs_4_
  82.0 1.4 %collective-permute-done.5.refs_5_ = f32[104,128]{1,0:T(8,128)S(1)} collective-permute-done((f32[104,128]{1,0:T(8,128)S(1)}, f32[104,128]{1,0:T(8,128)S(1)}, u32[]{:S(2)}, u32[]{:S(2)}) %collective-permute-start.5) | collective-permute-done | bytes 53280 | tf_op jit(solution)/shard_map/ppermute | solution.py:36
  83.4 0.0 collective-permute-done.6.refs_6_
  83.4 0.0 collective-permute-done.7.refs_7_
  83.4 3.1 %ghosts.3 = (f32[3328,128]{1,0:T(8,128)S(1)}, f32[104,128]{1,0:T(8,128)S(1)}, f32[104,128]{1,0:T(8,128)S(1)}, f32[104,128]{1,0:T(8,128)S(1)}, f32[104,128]{1,0:T(8,128)S(1)}) custom-call(s32[2,6]{1,0:T(2,128)S(1)} %copy-done.1, f32[13]{0:T(128)S(1)} %copy-done.2, f32[3328,128]{1,0:T(8,128)S(1)} %inside.4.part_ref, f32[104,128]{1,0:T(8,128)S(1)} %get-tuple-element.43.refs_0_, ...), custom_call_target="tpu_custom_call" | custom-call | tf_op jit(solution)/shard_map/ghosts/pallas_call | solution.py:420
  86.6 0.1 collective-permute-start.10
  86.6 2.1 %collective-permute-start.11 = (f32[104,128]{1,0:T(8,128)S(1)}, f32[104,128]{1,0:T(8,128)S(1)}, u32[]{:S(2)}, u32[]{:S(2)}) collective-permute-start(f32[104,128]{1,0:T(8,128)S(1)} %get-tuple-element.51.refs_3_), channel_id=1, source_target_pairs={{1,2},{2,1},{3,4},{4,3},{5,6},{6,5},{7,0},{0,7},{9,10},{10,9},{11,... | collective-permute-start | bytes 159752 | tf_op jit(solution)/shard_map/ppermute | solution.py:36
  88.7 0.0 collective-permute-start.8
  88.7 2.4 %collective-permute-start.9 = (f32[104,128]{1,0:T(8,128)S(1)}, f32[104,128]{1,0:T(8,128)S(1)}, u32[]{:S(2)}, u32[]{:S(2)}) collective-permute-start(f32[104,128]{1,0:T(8,128)S(1)} %get-tuple-element.49.refs_1_), channel_id=1, source_target_pairs={{8,16},{16,8},{24,32},{32,24},{40,48},{48,40},{56,64},{64,56},{72,... | collective-permute-start | bytes 159752 | tf_op jit(solution)/shard_map/ppermute | solution.py:36
  91.1 3.2 %inside.5.part_ref = f32[3328,128]{1,0:T(8,128)S(1)} custom-call(s32[2,6]{1,0:T(2,128)S(1)} %copy-done.1, f32[13]{0:T(128)S(1)} %copy-done.2, f32[9]{0:T(128)S(1)} %copy-done.3, f32[1]{0:T(128)S(6)} %copy.18.heat_ref, f32[1]{0:T(128)S(6)} %copy.19.pre_ref, f32[1]{0:T(128)S(6)} %copy.20.act_ref, f32[3328,128]{1,0:T(8,128)S(1)} %get-tuple-element.47.state_ref), custom_call_target="tpu_custom_call" | custom-call | flops 20000000 | bytes 4000000 | tf_op jit(solution)/shard_map/inside/pallas_call | solution.py:405
  94.3 0.0 collective-permute-done.10.refs_6_
  94.3 0.0 collective-permute-done.11.refs_7_
  94.3 0.0 collective-permute-done.8.refs_4_
  94.3 1.9 %collective-permute-done.9.refs_5_ = f32[104,128]{1,0:T(8,128)S(1)} collective-permute-done((f32[104,128]{1,0:T(8,128)S(1)}, f32[104,128]{1,0:T(8,128)S(1)}, u32[]{:S(2)}, u32[]{:S(2)}) %collective-permute-start.9) | collective-permute-done | bytes 53280 | tf_op jit(solution)/shard_map/ppermute | solution.py:36
  96.2 2.9 %ghosts_last.1 = f32[3328,128]{1,0:T(8,128)} custom-call(s32[2,6]{1,0:T(2,128)S(1)} %copy-done.1, f32[13]{0:T(128)S(1)} %copy-done.2, f32[3328,128]{1,0:T(8,128)S(1)} %inside.5.part_ref, f32[104,128]{1,0:T(8,128)S(1)} %get-tuple-element.48.refs_0_, f32[104,128]{1,0:T(8,128)S(1)} %get-tuple-element.49.refs_1_, f32[104,128]{1,0:T(8,128)S(1)} %get-tuple-element.50.refs_2_, ...), custom_call_target="tpu_custom_call" | custom-call | tf_op jit(solution)/shard_map/ghosts_last/pallas_call | solution.py:420
  (1 shorter events, 0.0 us)
Async XLA Ops:
  6.5 49.8 %all-gather.2.cloned.1.call-start = ((), (), s32[]{:S(2)}) async-start(), calls=%async_computation.3 | async-start | bytes 7704576 | tf_op jit(solution)/shard_map/all_gather | solution.py:454
  7.2 1.5 %copy-start = (f32[2,13,16384]{2,0,1:T(2,128)S(1)}, f32[2,13,16384]{2,0,1:T(2,128)}, u32[]{:S(2)}) copy-start(f32[2,13,16384]{2,0,1:T(2,128)} %param.11) | copy-start | bytes 5111812
  35.3 18.0 %copy-start.4 = (f32[16,112,128]{2,1,0:T(8,128)}, f32[16,112,128]{2,1,0:T(8,128)S(1)}, u32[]{:S(2)}) copy-start(f32[16,112,128]{2,1,0:T(8,128)S(1)} %get-tuple-element.52.second_ref) | copy-start | bytes 2752516
  56.0 13.4 %copy-start.1 = (s32[2,6]{1,0:T(2,128)S(1)}, s32[2,6]{1,0:T(2,128)}, u32[]{:S(2)}) copy-start(s32[2,6]{1,0:T(2,128)} %near_ref.11) | copy-start | bytes 148
  56.0 13.4 %copy-start.2 = (f32[13]{0:T(128)S(1)}, f32[13]{0:T(128)}, u32[]{:S(2)}) copy-start(f32[13]{0:T(128)} %diff_ref.11) | copy-start | bytes 160
  56.1 13.4 %copy-start.3 = (f32[9]{0:T(128)S(1)}, f32[9]{0:T(128)}, u32[]{:S(2)}) copy-start(f32[9]{0:T(128)} %stoi_ref.5) | copy-start | bytes 112
  60.5 12.1 %collective-permute-start = (f32[104,128]{1,0:T(8,128)S(1)}, f32[104,128]{1,0:T(8,128)S(1)}, u32[]{:S(2)}, u32[]{:S(2)}) collective-permute-start(f32[104,128]{1,0:T(8,128)S(1)} %get-tuple-element.38.refs_0_), channel_id=1, source_target_pairs={{0,8},{8,0},{16,24},{24,16},{32,40},{40,32},{48,56},{56,48},{64,72... | collective-permute-start | bytes 159752 | tf_op jit(solution)/shard_map/ppermute | solution.py:36
  62.2 10.5 %collective-permute-start.1 = (f32[104,128]{1,0:T(8,128)S(1)}, f32[104,128]{1,0:T(8,128)S(1)}, u32[]{:S(2)}, u32[]{:S(2)}) collective-permute-start(f32[104,128]{1,0:T(8,128)S(1)} %get-tuple-element.39.refs_1_), channel_id=1, source_target_pairs={{8,16},{16,8},{24,32},{32,24},{40,48},{48,40},{56,64},{64,56},{72,... | collective-permute-start | bytes 159752 | tf_op jit(solution)/shard_map/ppermute | solution.py:36
  66.5 6.2 %collective-permute-start.2 = (f32[104,128]{1,0:T(8,128)S(1)}, f32[104,128]{1,0:T(8,128)S(1)}, u32[]{:S(2)}, u32[]{:S(2)}) collective-permute-start(f32[104,128]{1,0:T(8,128)S(1)} %get-tuple-element.40.refs_2_), channel_id=1, source_target_pairs={{0,1},{1,0},{2,3},{3,2},{4,5},{5,4},{6,7},{7,6},{8,9},{9,8},{10,11... | collective-permute-start | bytes 159752 | tf_op jit(solution)/shard_map/ppermute | solution.py:36
  66.5 6.2 %collective-permute-start.3 = (f32[104,128]{1,0:T(8,128)S(1)}, f32[104,128]{1,0:T(8,128)S(1)}, u32[]{:S(2)}, u32[]{:S(2)}) collective-permute-start(f32[104,128]{1,0:T(8,128)S(1)} %get-tuple-element.41.refs_3_), channel_id=1, source_target_pairs={{1,2},{2,1},{3,4},{4,3},{5,6},{6,5},{7,0},{0,7},{9,10},{10,9},{11,... | collective-permute-start | bytes 159752 | tf_op jit(solution)/shard_map/ppermute | solution.py:36
  75.8 6.2 %collective-permute-start.4 = (f32[104,128]{1,0:T(8,128)S(1)}, f32[104,128]{1,0:T(8,128)S(1)}, u32[]{:S(2)}, u32[]{:S(2)}) collective-permute-start(f32[104,128]{1,0:T(8,128)S(1)} %get-tuple-element.43.refs_0_), channel_id=1, source_target_pairs={{0,8},{8,0},{16,24},{24,16},{32,40},{40,32},{48,56},{56,48},{64,72... | collective-permute-start | bytes 159752 | tf_op jit(solution)/shard_map/ppermute | solution.py:36
  75.9 7.5 %collective-permute-start.5 = (f32[104,128]{1,0:T(8,128)S(1)}, f32[104,128]{1,0:T(8,128)S(1)}, u32[]{:S(2)}, u32[]{:S(2)}) collective-permute-start(f32[104,128]{1,0:T(8,128)S(1)} %get-tuple-element.44.refs_1_), channel_id=1, source_target_pairs={{8,16},{16,8},{24,32},{32,24},{40,48},{48,40},{56,64},{64,56},{72,... | collective-permute-start | bytes 159752 | tf_op jit(solution)/shard_map/ppermute | solution.py:36
  77.7 5.8 %collective-permute-start.6 = (f32[104,128]{1,0:T(8,128)S(1)}, f32[104,128]{1,0:T(8,128)S(1)}, u32[]{:S(2)}, u32[]{:S(2)}) collective-permute-start(f32[104,128]{1,0:T(8,128)S(1)} %get-tuple-element.45.refs_2_), channel_id=1, source_target_pairs={{0,1},{1,0},{2,3},{3,2},{4,5},{5,4},{6,7},{7,6},{8,9},{9,8},{10,11... | collective-permute-start | bytes 159752 | tf_op jit(solution)/shard_map/ppermute | solution.py:36
  77.7 5.8 %collective-permute-start.7 = (f32[104,128]{1,0:T(8,128)S(1)}, f32[104,128]{1,0:T(8,128)S(1)}, u32[]{:S(2)}, u32[]{:S(2)}) collective-permute-start(f32[104,128]{1,0:T(8,128)S(1)} %get-tuple-element.46.refs_3_), channel_id=1, source_target_pairs={{1,2},{2,1},{3,4},{4,3},{5,6},{6,5},{7,0},{0,7},{9,10},{10,9},{11,... | collective-permute-start | bytes 159752 | tf_op jit(solution)/shard_map/ppermute | solution.py:36
  86.6 7.7 %collective-permute-start.10 = (f32[104,128]{1,0:T(8,128)S(1)}, f32[104,128]{1,0:T(8,128)S(1)}, u32[]{:S(2)}, u32[]{:S(2)}) collective-permute-start(f32[104,128]{1,0:T(8,128)S(1)} %get-tuple-element.50.refs_2_), channel_id=1, source_target_pairs={{0,1},{1,0},{2,3},{3,2},{4,5},{5,4},{6,7},{7,6},{8,9},{9,8},{10,11... | collective-permute-start | bytes 159752 | tf_op jit(solution)/shard_map/ppermute | solution.py:36
  86.6 7.6 %collective-permute-start.11 = (f32[104,128]{1,0:T(8,128)S(1)}, f32[104,128]{1,0:T(8,128)S(1)}, u32[]{:S(2)}, u32[]{:S(2)}) collective-permute-start(f32[104,128]{1,0:T(8,128)S(1)} %get-tuple-element.51.refs_3_), channel_id=1, source_target_pairs={{1,2},{2,1},{3,4},{4,3},{5,6},{6,5},{7,0},{0,7},{9,10},{10,9},{11,... | collective-permute-start | bytes 159752 | tf_op jit(solution)/shard_map/ppermute | solution.py:36
  88.7 5.6 %collective-permute-start.8 = (f32[104,128]{1,0:T(8,128)S(1)}, f32[104,128]{1,0:T(8,128)S(1)}, u32[]{:S(2)}, u32[]{:S(2)}) collective-permute-start(f32[104,128]{1,0:T(8,128)S(1)} %get-tuple-element.48.refs_0_), channel_id=1, source_target_pairs={{0,8},{8,0},{16,24},{24,16},{32,40},{40,32},{48,56},{56,48},{64,72... | collective-permute-start | bytes 159752 | tf_op jit(solution)/shard_map/ppermute | solution.py:36
  88.7 7.5 %collective-permute-start.9 = (f32[104,128]{1,0:T(8,128)S(1)}, f32[104,128]{1,0:T(8,128)S(1)}, u32[]{:S(2)}, u32[]{:S(2)}) collective-permute-start(f32[104,128]{1,0:T(8,128)S(1)} %get-tuple-element.49.refs_1_), channel_id=1, source_target_pairs={{8,16},{16,8},{24,32},{32,24},{40,48},{48,40},{56,64},{64,56},{72,... | collective-permute-start | bytes 159752 | tf_op jit(solution)/shard_map/ppermute | solution.py:36
Sparse Core Ops, SparseCore 0:
  10.5 45.7 all-gather.1

commit v4 on v3

--- a/solution.py
+++ b/solution.py
@@ -169,58 +169,58 @@
         yb_ref[rows, :] = jnp.where(even_y, low, high)
 
 
-def into(state_ref, slot):
-    return state_ref.at[pl.ds(pl.multiple_of(slot * BROWS, 8), BROWS), :]
-
-
-def place_kernel(count_y, target_ref, box_ref, first_ref, second_ref, state_ref, sems):
+def place_kernel(count_y, target_ref, box_ref, first_ref, second_ref, state_ref):
     index_x = lax.axis_index("gx")
     index_y = lax.axis_index("gy")
+    tags = [tag_of(source[0, LROWS:, :]) for source in (first_ref, second_ref)]
+
+    def put(slot, z, value):
+        state_ref[pl.ds(pl.multiple_of(slot * BROWS + z * LROWS, 8), LROWS), :] = value
+
     for n in range(SLOTS):
         dest_x, dest_y, slot, goes_x, goes_y = moves(target_ref, n, count_y, index_x, index_y)
 
         @pl.when((dest_x == index_x) & (dest_y == index_y))
         def _():
-            load = pltpu.make_async_copy(
-                box_ref.at[pl.ds(n * BROWS, BROWS), :], into(state_ref, slot), sems.at[0]
-            )
-            load.start()
-            load.wait()
-
-    for source in (first_ref, second_ref):
-        tag = tag_of(source[0, LROWS:, :])
+            for z in range(BZ):
+                put(slot, z, box_ref[pl.ds(n * BROWS + z * LROWS, LROWS), :])
+
+    for tag, source in zip(tags, (first_ref, second_ref)):
 
         @pl.when(tag >= 0)
         def _():
-            base = lax.rem(tag, SLOTS) * BROWS
-            loads = [
-                pltpu.make_async_copy(
-                    source.at[z, pl.ds(0, LROWS), :],
-                    state_ref.at[pl.ds(pl.multiple_of(base + z * LROWS, 8), LROWS), :],
-                    sems.at[z],
-                )
-                for z in range(BZ)
-            ]
-            for load in loads:
-                load.start()
-            for load in loads:
-                load.wait()
-
-
-def place_y_kernel(_, ally_ref, state_ref, xa_ref, xb_ref, ya_ref, yb_ref, tag_ref, sem):
-    index_y = lax.axis_index("gy")
-    load = pltpu.make_async_copy(ally_ref.at[:, pl.ds(BROWS, TAG), :], tag_ref, sem)
+            for z in range(BZ):
+                put(lax.rem(tag, SLOTS), z, source[z, :LROWS, :])
+
+
+def place_y_kernel(_, ally_ref, state_ref, xa_ref, xb_ref, ya_ref, yb_ref, tag_ref, tag_sem, sems):
+    load = pltpu.make_async_copy(ally_ref.at[:, pl.ds(BROWS, TAG), :], tag_ref, tag_sem)
     load.start()
+    index_y = jnp.full((TAG, 128), lax.axis_index("gy"), jnp.int32)
     load.wait()
-    for p in range(tag_ref.shape[0]):
-        tag = tag_of(tag_ref[p])
-
-        @pl.when((tag >= 0) & (tag // SLOTS == index_y))
+    places = []
+    for slot in range(SLOTS):
+        wanted = (index_y * SLOTS + slot).astype(F32)
+        hits = [jnp.where(tag_ref[p] == wanted, p + 1.0, 0.0) for p in range(tag_ref.shape[0])]
+        places.append(tag_of(functools.reduce(jnp.maximum, hits)))
+    boxes = [
+        pltpu.make_async_copy(
+            ally_ref.at[jnp.maximum(place - 1, 0), pl.ds(0, BROWS), :],
+            state_ref.at[pl.ds(slot * BROWS, BROWS), :],
+            sems.at[slot],
+        )
+        for slot, place in enumerate(places)
+    ]
+    for place, box in zip(places, boxes):
+
+        @pl.when(place > 0)
         def _():
-            box = pltpu.make_async_copy(
-                ally_ref.at[p, pl.ds(0, BROWS), :], into(state_ref, lax.rem(tag, SLOTS)), sem
-            )
             box.start()
+
+    for place, box in zip(places, boxes):
+
+        @pl.when(place > 0)
+        def _():
             box.wait()
 
     put_faces(
@@ -234,7 +234,7 @@
     return jnp.exp(0.7 * jnp.log(value))
 
 
-UNROLL = 4
+UNROLL = 8
 
 
 def inside_kernel(near_ref, diff_ref, stoi_ref, heat_ref, pre_ref, act_ref, state_ref, new_ref, coef_ref):
@@ -315,7 +315,11 @@
 
 
 def ghost_kernel(last, near_ref, diff_ref, part_ref, *refs):
-    own_refs, got_refs, (new_ref, *out_refs, ym_ref, yp_ref) = refs[:4], refs[4:8], refs[8:]
+    own_refs, got_refs = refs[:4], refs[4:8]
+    if last:
+        out_ref, ym_ref, yp_ref, new_ref, sems = refs[8:]
+    else:
+        new_ref, *out_refs, ym_ref, yp_ref = refs[8:]
     lane = lanes()
     even = (lane & 1) == 0
     ends = ((lane & 31) == 0) | ((lane & 31) == 31)
@@ -382,10 +386,16 @@
         return value
 
     if last:
+        stores = []
         for c in range(COMPS):
             for n in range(SLOTS):
                 for z in range(BZ):
                     value_of(n, z, c)
+            rows = pl.ds(c * 256, 256)
+            stores.append(pltpu.make_async_copy(new_ref.at[rows, :], out_ref.at[rows, :], sems.at[c]))
+            stores[c].start()
+        for store in stores:
+            store.wait()
     else:
         put_faces(value_of, new_ref, out_refs)
 
@@ -416,13 +426,16 @@
 
 def add_ghosts(last, near, diffusivity, part, sent, received):
     out_shape = struct(ROWS, 128) if last else [struct(ROWS, 128)] + PLANES
-    out_specs = spec(VMEM) if last else [spec(VMEM)] * 5
+    out_specs = spec(pl.ANY) if last else [spec(VMEM)] * 5
+    scratch = [VMEM((COMPS * SLOTS * BZ, 128), F32)] * 2
+    if last:
+        scratch += [VMEM((ROWS, 128), F32), pltpu.SemaphoreType.DMA((COMPS,))]
     return pl.pallas_call(
         functools.partial(ghost_kernel, last),
         out_shape=out_shape,
         in_specs=[spec(SMEM)] * 2 + [spec(VMEM)] * 9,
         out_specs=out_specs,
-        scratch_shapes=[VMEM((COMPS * SLOTS * BZ, 128), F32)] * 2,
+        scratch_shapes=scratch,
         compiler_params=PARAMS,
         name="ghosts_last" if last else "ghosts",
     )(near, diffusivity, part, *sent, *received)
@@ -474,7 +487,6 @@
         out_shape=struct(ROWS, 128),
         in_specs=[spec(SMEM)] + [spec(VMEM)] * 3,
         out_specs=spec(VMEM),
-        scratch_shapes=[pltpu.SemaphoreType.DMA((BZ,))],
         compiler_params=PARAMS,
         name="place",
     )(target, boxes, first, second)
@@ -484,7 +496,11 @@
         in_specs=[spec(VMEM), spec(pl.ANY)],
         out_specs=[spec(VMEM)] * 5,
         input_output_aliases={0: 0},
-        scratch_shapes=[VMEM((count_y, TAG, 128), F32), pltpu.SemaphoreType.DMA],
+        scratch_shapes=[
+            VMEM((count_y, TAG, 128), F32),
+            pltpu.SemaphoreType.DMA,
+            pltpu.SemaphoreType.DMA((SLOTS,)),
+        ],
         compiler_params=PARAMS,
         name="place_y",
     )(state, all_y)

time: 106 us -> 105 us (level)
  Pallas kernels: 28.5 us -> 25 us
  waiting for transfers between devices: 3.59 us -> 5.6 us
    all_gather x1, waiting for transfers between devices: 0.25 us -> 1.62 us  [shards(): all_y = lax.all_gather(outbox_y, 'gy', axis=0, tiled=True)]
    pallas_call x1, Pallas kernels: 2.75 us -> 1.4 us  [shards(): pl.pallas_call(functools.partial(place_kernel, count_y), out_shape=struct...]
  transfers between devices with their start and end apart: 13 -> 13, of which waited for: 3 -> 3; matrix products, arithmetic and copies ran while one was open for 0% -> 0% of each run, Pallas kernels for 13% -> 11%
where the time goes in v4:
time: 105 us; the launch traced here: 104 us
  blocking collectives  41.1 us (39%)
  Pallas kernels  25 us (24%)
  between operations  16.2 us (15%)
  starting transfers between devices  14.4 us (14%)
  waiting for transfers between devices  5.6 us (5%)
  local copies, waits for them, and re-layouts  1.48 us (1%)
    all_to_all x1, blocking collectives, shards(): pieces = lax.all_to_all(outbox_x, 'gx', 0, 0, tiled=True)  23.2 us
    all_to_all x1, blocking collectives, shards(): first = lax.all_to_all(first, 'gx', 0, 0, tiled=True)  17.9 us
    ppermute x12, starting transfers between devices, swapped(): return lax.ppermute(value, axis, pairs)  14.3 us
    pallas_call x3, Pallas kernels, add_ghosts(): pl.pallas_call(functools.partial(ghost_kernel, last), out_shape=out_shape...  8.88 us
    pallas_call x3, Pallas kernels, inside(): pl.pallas_call(inside_kernel, out_shape=struct(ROWS, 128), in_specs=[spec...  8.62 us
    ppermute x12, waiting for transfers between devices, swapped(): return lax.ppermute(value, axis, pairs)  3.96 us
    pallas_call x1, Pallas kernels, shards(): pl.pallas_call(place_y_kernel, out_shape=[struct(ROWS, 128)] + PLANES, in...  3.37 us
  transfers between devices with their start and end apart: 13, of which 3 were waited for; matrix products, arithmetic and copies ran while one was open for 0% of the time, Pallas kernels for 11%

profile of v4, /device:TPU:0, one launch (start us, length us, event | category | flops | bytes accessed | tf_op | source)
XLA Modules:
  0.0 104.5 jit_solution(2145795782489255376)
XLA Ops:
  6.5 0.0 all-gather.2.cloned.1.call-start
  6.5 0.7 multiply_add_fusion.target_ref
  7.2 0.0 copy-start
  7.2 1.5 %copy-done = f32[2,13,16384]{2,0,1:T(2,128)S(1)} copy-done((f32[2,13,16384]{2,0,1:T(2,128)S(1)}, f32[2,13,16384]{2,0,1:T(2,128)}, u32[]{:S(2)}) %copy-start) | copy-done | bytes 1703960
  8.7 1.7 %pack.1 = (f32[3328,128]{1,0:T(8,128)S(1)}, f32[16,112,128]{2,1,0:T(8,128)S(1)}, f32[1,1672,128]{2,1,0:T(8,128)}) custom-call(s32[2]{0:T(128)S(1)} %multiply_add_fusion.target_ref, f32[3328,128]{1,0:T(8,128)S(1)} %bitcast.11), custom_call_target="tpu_custom_call" | custom-call | tf_op jit(solution)/shard_map/pack/pallas_call | solution.py:459
  10.4 0.0 all-gather.2.cloned.1.call-update
  10.4 23.2 %all_to_all.15.pieces_ref = f32[16,112,128]{2,1,0:T(8,128)S(1)} all-to-all(f32[16,112,128]{2,1,0:T(8,128)S(1)} %get-tuple-element.32), channel_id=1, replica_groups=mesh['gx'=16,'gy'=8] {'gx'}, dimensions={0} | all-to-all | bytes 1835008 | tf_op jit(solution)/shard_map/all_to_all | solution.py:468
  33.6 1.0 sort.1
  35.3 0.0 copy-start.4
  35.3 17.9 %all_to_all.16.first_ref = f32[16,112,128]{2,1,0:T(8,128)S(1)} all-to-all(f32[16,112,128]{2,1,0:T(8,128)S(1)} %get-tuple-element.33), channel_id=1, replica_groups=mesh['gx'=16,'gy'=8] {'gx'}, dimensions={0} | all-to-all | bytes 1835008 | tf_op jit(solution)/shard_map/all_to_all | solution.py:478
  53.2 0.0 copy-done.4
  53.3 1.4 %place.1._ = f32[3328,128]{1,0:T(8,128)S(1)} custom-call(s32[2]{0:T(128)S(1)} %multiply_add_fusion.target_ref, f32[3328,128]{1,0:T(8,128)S(1)} %get-tuple-element.31.box_ref, f32[16,112,128]{2,1,0:T(8,128)S(1)} %all_to_all.16.first_ref, f32[16,112,128]{2,1,0:T(8,128)} %copy-done.4), custom_call_target="tpu_custom_call" | custom-call | tf_op jit(solution)/shard_map/place/pallas_call | solution.py:485
  54.7 0.0 copy-start.1
  54.7 0.0 copy-start.2
  54.7 0.0 copy-start.3
  54.7 1.6 %all-gather.2.cloned.1.call-done.ally_ref = f32[8,1672,128]{2,1,0:T(8,128)} async-done(((f32[1,1672,128]{2,1,0:T(8,128)}), f32[8,1672,128]{2,1,0:T(8,128)}) %all-gather.2.cloned.1.call-update) | async-done | bytes 6848528 | tf_op jit(solution)/shard_map/all_gather | solution.py:467
  56.3 3.4 %place_y.1 = (f32[3328,128]{1,0:T(8,128)S(1)}, f32[104,128]{1,0:T(8,128)S(1)}, f32[104,128]{1,0:T(8,128)S(1)}, f32[104,128]{1,0:T(8,128)S(1)}, f32[104,128]{1,0:T(8,128)S(1)}) custom-call(f32[3328,128]{1,0:T(8,128)S(1)} %place.1._, f32[8,1672,128]{2,1,0:T(8,128)} %all-gather.2.cloned.1.call-done.ally_ref), custom_call_target="tpu_custom_call", output_to_operand_aliasing={{0}: (0, {})} | custom-call | tf_op jit(solution)/shard_map/place_y/pallas_call | solution.py:493
  59.7 1.6 %collective-permute-start = (f32[104,128]{1,0:T(8,128)S(1)}, f32[104,128]{1,0:T(8,128)S(1)}, u32[]{:S(2)}, u32[]{:S(2)}) collective-permute-start(f32[104,128]{1,0:T(8,128)S(1)} %get-tuple-element.38.refs_0_), channel_id=1, source_target_pairs={{0,8},{8,0},{16,24},{24,16},{32,40},{40,32},{48,56},{56,48},{64,72... | collective-permute-start | bytes 159752 | tf_op jit(solution)/shard_map/ppermute | solution.py:36
  61.3 4.3 %collective-permute-start.1 = (f32[104,128]{1,0:T(8,128)S(1)}, f32[104,128]{1,0:T(8,128)S(1)}, u32[]{:S(2)}, u32[]{:S(2)}) collective-permute-start(f32[104,128]{1,0:T(8,128)S(1)} %get-tuple-element.39.refs_1_), channel_id=1, source_target_pairs={{8,16},{16,8},{24,32},{32,24},{40,48},{48,40},{56,64},{64,56},{72,... | collective-permute-start | bytes 159752 | tf_op jit(solution)/shard_map/ppermute | solution.py:36
  65.6 0.0 collective-permute-start.2
  65.6 1.0 collective-permute-start.3
  68.5 0.0 copy-done.1
  68.5 0.0 copy-done.2
  68.6 0.0 copy-done.3
  68.6 2.9 %inside.3.part_ref = f32[3328,128]{1,0:T(8,128)S(1)} custom-call(s32[2,6]{1,0:T(2,128)S(1)} %copy-done.1, f32[13]{0:T(128)S(1)} %copy-done.2, f32[9]{0:T(128)S(1)} %copy-done.3, f32[1]{0:T(128)S(6)} %copy.18.heat_ref, f32[1]{0:T(128)S(6)} %copy.19.pre_ref, f32[1]{0:T(128)S(6)} %copy.20.act_ref, f32[3328,128]{1,0:T(8,128)S(1)} %get-tuple-element.37.state_ref), custom_call_target="tpu_custom_call" | custom-call | flops 20000000 | bytes 4000000 | tf_op jit(solution)/shard_map/inside/pallas_call | solution.py:415
  71.5 0.0 collective-permute-done.refs_4_
  71.5 0.0 collective-permute-done.1.refs_5_
  71.5 0.0 collective-permute-done.2.refs_6_
  71.5 0.0 collective-permute-done.3.refs_7_
  71.5 3.1 %ghosts.2 = (f32[3328,128]{1,0:T(8,128)S(1)}, f32[104,128]{1,0:T(8,128)S(1)}, f32[104,128]{1,0:T(8,128)S(1)}, f32[104,128]{1,0:T(8,128)S(1)}, f32[104,128]{1,0:T(8,128)S(1)}) custom-call(s32[2,6]{1,0:T(2,128)S(1)} %copy-done.1, f32[13]{0:T(128)S(1)} %copy-done.2, f32[3328,128]{1,0:T(8,128)S(1)} %inside.3.part_ref, f32[104,128]{1,0:T(8,128)S(1)} %get-tuple-element.38.refs_0_, ...), custom_call_target="tpu_custom_call" | custom-call | tf_op jit(solution)/shard_map/ghosts/pallas_call | solution.py:433
  74.6 0.1 collective-permute-start.4
  74.7 1.6 %collective-permute-start.5 = (f32[104,128]{1,0:T(8,128)S(1)}, f32[104,128]{1,0:T(8,128)S(1)}, u32[]{:S(2)}, u32[]{:S(2)}) collective-permute-start(f32[104,128]{1,0:T(8,128)S(1)} %get-tuple-element.44.refs_1_), channel_id=1, source_target_pairs={{8,16},{16,8},{24,32},{32,24},{40,48},{48,40},{56,64},{64,56},{72,... | collective-permute-start | bytes 159752 | tf_op jit(solution)/shard_map/ppermute | solution.py:36
  76.4 0.0 collective-permute-start.6
  76.4 1.2 %collective-permute-start.7 = (f32[104,128]{1,0:T(8,128)S(1)}, f32[104,128]{1,0:T(8,128)S(1)}, u32[]{:S(2)}, u32[]{:S(2)}) collective-permute-start(f32[104,128]{1,0:T(8,128)S(1)} %get-tuple-element.46.refs_3_), channel_id=1, source_target_pairs={{1,2},{2,1},{3,4},{4,3},{5,6},{6,5},{7,0},{0,7},{9,10},{10,9},{11,... | collective-permute-start | bytes 159752 | tf_op jit(solution)/shard_map/ppermute | solution.py:36
  77.6 2.9 %inside.4.part_ref = f32[3328,128]{1,0:T(8,128)S(1)} custom-call(s32[2,6]{1,0:T(2,128)S(1)} %copy-done.1, f32[13]{0:T(128)S(1)} %copy-done.2, f32[9]{0:T(128)S(1)} %copy-done.3, f32[1]{0:T(128)S(6)} %copy.18.heat_ref, f32[1]{0:T(128)S(6)} %copy.19.pre_ref, f32[1]{0:T(128)S(6)} %copy.20.act_ref, f32[3328,128]{1,0:T(8,128)S(1)} %get-tuple-element.42.state_ref), custom_call_target="tpu_custom_call" | custom-call | flops 20000000 | bytes 4000000 | tf_op jit(solution)/shard_map/inside/pallas_call | solution.py:415
  80.5 0.0 collective-permute-done.4.refs_4_
  80.5 1.7 %collective-permute-done.5.refs_5_ = f32[104,128]{1,0:T(8,128)S(1)} collective-permute-done((f32[104,128]{1,0:T(8,128)S(1)}, f32[104,128]{1,0:T(8,128)S(1)}, u32[]{:S(2)}, u32[]{:S(2)}) %collective-permute-start.5) | collective-permute-done | bytes 53280 | tf_op jit(solution)/shard_map/ppermute | solution.py:36
  82.2 0.0 collective-permute-done.6.refs_6_
  82.2 0.0 collective-permute-done.7.refs_7_
  82.2 3.1 %ghosts.3 = (f32[3328,128]{1,0:T(8,128)S(1)}, f32[104,128]{1,0:T(8,128)S(1)}, f32[104,128]{1,0:T(8,128)S(1)}, f32[104,128]{1,0:T(8,128)S(1)}, f32[104,128]{1,0:T(8,128)S(1)}) custom-call(s32[2,6]{1,0:T(2,128)S(1)} %copy-done.1, f32[13]{0:T(128)S(1)} %copy-done.2, f32[3328,128]{1,0:T(8,128)S(1)} %inside.4.part_ref, f32[104,128]{1,0:T(8,128)S(1)} %get-tuple-element.43.refs_0_, ...), custom_call_target="tpu_custom_call" | custom-call | tf_op jit(solution)/shard_map/ghosts/pallas_call | solution.py:433
  85.4 0.1 collective-permute-start.10
  85.5 2.1 %collective-permute-start.11 = (f32[104,128]{1,0:T(8,128)S(1)}, f32[104,128]{1,0:T(8,128)S(1)}, u32[]{:S(2)}, u32[]{:S(2)}) collective-permute-start(f32[104,128]{1,0:T(8,128)S(1)} %get-tuple-element.51.refs_3_), channel_id=1, source_target_pairs={{1,2},{2,1},{3,4},{4,3},{5,6},{6,5},{7,0},{0,7},{9,10},{10,9},{11,... | collective-permute-start | bytes 159752 | tf_op jit(solution)/shard_map/ppermute | solution.py:36
  87.5 0.0 collective-permute-start.8
  87.5 2.4 %collective-permute-start.9 = (f32[104,128]{1,0:T(8,128)S(1)}, f32[104,128]{1,0:T(8,128)S(1)}, u32[]{:S(2)}, u32[]{:S(2)}) collective-permute-start(f32[104,128]{1,0:T(8,128)S(1)} %get-tuple-element.49.refs_1_), channel_id=1, source_target_pairs={{8,16},{16,8},{24,32},{32,24},{40,48},{48,40},{56,64},{64,56},{72,... | collective-permute-start | bytes 159752 | tf_op jit(solution)/shard_map/ppermute | solution.py:36
  89.9 2.9 %inside.5.part_ref = f32[3328,128]{1,0:T(8,128)S(1)} custom-call(s32[2,6]{1,0:T(2,128)S(1)} %copy-done.1, f32[13]{0:T(128)S(1)} %copy-done.2, f32[9]{0:T(128)S(1)} %copy-done.3, f32[1]{0:T(128)S(6)} %copy.18.heat_ref, f32[1]{0:T(128)S(6)} %copy.19.pre_ref, f32[1]{0:T(128)S(6)} %copy.20.act_ref, f32[3328,128]{1,0:T(8,128)S(1)} %get-tuple-element.47.state_ref), custom_call_target="tpu_custom_call" | custom-call | flops 20000000 | bytes 4000000 | tf_op jit(solution)/shard_map/inside/pallas_call | solution.py:415
  92.8 0.0 collective-permute-done.10.refs_6_
  92.8 0.0 collective-permute-done.11.refs_7_
  92.8 0.0 collective-permute-done.8.refs_4_
  92.8 2.2 %collective-permute-done.9.refs_5_ = f32[104,128]{1,0:T(8,128)S(1)} collective-permute-done((f32[104,128]{1,0:T(8,128)S(1)}, f32[104,128]{1,0:T(8,128)S(1)}, u32[]{:S(2)}, u32[]{:S(2)}) %collective-permute-start.9) | collective-permute-done | bytes 53280 | tf_op jit(solution)/shard_map/ppermute | solution.py:36
  95.0 2.6 %ghosts_last.1 = f32[3328,128]{1,0:T(8,128)} custom-call(s32[2,6]{1,0:T(2,128)S(1)} %copy-done.1, f32[13]{0:T(128)S(1)} %copy-done.2, f32[3328,128]{1,0:T(8,128)S(1)} %inside.5.part_ref, f32[104,128]{1,0:T(8,128)S(1)} %get-tuple-element.48.refs_0_, f32[104,128]{1,0:T(8,128)S(1)} %get-tuple-element.49.refs_1_, f32[104,128]{1,0:T(8,128)S(1)} %get-tuple-element.50.refs_2_, ...), custom_call_target="tpu_custom_call" | custom-call | tf_op jit(solution)/shard_map/ghosts_last/pallas_call | solution.py:433
  (1 shorter events, 0.0 us)
Async XLA Ops:
  6.5 49.8 %all-gather.2.cloned.1.call-start = ((), (), s32[]{:S(2)}) async-start(), calls=%async_computation.3 | async-start | bytes 7704576 | tf_op jit(solution)/shard_map/all_gather | solution.py:467
  7.2 1.5 %copy-start = (f32[2,13,16384]{2,0,1:T(2,128)S(1)}, f32[2,13,16384]{2,0,1:T(2,128)}, u32[]{:S(2)}) copy-start(f32[2,13,16384]{2,0,1:T(2,128)} %param.11) | copy-start | bytes 5111812
  35.3 17.9 %copy-start.4 = (f32[16,112,128]{2,1,0:T(8,128)}, f32[16,112,128]{2,1,0:T(8,128)S(1)}, u32[]{:S(2)}) copy-start(f32[16,112,128]{2,1,0:T(8,128)S(1)} %get-tuple-element.52.second_ref) | copy-start | bytes 2752516
  54.7 13.9 %copy-start.1 = (s32[2,6]{1,0:T(2,128)S(1)}, s32[2,6]{1,0:T(2,128)}, u32[]{:S(2)}) copy-start(s32[2,6]{1,0:T(2,128)} %near_ref.11) | copy-start | bytes 148
  54.7 13.9 %copy-start.2 = (f32[13]{0:T(128)S(1)}, f32[13]{0:T(128)}, u32[]{:S(2)}) copy-start(f32[13]{0:T(128)} %diff_ref.11) | copy-start | bytes 160
  54.7 13.9 %copy-start.3 = (f32[9]{0:T(128)S(1)}, f32[9]{0:T(128)}, u32[]{:S(2)}) copy-start(f32[9]{0:T(128)} %stoi_ref.5) | copy-start | bytes 112
  59.7 11.8 %collective-permute-start = (f32[104,128]{1,0:T(8,128)S(1)}, f32[104,128]{1,0:T(8,128)S(1)}, u32[]{:S(2)}, u32[]{:S(2)}) collective-permute-start(f32[104,128]{1,0:T(8,128)S(1)} %get-tuple-element.38.refs_0_), channel_id=1, source_target_pairs={{0,8},{8,0},{16,24},{24,16},{32,40},{40,32},{48,56},{56,48},{64,72... | collective-permute-start | bytes 159752 | tf_op jit(solution)/shard_map/ppermute | solution.py:36
  61.3 10.1 %collective-permute-start.1 = (f32[104,128]{1,0:T(8,128)S(1)}, f32[104,128]{1,0:T(8,128)S(1)}, u32[]{:S(2)}, u32[]{:S(2)}) collective-permute-start(f32[104,128]{1,0:T(8,128)S(1)} %get-tuple-element.39.refs_1_), channel_id=1, source_target_pairs={{8,16},{16,8},{24,32},{32,24},{40,48},{48,40},{56,64},{64,56},{72,... | collective-permute-start | bytes 159752 | tf_op jit(solution)/shard_map/ppermute | solution.py:36
  65.6 5.9 %collective-permute-start.2 = (f32[104,128]{1,0:T(8,128)S(1)}, f32[104,128]{1,0:T(8,128)S(1)}, u32[]{:S(2)}, u32[]{:S(2)}) collective-permute-start(f32[104,128]{1,0:T(8,128)S(1)} %get-tuple-element.40.refs_2_), channel_id=1, source_target_pairs={{0,1},{1,0},{2,3},{3,2},{4,5},{5,4},{6,7},{7,6},{8,9},{9,8},{10,11... | collective-permute-start | bytes 159752 | tf_op jit(solution)/shard_map/ppermute | solution.py:36
  65.6 5.9 %collective-permute-start.3 = (f32[104,128]{1,0:T(8,128)S(1)}, f32[104,128]{1,0:T(8,128)S(1)}, u32[]{:S(2)}, u32[]{:S(2)}) collective-permute-start(f32[104,128]{1,0:T(8,128)S(1)} %get-tuple-element.41.refs_3_), channel_id=1, source_target_pairs={{1,2},{2,1},{3,4},{4,3},{5,6},{6,5},{7,0},{0,7},{9,10},{10,9},{11,... | collective-permute-start | bytes 159752 | tf_op jit(solution)/shard_map/ppermute | solution.py:36
  74.6 5.8 %collective-permute-start.4 = (f32[104,128]{1,0:T(8,128)S(1)}, f32[104,128]{1,0:T(8,128)S(1)}, u32[]{:S(2)}, u32[]{:S(2)}) collective-permute-start(f32[104,128]{1,0:T(8,128)S(1)} %get-tuple-element.43.refs_0_), channel_id=1, source_target_pairs={{0,8},{8,0},{16,24},{24,16},{32,40},{40,32},{48,56},{56,48},{64,72... | collective-permute-start | bytes 159752 | tf_op jit(solution)/shard_map/ppermute | solution.py:36
  74.7 7.5 %collective-permute-start.5 = (f32[104,128]{1,0:T(8,128)S(1)}, f32[104,128]{1,0:T(8,128)S(1)}, u32[]{:S(2)}, u32[]{:S(2)}) collective-permute-start(f32[104,128]{1,0:T(8,128)S(1)} %get-tuple-element.44.refs_1_), channel_id=1, source_target_pairs={{8,16},{16,8},{24,32},{32,24},{40,48},{48,40},{56,64},{64,56},{72,... | collective-permute-start | bytes 159752 | tf_op jit(solution)/shard_map/ppermute | solution.py:36
  76.4 5.9 %collective-permute-start.6 = (f32[104,128]{1,0:T(8,128)S(1)}, f32[104,128]{1,0:T(8,128)S(1)}, u32[]{:S(2)}, u32[]{:S(2)}) collective-permute-start(f32[104,128]{1,0:T(8,128)S(1)} %get-tuple-element.45.refs_2_), channel_id=1, source_target_pairs={{0,1},{1,0},{2,3},{3,2},{4,5},{5,4},{6,7},{7,6},{8,9},{9,8},{10,11... | collective-permute-start | bytes 159752 | tf_op jit(solution)/shard_map/ppermute | solution.py:36
  76.4 5.9 %collective-permute-start.7 = (f32[104,128]{1,0:T(8,128)S(1)}, f32[104,128]{1,0:T(8,128)S(1)}, u32[]{:S(2)}, u32[]{:S(2)}) collective-permute-start(f32[104,128]{1,0:T(8,128)S(1)} %get-tuple-element.46.refs_3_), channel_id=1, source_target_pairs={{1,2},{2,1},{3,4},{4,3},{5,6},{6,5},{7,0},{0,7},{9,10},{10,9},{11,... | collective-permute-start | bytes 159752 | tf_op jit(solution)/shard_map/ppermute | solution.py:36
  85.4 7.4 %collective-permute-start.10 = (f32[104,128]{1,0:T(8,128)S(1)}, f32[104,128]{1,0:T(8,128)S(1)}, u32[]{:S(2)}, u32[]{:S(2)}) collective-permute-start(f32[104,128]{1,0:T(8,128)S(1)} %get-tuple-element.50.refs_2_), channel_id=1, source_target_pairs={{0,1},{1,0},{2,3},{3,2},{4,5},{5,4},{6,7},{7,6},{8,9},{9,8},{10,11... | collective-permute-start | bytes 159752 | tf_op jit(solution)/shard_map/ppermute | solution.py:36
  85.5 7.3 %collective-permute-start.11 = (f32[104,128]{1,0:T(8,128)S(1)}, f32[104,128]{1,0:T(8,128)S(1)}, u32[]{:S(2)}, u32[]{:S(2)}) collective-permute-start(f32[104,128]{1,0:T(8,128)S(1)} %get-tuple-element.51.refs_3_), channel_id=1, source_target_pairs={{1,2},{2,1},{3,4},{4,3},{5,6},{6,5},{7,0},{0,7},{9,10},{10,9},{11,... | collective-permute-start | bytes 159752 | tf_op jit(solution)/shard_map/ppermute | solution.py:36
  87.5 5.3 %collective-permute-start.8 = (f32[104,128]{1,0:T(8,128)S(1)}, f32[104,128]{1,0:T(8,128)S(1)}, u32[]{:S(2)}, u32[]{:S(2)}) collective-permute-start(f32[104,128]{1,0:T(8,128)S(1)} %get-tuple-element.48.refs_0_), channel_id=1, source_target_pairs={{0,8},{8,0},{16,24},{24,16},{32,40},{40,32},{48,56},{56,48},{64,72... | collective-permute-start | bytes 159752 | tf_op jit(solution)/shard_map/ppermute | solution.py:36
  87.5 7.5 %collective-permute-start.9 = (f32[104,128]{1,0:T(8,128)S(1)}, f32[104,128]{1,0:T(8,128)S(1)}, u32[]{:S(2)}, u32[]{:S(2)}) collective-permute-start(f32[104,128]{1,0:T(8,128)S(1)} %get-tuple-element.49.refs_1_), channel_id=1, source_target_pairs={{8,16},{16,8},{24,32},{32,24},{40,48},{48,40},{56,64},{64,56},{72,... | collective-permute-start | bytes 159752 | tf_op jit(solution)/shard_map/ppermute | solution.py:36
Sparse Core Ops, SparseCore 0:
  10.5 45.7 all-gather.1

commit v5 on v4

--- a/solution.py
+++ b/solution.py
@@ -169,7 +169,30 @@
         yb_ref[rows, :] = jnp.where(even_y, low, high)
 
 
-def place_kernel(count_y, target_ref, box_ref, first_ref, second_ref, state_ref):
+STOI = COMPS
+HEAT = STOI + NSPEC
+PRE = HEAT + 1
+ACT = PRE + 1
+NEAR = ACT + 1
+TABLES = (NEAR + 6 * SLOTS) * 8
+
+
+def entry(table_ref, k):
+    return table_ref[k * 8 : k * 8 + 8, :]
+
+
+def place_kernel(
+    count_y, target_ref, near_ref, diff_ref, stoi_ref, heat_ref, pre_ref, act_ref,
+    box_ref, first_ref, second_ref, state_ref, table_ref,
+):
+    constants = [diff_ref[c] for c in range(COMPS)] + [stoi_ref[c] for c in range(NSPEC)]
+    constants += [heat_ref[0], pre_ref[0], act_ref[0]]
+    for k, constant in enumerate(constants):
+        table_ref[k * 8 : k * 8 + 8, :] = jnp.full((8, 128), constant, F32)
+    for side in range(6):
+        for n in range(SLOTS):
+            k = NEAR + side * SLOTS + n
+            table_ref[k * 8 : k * 8 + 8, :] = jnp.full((8, 128), near_ref[n, side], jnp.int32).astype(F32)
     index_x = lax.axis_index("gx")
     index_y = lax.axis_index("gy")
     tags = [tag_of(source[0, LROWS:, :]) for source in (first_ref, second_ref)]
@@ -237,7 +260,7 @@
 UNROLL = 8
 
 
-def inside_kernel(near_ref, diff_ref, stoi_ref, heat_ref, pre_ref, act_ref, state_ref, new_ref, coef_ref):
+def inside_kernel(table_ref, state_ref, new_ref, coef_ref):
     lane = lanes()
     sub = sublanes()
     y_low_lanes = lane < 32
@@ -257,12 +280,24 @@
 
     lax.fori_loop(0, LAYERS // 8, power_layer, 0)
 
-    def layer(n, z):
+    def layer(n, z, z_unrolled):
         index = n * BZ + z
-        near_zm = near_ref[n, 4]
-        near_zp = near_ref[n, 5]
-        index_m = jnp.where(z == 0, jnp.where(near_zm < 0, index, near_zm * BZ + BZ - 1), index - 1)
-        index_p = jnp.where(z == BZ - 1, jnp.where(near_zp < 0, index, near_zp * BZ), index + 1)
+        first = jnp.full((8, 128), z, jnp.int32) == 0
+        last = jnp.full((8, 128), z, jnp.int32) == BZ - 1
+        index_m = jnp.maximum(index - 1, 0)
+        index_p = jnp.minimum(index + 1, LAYERS - 1)
+        near_m = table_ref[tile((NEAR + 4 * SLOTS + n) * 8), :]
+        near_p = table_ref[tile((NEAR + 5 * SLOTS + n) * 8), :]
+
+        def layers_beside(load):
+            below, above = load(index_m), load(index_p)
+            if z_unrolled == 0:
+                ghost = jnp.where(near_m < 0, load(index), jnp.where(near_m == 0, load(BZ - 1), load(2 * BZ - 1)))
+                below = jnp.where(first, ghost, below)
+            if z_unrolled == UNROLL - 1:
+                ghost = jnp.where(near_p < 0, load(index), jnp.where(near_p == 0, load(0), load(BZ)))
+                above = jnp.where(last, ghost, above)
+            return below, above
 
         def beside(value):
             down = roll(value, 32, 1)
@@ -278,43 +313,41 @@
         weights = [
             jnp.where(mask, 0.5 * (center + side), 0.0) for mask, side in zip(inner, beside(center))
         ]
-        for at in (index_m, index_p):
-            weights.append(0.5 * (center + coef_ref[tile(at * 8), :]))
+        for side in layers_beside(lambda at: coef_ref[tile(at * 8), :]):
+            weights.append(0.5 * (center + side))
         total = functools.reduce(lambda a, b: a + b, weights)
         row = pl.multiple_of(index * LROWS, 8)
-        row_m = pl.multiple_of(index_m * LROWS, 8)
-        row_p = pl.multiple_of(index_p * LROWS, 8)
         rate = (
-            pre_ref[0]
+            entry(table_ref, PRE)
             * state_ref[pl.ds(row, 8), :]
             * state_ref[pl.ds(row + 8, 8), :]
-            * jnp.exp(-act_ref[0] / state_ref[pl.ds(row + TEMP * 8, 8), :])
+            * jnp.exp(-entry(table_ref, ACT) / state_ref[pl.ds(row + TEMP * 8, 8), :])
         )
         for c in range(COMPS):
             value = state_ref[pl.ds(row + c * 8, 8), :]
             sides = beside(value)
-            sides = sides + (state_ref[pl.ds(row_m + c * 8, 8), :], state_ref[pl.ds(row_p + c * 8, 8), :])
+            sides = sides + layers_beside(lambda at: state_ref[tile(at * LROWS + c * 8), :])
             change = -total * value
             for weight, side in zip(weights, sides):
                 change = change + weight * side
-            value = value + diff_ref[c] * change
+            value = value + entry(table_ref, c) * change
             if c < NSPEC:
-                value = value + stoi_ref[c] * rate
+                value = value + entry(table_ref, STOI + c) * rate
             elif c == TEMP:
-                value = value + heat_ref[0] * rate
+                value = value + entry(table_ref, HEAT) * rate
             new_ref[pl.ds(row + c * 8, 8), :] = value
 
     def layers(block, carry):
         n = block // (BZ // UNROLL)
         z = (block - n * (BZ // UNROLL)) * UNROLL
         for u in range(UNROLL):
-            layer(n, z + u)
+            layer(n, z + u, u)
         return carry
 
     lax.fori_loop(0, LAYERS // UNROLL, layers, 0)
 
 
-def ghost_kernel(last, near_ref, diff_ref, part_ref, *refs):
+def ghost_kernel(last, table_ref, part_ref, *refs):
     own_refs, got_refs = refs[:4], refs[4:8]
     if last:
         out_ref, ym_ref, yp_ref, new_ref, sems = refs[8:]
@@ -329,6 +362,9 @@
     even_x = lax.rem(lax.axis_index("gx"), 2) == 0
     even_y = lax.rem(lax.axis_index("gy"), 2) == 0
 
+    def first_slot(n, side):
+        return entry(table_ref, NEAR + side * SLOTS + n) == 0
+
     def plane_pairs(c):
         rows = slice(c * 8, c * 8 + 8)
         own_a, own_b, own_ya, own_yb = (ref[rows, :] for ref in own_refs)
@@ -339,9 +375,11 @@
         above = jnp.where(even_x, got_a, got_b)
         own = (jnp.where(even, low, high), roll(jnp.where(even, high, low), -1, 1))
         pairs = []
+        below = (roll(below, -31, 1), roll(below, -32, 1))
+        above = (roll(above, 31, 1), roll(above, 30, 1))
         for n in range(SLOTS):
             ghost = jnp.where(
-                even, roll(below, -31 - near_ref[n, 0], 1), roll(above, 31 - near_ref[n, 1], 1)
+                even, jnp.where(first_slot(n, 0), *below), jnp.where(first_slot(n, 1), *above)
             )
             pairs.append((own[n], ghost))
         low = jnp.where(even_y, own_yb, own_ya)
@@ -352,8 +390,8 @@
             other = roll(theirs, 64, 1)
             ghost = jnp.where(
                 first_box,
-                jnp.where(near_ref[0, side] == 0, theirs, other),
-                jnp.where(near_ref[1, side] == 1, theirs, other),
+                jnp.where(first_slot(0, side), theirs, other),
+                jnp.where(first_slot(1, side), other, theirs),
             )
             pairs.append((mine, ghost))
         return pairs
@@ -362,7 +400,7 @@
     x_terms = []
     for c in range(COMPS):
         terms = [
-            diff_ref[c] * (weight * (ghost - own)) for weight, (own, ghost) in zip(weights, plane_pairs(c))
+            entry(table_ref, c) * (weight * (ghost - own)) for weight, (own, ghost) in zip(weights, plane_pairs(c))
         ]
         x_terms.append(terms[:SLOTS])
         for n in range(SLOTS):
@@ -411,20 +449,20 @@
 PLANES = [struct(LROWS, 128)] * 4
 
 
-def inside(near, constants, state):
+def inside(table, state):
     return pl.pallas_call(
         inside_kernel,
         out_shape=struct(ROWS, 128),
-        in_specs=[spec(SMEM)] * 6 + [spec(VMEM)],
+        in_specs=[spec(VMEM)] * 2,
         out_specs=spec(VMEM),
         scratch_shapes=[VMEM((LAYERS * 8, 128), F32)],
         compiler_params=PARAMS,
         cost_estimate=pl.CostEstimate(flops=20_000_000, bytes_accessed=4_000_000, transcendentals=0),
         name="inside",
-    )(near, *constants, state)
-
-
-def add_ghosts(last, near, diffusivity, part, sent, received):
+    )(table, state)
+
+
+def add_ghosts(last, table, part, sent, received):
     out_shape = struct(ROWS, 128) if last else [struct(ROWS, 128)] + PLANES
     out_specs = spec(pl.ANY) if last else [spec(VMEM)] * 5
     scratch = [VMEM((COMPS * SLOTS * BZ, 128), F32)] * 2
@@ -433,12 +471,12 @@
     return pl.pallas_call(
         functools.partial(ghost_kernel, last),
         out_shape=out_shape,
-        in_specs=[spec(SMEM)] * 2 + [spec(VMEM)] * 9,
+        in_specs=[spec(VMEM)] * 10,
         out_specs=out_specs,
         scratch_shapes=scratch,
         compiler_params=PARAMS,
         name="ghosts_last" if last else "ghosts",
-    )(near, diffusivity, part, *sent, *received)
+    )(table, part, *sent, *received)
 
 
 def shards(
@@ -482,14 +520,15 @@
         lambda value: value,
         second,
     )
-    state = pl.pallas_call(
+    constants = (diffusivity, stoichiometry, heat_release, prefactor, activation)
+    state, table = pl.pallas_call(
         functools.partial(place_kernel, count_y),
-        out_shape=struct(ROWS, 128),
-        in_specs=[spec(SMEM)] + [spec(VMEM)] * 3,
-        out_specs=spec(VMEM),
+        out_shape=[struct(ROWS, 128), struct(TABLES, 128)],
+        in_specs=[spec(SMEM)] * 7 + [spec(VMEM)] * 3,
+        out_specs=[spec(VMEM)] * 2,
         compiler_params=PARAMS,
         name="place",
-    )(target, boxes, first, second)
+    )(target, neighbours, *constants, boxes, first, second)
     state, *planes = pl.pallas_call(
         place_y_kernel,
         out_shape=[struct(ROWS, 128)] + PLANES,
@@ -504,15 +543,14 @@
         compiler_params=PARAMS,
         name="place_y",
     )(state, all_y)
-    constants = (diffusivity, stoichiometry, heat_release, prefactor, activation)
     for step_index in range(STEPS):
         x_a, x_b, y_a, y_b = planes
         received = (swapped(x_a, "gx", 0), swapped(x_b, "gx", 1), swapped(y_a, "gy", 0), swapped(y_b, "gy", 1))
-        part = inside(neighbours, constants, state)
+        part = inside(table, state)
         if step_index < STEPS - 1:
-            state, *planes = add_ghosts(False, neighbours, diffusivity, part, planes, received)
+            state, *planes = add_ghosts(False, table, part, planes, received)
         else:
-            state = add_ghosts(True, neighbours, diffusivity, part, planes, received)
+            state = add_ghosts(True, table, part, planes, received)
     return state.reshape(COMPS, 128, SLOTS, 128).transpose(2, 0, 1, 3).reshape(SLOTS, COMPS, BZ * BX * BX)
 
 

time: 105 us -> 102 us (0.971)
  blocking collectives: 41.1 us -> 23.2 us
  waiting for transfers between devices: 5.6 us -> 16.3 us
  starting transfers between devices: 14.4 us -> 18.1 us
  Pallas kernels: 25 us -> 22.3 us
  local copies, waits for them, and re-layouts: 1.48 us -> 4.11 us
    all_to_all x1 -> x0, blocking collectives: 17.9 us -> none  [shards(): first = lax.all_to_all(first, 'gx', 0, 0, tiled=True)]
    all_to_all x0 -> x1, waiting for transfers between devices: none -> 12.7 us  [shards(): first = lax.all_to_all(first, 'gx', 0, 0, tiled=True)]
    all_to_all x0 -> x1, starting transfers between devices: none -> 3.93 us  [shards(): first = lax.all_to_all(first, 'gx', 0, 0, tiled=True)]
    unnamed x10 -> x14, local copies, waits for them, and re-layouts: 1.48 us -> 4.11 us
    pallas_call x3, Pallas kernels: 8.88 us -> 7.24 us  [add_ghosts(): pl.pallas_call(functools.partial(ghost_kernel, last), out_shape=out_shape...]
    all_gather x1, waiting for transfers between devices: 1.62 us -> 0.02 us  [shards(): all_y = lax.all_gather(outbox_y, 'gy', axis=0, tiled=True)]
    pallas_call x3, Pallas kernels: 8.62 us -> 7.09 us  [inside(): pl.pallas_call(inside_kernel, out_shape=struct(ROWS, 128), in_specs=[spec...]
  transfers between devices with their start and end apart: 13 -> 14, of which waited for: 3 -> 4; matrix products, arithmetic and copies ran while one was open for 0% -> 0% of each run, Pallas kernels for 11% -> 10%
where the time goes in v5:
time: 102 us; the launch traced here: 101 us
  blocking collectives  23.2 us (23%)
  Pallas kernels  22.3 us (22%)
  starting transfers between devices  18.1 us (18%)
  waiting for transfers between devices  16.3 us (16%)
  between operations  16.2 us (16%)
  local copies, waits for them, and re-layouts  4.11 us (4%)
    all_to_all x1, blocking collectives, shards(): pieces = lax.all_to_all(outbox_x, 'gx', 0, 0, tiled=True)  23.2 us
    ppermute x12, starting transfers between devices, swapped(): return lax.ppermute(value, axis, pairs)  14.2 us
    all_to_all x1, waiting for transfers between devices, shards(): first = lax.all_to_all(first, 'gx', 0, 0, tiled=True)  12.7 us
    pallas_call x3, Pallas kernels, add_ghosts(): pl.pallas_call(functools.partial(ghost_kernel, last), out_shape=out_shape...  7.24 us
    pallas_call x3, Pallas kernels, inside(): pl.pallas_call(inside_kernel, out_shape=struct(ROWS, 128), in_specs=[spec...  7.09 us
    unnamed x14, local copies, waits for them, and re-layouts  4.11 us
    all_to_all x1, starting transfers between devices, shards(): first = lax.all_to_all(first, 'gx', 0, 0, tiled=True)  3.93 us
    ppermute x12, waiting for transfers between devices, swapped(): return lax.ppermute(value, axis, pairs)  3.56 us
  transfers between devices with their start and end apart: 14, of which 4 were waited for; matrix products, arithmetic and copies ran while one was open for 0% of the time, Pallas kernels for 10%

profile of v5, /device:TPU:0, one launch (start us, length us, event | category | flops | bytes accessed | tf_op | source)
XLA Modules:
  0.0 100.9 jit_solution(5480030869799708011)
XLA Ops:
  6.5 0.0 all-gather.2.cloned.1.call-start
  6.5 0.7 multiply_add_fusion.target_ref
  7.2 0.0 copy-start
  7.2 1.5 %copy-done = f32[2,13,16384]{2,0,1:T(2,128)S(1)} copy-done((f32[2,13,16384]{2,0,1:T(2,128)S(1)}, f32[2,13,16384]{2,0,1:T(2,128)}, u32[]{:S(2)}) %copy-start) | copy-done | bytes 1703960
  8.7 1.8 %pack.1 = (f32[3328,128]{1,0:T(8,128)S(1)}, f32[16,112,128]{2,1,0:T(8,128)S(1)}, f32[1,1672,128]{2,1,0:T(8,128)}) custom-call(s32[2]{0:T(128)S(1)} %multiply_add_fusion.target_ref, f32[3328,128]{1,0:T(8,128)S(1)} %bitcast.11), custom_call_target="tpu_custom_call" | custom-call | tf_op jit(solution)/shard_map/pack/pallas_call | solution.py:497
  10.4 0.0 copy-start.1
  10.4 1.2 %copy-done.1 = f32[3328,128]{1,0:T(8,128)} copy-done((f32[3328,128]{1,0:T(8,128)}, f32[3328,128]{1,0:T(8,128)S(1)}, u32[]{:S(2)}) %copy-start.1) | copy-done | bytes 1703960
  11.6 0.0 all-gather.2.cloned.1.call-update
  11.6 23.2 %all_to_all.15.pieces_ref = f32[16,112,128]{2,1,0:T(8,128)S(1)} all-to-all(f32[16,112,128]{2,1,0:T(8,128)S(1)} %get-tuple-element.34), channel_id=1, replica_groups=mesh['gx'=16,'gy'=8] {'gx'}, dimensions={0} | all-to-all | bytes 1835008 | tf_op jit(solution)/shard_map/all_to_all | solution.py:506
  34.8 1.4 %sort.1 = (f32[16,112,128]{2,1,0:T(8,128)}, f32[16,112,128]{2,1,0:T(8,128)S(1)}, s32[1]{0:T(128)}) custom-call(f32[16,112,128]{2,1,0:T(8,128)S(1)} %all_to_all.15.pieces_ref), custom_call_target="tpu_custom_call" | custom-call | tf_op jit(solution)/shard_map/sort/pallas_call | solution.py:507
  37.0 0.0 copy-start.6
  37.0 0.0 copy-start.3
  37.0 0.0 copy-start.4
  37.0 0.0 copy-start.5
  37.0 3.9 %all-to-all-start.2 = ((f32[16,112,128]{2,1,0:T(8,128)}), f32[16,112,128]{2,1,0:T(8,128)S(1)}, u32[]{:S(2)}, u32[]{:S(2)}) async-start(f32[16,112,128]{2,1,0:T(8,128)} %get-tuple-element.35), calls=%async_computation.2 | async-start | bytes 1835008 | tf_op jit(solution)/shard_map/all_to_all | solution.py:516
  42.9 12.7 %all-to-all-done.2.first_ref = f32[16,112,128]{2,1,0:T(8,128)S(1)} async-done(((f32[16,112,128]{2,1,0:T(8,128)}), f32[16,112,128]{2,1,0:T(8,128)S(1)}, u32[]{:S(2)}, u32[]{:S(2)}) %all-to-all-start.2) | async-done | bytes 917536 | tf_op jit(solution)/shard_map/all_to_all | solution.py:516
  55.6 0.0 copy-done.6
  55.6 0.0 copy-done.3
  55.6 0.0 copy-done.4
  55.6 0.0 copy-done.5
  55.6 0.0 copy-start.2
  55.6 1.4 %copy-done.2 = f32[3328,128]{1,0:T(8,128)S(1)} copy-done((f32[3328,128]{1,0:T(8,128)S(1)}, f32[3328,128]{1,0:T(8,128)}, u32[]{:S(2)}) %copy-start.2) | copy-done | bytes 1703960
  57.1 1.4 %place.1 = (f32[3328,128]{1,0:T(8,128)S(1)}, f32[296,128]{1,0:T(8,128)S(1)}) custom-call(s32[2]{0:T(128)S(1)} %multiply_add_fusion.target_ref, s32[2,6]{1,0:T(2,128)S(1)} %copy-done.3, f32[13]{0:T(128)S(1)} %copy-done.4, f32[9]{0:T(128)S(1)} %copy-done.5, f32[1]{0:T(128)S(6)} %copy.18.heat_ref, f32[1]{0:T(128)S(6)} %copy.19.pre_ref, f32[1]{0:T(128)S(6)} %copy.20.act_ref, ...), custom_call_target="tpu_custom_call" | custom-call | tf_op jit(solution)/shard_map/place/pallas_call | solution.py:524
  58.5 0.0 all-gather.2.cloned.1.call-done.ally_ref
  58.5 3.4 %place_y.1 = (f32[3328,128]{1,0:T(8,128)S(1)}, f32[104,128]{1,0:T(8,128)S(1)}, f32[104,128]{1,0:T(8,128)S(1)}, f32[104,128]{1,0:T(8,128)S(1)}, f32[104,128]{1,0:T(8,128)S(1)}) custom-call(f32[3328,128]{1,0:T(8,128)S(1)} %get-tuple-element.39._, f32[8,1672,128]{2,1,0:T(8,128)} %all-gather.2.cloned.1.call-done.ally_ref), custom_call_target="tpu_custom_call", output_to_operand_aliasing={{0}: (0, {})} | custom-call | tf_op jit(solution)/shard_map/place_y/pallas_call | solution.py:532
  61.9 0.7 collective-permute-start
  62.6 4.2 %collective-permute-start.1 = (f32[104,128]{1,0:T(8,128)S(1)}, f32[104,128]{1,0:T(8,128)S(1)}, u32[]{:S(2)}, u32[]{:S(2)}) collective-permute-start(f32[104,128]{1,0:T(8,128)S(1)} %get-tuple-element.43.refs_1_), channel_id=1, source_target_pairs={{8,16},{16,8},{24,32},{32,24},{40,48},{48,40},{56,64},{64,56},{72,... | collective-permute-start | bytes 159752 | tf_op jit(solution)/shard_map/ppermute | solution.py:36
  66.8 0.0 collective-permute-start.2
  66.8 1.0 collective-permute-start.3
  67.8 2.4 %inside.3.part_ref = f32[3328,128]{1,0:T(8,128)S(1)} custom-call(f32[296,128]{1,0:T(8,128)S(1)} %get-tuple-element.38.table_ref, f32[3328,128]{1,0:T(8,128)S(1)} %get-tuple-element.41.state_ref), custom_call_target="tpu_custom_call" | custom-call | flops 20000000 | bytes 4000000 | tf_op jit(solution)/shard_map/inside/pallas_call | solution.py:453
  70.2 0.0 collective-permute-done.refs_4_
  70.2 0.0 collective-permute-done.1.refs_5_
  70.2 0.0 collective-permute-done.2.refs_6_
  70.2 1.4 %collective-permute-done.3.refs_7_ = f32[104,128]{1,0:T(8,128)S(1)} collective-permute-done((f32[104,128]{1,0:T(8,128)S(1)}, f32[104,128]{1,0:T(8,128)S(1)}, u32[]{:S(2)}, u32[]{:S(2)}) %collective-permute-start.3) | collective-permute-done | bytes 53280 | tf_op jit(solution)/shard_map/ppermute | solution.py:36
  71.6 2.6 %ghosts.2 = (f32[3328,128]{1,0:T(8,128)S(1)}, f32[104,128]{1,0:T(8,128)S(1)}, f32[104,128]{1,0:T(8,128)S(1)}, f32[104,128]{1,0:T(8,128)S(1)}, f32[104,128]{1,0:T(8,128)S(1)}) custom-call(f32[296,128]{1,0:T(8,128)S(1)} %get-tuple-element.38.table_ref, f32[3328,128]{1,0:T(8,128)S(1)} %inside.3.part_ref, f32[104,128]{1,0:T(8,128)S(1)} %get-tuple-element.42.refs_0_, ...), custom_call_target="tpu_custom_call" | custom-call | tf_op jit(solution)/shard_map/ghosts/pallas_call | solution.py:471
  74.2 0.1 collective-permute-start.4
  74.2 2.8 %collective-permute-start.5 = (f32[104,128]{1,0:T(8,128)S(1)}, f32[104,128]{1,0:T(8,128)S(1)}, u32[]{:S(2)}, u32[]{:S(2)}) collective-permute-start(f32[104,128]{1,0:T(8,128)S(1)} %get-tuple-element.48.refs_1_), channel_id=1, source_target_pairs={{8,16},{16,8},{24,32},{32,24},{40,48},{48,40},{56,64},{64,56},{72,... | collective-permute-start | bytes 159752 | tf_op jit(solution)/shard_map/ppermute | solution.py:36
  77.0 0.0 collective-permute-start.6
  77.0 1.1 %collective-permute-start.7 = (f32[104,128]{1,0:T(8,128)S(1)}, f32[104,128]{1,0:T(8,128)S(1)}, u32[]{:S(2)}, u32[]{:S(2)}) collective-permute-start(f32[104,128]{1,0:T(8,128)S(1)} %get-tuple-element.50.refs_3_), channel_id=1, source_target_pairs={{1,2},{2,1},{3,4},{4,3},{5,6},{6,5},{7,0},{0,7},{9,10},{10,9},{11,... | collective-permute-start | bytes 159752 | tf_op jit(solution)/shard_map/ppermute | solution.py:36
  78.1 2.4 %inside.4.part_ref = f32[3328,128]{1,0:T(8,128)S(1)} custom-call(f32[296,128]{1,0:T(8,128)S(1)} %get-tuple-element.38.table_ref, f32[3328,128]{1,0:T(8,128)S(1)} %get-tuple-element.46.state_ref), custom_call_target="tpu_custom_call" | custom-call | flops 20000000 | bytes 4000000 | tf_op jit(solution)/shard_map/inside/pallas_call | solution.py:453
  80.5 0.0 collective-permute-done.4.refs_4_
  80.5 1.3 %collective-permute-done.5.refs_5_ = f32[104,128]{1,0:T(8,128)S(1)} collective-permute-done((f32[104,128]{1,0:T(8,128)S(1)}, f32[104,128]{1,0:T(8,128)S(1)}, u32[]{:S(2)}, u32[]{:S(2)}) %collective-permute-start.5) | collective-permute-done | bytes 53280 | tf_op jit(solution)/shard_map/ppermute | solution.py:36
  81.8 0.0 collective-permute-done.6.refs_6_
  81.8 0.0 collective-permute-done.7.refs_7_
  81.8 2.6 %ghosts.3 = (f32[3328,128]{1,0:T(8,128)S(1)}, f32[104,128]{1,0:T(8,128)S(1)}, f32[104,128]{1,0:T(8,128)S(1)}, f32[104,128]{1,0:T(8,128)S(1)}, f32[104,128]{1,0:T(8,128)S(1)}) custom-call(f32[296,128]{1,0:T(8,128)S(1)} %get-tuple-element.38.table_ref, f32[3328,128]{1,0:T(8,128)S(1)} %inside.4.part_ref, f32[104,128]{1,0:T(8,128)S(1)} %get-tuple-element.47.refs_0_, ...), custom_call_target="tpu_custom_call" | custom-call | tf_op jit(solution)/shard_map/ghosts/pallas_call | solution.py:471
  84.4 0.1 collective-permute-start.8
  84.5 2.8 %collective-permute-start.9 = (f32[104,128]{1,0:T(8,128)S(1)}, f32[104,128]{1,0:T(8,128)S(1)}, u32[]{:S(2)}, u32[]{:S(2)}) collective-permute-start(f32[104,128]{1,0:T(8,128)S(1)} %get-tuple-element.53.refs_1_), channel_id=1, source_target_pairs={{8,16},{16,8},{24,32},{32,24},{40,48},{48,40},{56,64},{64,56},{72,... | collective-permute-start | bytes 159752 | tf_op jit(solution)/shard_map/ppermute | solution.py:36
  87.2 0.0 collective-permute-start.10
  87.2 1.5 %collective-permute-start.11 = (f32[104,128]{1,0:T(8,128)S(1)}, f32[104,128]{1,0:T(8,128)S(1)}, u32[]{:S(2)}, u32[]{:S(2)}) collective-permute-start(f32[104,128]{1,0:T(8,128)S(1)} %get-tuple-element.55.refs_3_), channel_id=1, source_target_pairs={{1,2},{2,1},{3,4},{4,3},{5,6},{6,5},{7,0},{0,7},{9,10},{10,9},{11,... | collective-permute-start | bytes 159752 | tf_op jit(solution)/shard_map/ppermute | solution.py:36
  88.7 2.4 %inside.5.part_ref = f32[3328,128]{1,0:T(8,128)S(1)} custom-call(f32[296,128]{1,0:T(8,128)S(1)} %get-tuple-element.38.table_ref, f32[3328,128]{1,0:T(8,128)S(1)} %get-tuple-element.51.state_ref), custom_call_target="tpu_custom_call" | custom-call | flops 20000000 | bytes 4000000 | tf_op jit(solution)/shard_map/inside/pallas_call | solution.py:453
  91.1 0.0 collective-permute-done.8.refs_4_
  91.1 0.9 collective-permute-done.9.refs_5_
  92.0 0.0 collective-permute-done.10.refs_6_
  92.0 0.0 collective-permute-done.11.refs_7_
  92.0 2.0 %ghosts_last.1 = f32[3328,128]{1,0:T(8,128)} custom-call(f32[296,128]{1,0:T(8,128)S(1)} %get-tuple-element.38.table_ref, f32[3328,128]{1,0:T(8,128)S(1)} %inside.5.part_ref, f32[104,128]{1,0:T(8,128)S(1)} %get-tuple-element.52.refs_0_, f32[104,128]{1,0:T(8,128)S(1)} %get-tuple-element.53.refs_1_, f32[104,128]{1,0:T(8,128)S(1)} %get-tuple-element.54.refs_2_, ...), custom_call_target="tpu_custom_call" | custom-call | tf_op jit(solution)/shard_map/ghosts_last/pallas_call | solution.py:471
  (1 shorter events, 0.0 us)
Async XLA Ops:
  6.5 52.0 %all-gather.2.cloned.1.call-start = ((), (), s32[]{:S(2)}) async-start(), calls=%async_computation.3 | async-start | bytes 7704576 | tf_op jit(solution)/shard_map/all_gather | solution.py:505
  7.2 1.5 %copy-start = (f32[2,13,16384]{2,0,1:T(2,128)S(1)}, f32[2,13,16384]{2,0,1:T(2,128)}, u32[]{:S(2)}) copy-start(f32[2,13,16384]{2,0,1:T(2,128)} %param.11) | copy-start | bytes 5111812
  10.4 1.2 %copy-start.1 = (f32[3328,128]{1,0:T(8,128)}, f32[3328,128]{1,0:T(8,128)S(1)}, u32[]{:S(2)}) copy-start(f32[3328,128]{1,0:T(8,128)S(1)} %get-tuple-element.33.box_ref) | copy-start | bytes 5111812
  37.0 18.6 %copy-start.6 = (f32[16,112,128]{2,1,0:T(8,128)}, f32[16,112,128]{2,1,0:T(8,128)S(1)}, u32[]{:S(2)}) copy-start(f32[16,112,128]{2,1,0:T(8,128)S(1)} %get-tuple-element.56.second_ref) | copy-start | bytes 2752516
  37.0 18.6 %copy-start.3 = (s32[2,6]{1,0:T(2,128)S(1)}, s32[2,6]{1,0:T(2,128)}, u32[]{:S(2)}) copy-start(s32[2,6]{1,0:T(2,128)} %near_ref.1) | copy-start | bytes 148
  37.0 18.6 %copy-start.4 = (f32[13]{0:T(128)S(1)}, f32[13]{0:T(128)}, u32[]{:S(2)}) copy-start(f32[13]{0:T(128)} %diff_ref.1) | copy-start | bytes 160
  37.0 18.6 %copy-start.5 = (f32[9]{0:T(128)S(1)}, f32[9]{0:T(128)}, u32[]{:S(2)}) copy-start(f32[9]{0:T(128)} %stoi_ref.1) | copy-start | bytes 112
  37.0 18.6 %all-to-all-start.2 = ((f32[16,112,128]{2,1,0:T(8,128)}), f32[16,112,128]{2,1,0:T(8,128)S(1)}, u32[]{:S(2)}, u32[]{:S(2)}) async-start(f32[16,112,128]{2,1,0:T(8,128)} %get-tuple-element.35), calls=%async_computation.2 | async-start | bytes 1835008 | tf_op jit(solution)/shard_map/all_to_all | solution.py:516
  55.6 1.5 %copy-start.2 = (f32[3328,128]{1,0:T(8,128)S(1)}, f32[3328,128]{1,0:T(8,128)}, u32[]{:S(2)}) copy-start(f32[3328,128]{1,0:T(8,128)} %copy-done.1) | copy-start | bytes 5111812
  61.9 8.3 %collective-permute-start = (f32[104,128]{1,0:T(8,128)S(1)}, f32[104,128]{1,0:T(8,128)S(1)}, u32[]{:S(2)}, u32[]{:S(2)}) collective-permute-start(f32[104,128]{1,0:T(8,128)S(1)} %get-tuple-element.42.refs_0_), channel_id=1, source_target_pairs={{0,8},{8,0},{16,24},{24,16},{32,40},{40,32},{48,56},{56,48},{64,72... | collective-permute-start | bytes 159752 | tf_op jit(solution)/shard_map/ppermute | solution.py:36
  62.6 7.6 %collective-permute-start.1 = (f32[104,128]{1,0:T(8,128)S(1)}, f32[104,128]{1,0:T(8,128)S(1)}, u32[]{:S(2)}, u32[]{:S(2)}) collective-permute-start(f32[104,128]{1,0:T(8,128)S(1)} %get-tuple-element.43.refs_1_), channel_id=1, source_target_pairs={{8,16},{16,8},{24,32},{32,24},{40,48},{48,40},{56,64},{64,56},{72,... | collective-permute-start | bytes 159752 | tf_op jit(solution)/shard_map/ppermute | solution.py:36
  66.8 3.4 %collective-permute-start.2 = (f32[104,128]{1,0:T(8,128)S(1)}, f32[104,128]{1,0:T(8,128)S(1)}, u32[]{:S(2)}, u32[]{:S(2)}) collective-permute-start(f32[104,128]{1,0:T(8,128)S(1)} %get-tuple-element.44.refs_2_), channel_id=1, source_target_pairs={{0,1},{1,0},{2,3},{3,2},{4,5},{5,4},{6,7},{7,6},{8,9},{9,8},{10,11... | collective-permute-start | bytes 159752 | tf_op jit(solution)/shard_map/ppermute | solution.py:36
  66.8 4.8 %collective-permute-start.3 = (f32[104,128]{1,0:T(8,128)S(1)}, f32[104,128]{1,0:T(8,128)S(1)}, u32[]{:S(2)}, u32[]{:S(2)}) collective-permute-start(f32[104,128]{1,0:T(8,128)S(1)} %get-tuple-element.45.refs_3_), channel_id=1, source_target_pairs={{1,2},{2,1},{3,4},{4,3},{5,6},{6,5},{7,0},{0,7},{9,10},{10,9},{11,... | collective-permute-start | bytes 159752 | tf_op jit(solution)/shard_map/ppermute | solution.py:36
  74.2 6.3 %collective-permute-start.4 = (f32[104,128]{1,0:T(8,128)S(1)}, f32[104,128]{1,0:T(8,128)S(1)}, u32[]{:S(2)}, u32[]{:S(2)}) collective-permute-start(f32[104,128]{1,0:T(8,128)S(1)} %get-tuple-element.47.refs_0_), channel_id=1, source_target_pairs={{0,8},{8,0},{16,24},{24,16},{32,40},{40,32},{48,56},{56,48},{64,72... | collective-permute-start | bytes 159752 | tf_op jit(solution)/shard_map/ppermute | solution.py:36
  74.2 7.5 %collective-permute-start.5 = (f32[104,128]{1,0:T(8,128)S(1)}, f32[104,128]{1,0:T(8,128)S(1)}, u32[]{:S(2)}, u32[]{:S(2)}) collective-permute-start(f32[104,128]{1,0:T(8,128)S(1)} %get-tuple-element.48.refs_1_), channel_id=1, source_target_pairs={{8,16},{16,8},{24,32},{32,24},{40,48},{48,40},{56,64},{64,56},{72,... | collective-permute-start | bytes 159752 | tf_op jit(solution)/shard_map/ppermute | solution.py:36
  77.0 4.8 %collective-permute-start.6 = (f32[104,128]{1,0:T(8,128)S(1)}, f32[104,128]{1,0:T(8,128)S(1)}, u32[]{:S(2)}, u32[]{:S(2)}) collective-permute-start(f32[104,128]{1,0:T(8,128)S(1)} %get-tuple-element.49.refs_2_), channel_id=1, source_target_pairs={{0,1},{1,0},{2,3},{3,2},{4,5},{5,4},{6,7},{7,6},{8,9},{9,8},{10,11... | collective-permute-start | bytes 159752 | tf_op jit(solution)/shard_map/ppermute | solution.py:36
  77.0 4.8 %collective-permute-start.7 = (f32[104,128]{1,0:T(8,128)S(1)}, f32[104,128]{1,0:T(8,128)S(1)}, u32[]{:S(2)}, u32[]{:S(2)}) collective-permute-start(f32[104,128]{1,0:T(8,128)S(1)} %get-tuple-element.50.refs_3_), channel_id=1, source_target_pairs={{1,2},{2,1},{3,4},{4,3},{5,6},{6,5},{7,0},{0,7},{9,10},{10,9},{11,... | collective-permute-start | bytes 159752 | tf_op jit(solution)/shard_map/ppermute | solution.py:36
  84.4 6.7 %collective-permute-start.8 = (f32[104,128]{1,0:T(8,128)S(1)}, f32[104,128]{1,0:T(8,128)S(1)}, u32[]{:S(2)}, u32[]{:S(2)}) collective-permute-start(f32[104,128]{1,0:T(8,128)S(1)} %get-tuple-element.52.refs_0_), channel_id=1, source_target_pairs={{0,8},{8,0},{16,24},{24,16},{32,40},{40,32},{48,56},{56,48},{64,72... | collective-permute-start | bytes 159752 | tf_op jit(solution)/shard_map/ppermute | solution.py:36
  84.5 7.5 %collective-permute-start.9 = (f32[104,128]{1,0:T(8,128)S(1)}, f32[104,128]{1,0:T(8,128)S(1)}, u32[]{:S(2)}, u32[]{:S(2)}) collective-permute-start(f32[104,128]{1,0:T(8,128)S(1)} %get-tuple-element.53.refs_1_), channel_id=1, source_target_pairs={{8,16},{16,8},{24,32},{32,24},{40,48},{48,40},{56,64},{64,56},{72,... | collective-permute-start | bytes 159752 | tf_op jit(solution)/shard_map/ppermute | solution.py:36
  87.2 4.8 %collective-permute-start.10 = (f32[104,128]{1,0:T(8,128)S(1)}, f32[104,128]{1,0:T(8,128)S(1)}, u32[]{:S(2)}, u32[]{:S(2)}) collective-permute-start(f32[104,128]{1,0:T(8,128)S(1)} %get-tuple-element.54.refs_2_), channel_id=1, source_target_pairs={{0,1},{1,0},{2,3},{3,2},{4,5},{5,4},{6,7},{7,6},{8,9},{9,8},{10,11... | collective-permute-start | bytes 159752 | tf_op jit(solution)/shard_map/ppermute | solution.py:36
  87.2 4.8 %collective-permute-start.11 = (f32[104,128]{1,0:T(8,128)S(1)}, f32[104,128]{1,0:T(8,128)S(1)}, u32[]{:S(2)}, u32[]{:S(2)}) collective-permute-start(f32[104,128]{1,0:T(8,128)S(1)} %get-tuple-element.55.refs_3_), channel_id=1, source_target_pairs={{1,2},{2,1},{3,4},{4,3},{5,6},{6,5},{7,0},{0,7},{9,10},{10,9},{11,... | collective-permute-start | bytes 159752 | tf_op jit(solution)/shard_map/ppermute | solution.py:36
Sparse Core Ops, SparseCore 0:
  11.7 45.7 all-gather.1

commit v6 on v5

--- a/solution.py
+++ b/solution.py
@@ -25,7 +25,7 @@
 SMEM = pltpu.SMEM
 VMEM = pltpu.VMEM
 F32 = jnp.float32
-PARAMS = pltpu.CompilerParams(vmem_limit_bytes=48 * 1024 * 1024)
+PARAMS = pltpu.CompilerParams(vmem_limit_bytes=16 * 1024 * 1024)
 
 
 def swapped(value, axis, first):

time: 102 us -> 103 us (level)
  local copies, waits for them, and re-layouts: 4.11 us -> 7.05 us
  Pallas kernels: 22.3 us -> 20.5 us
    unnamed x14 -> x16, local copies, waits for them, and re-layouts: 4.11 us -> 7.05 us
    pallas_call x1, Pallas kernels: 3.38 us -> 1.62 us  [shards(): pl.pallas_call(place_y_kernel, out_shape=[struct(ROWS, 128)] + PLANES, in...]
where the time goes in v6:
time: 103 us; the launch traced here: 102 us
  blocking collectives  23.2 us (23%)
  Pallas kernels  20.5 us (20%)
  starting transfers between devices  17.9 us (17%)
  waiting for transfers between devices  16.6 us (16%)
  between operations  16.2 us (16%)
  local copies, waits for them, and re-layouts  7.05 us (7%)
    all_to_all x1, blocking collectives, shards(): pieces = lax.all_to_all(outbox_x, 'gx', 0, 0, tiled=True)  23.2 us
    ppermute x12, starting transfers between devices, swapped(): return lax.ppermute(value, axis, pairs)  14 us
    all_to_all x1, waiting for transfers between devices, shards(): first = lax.all_to_all(first, 'gx', 0, 0, tiled=True)  12.7 us
    pallas_call x3, Pallas kernels, add_ghosts(): pl.pallas_call(functools.partial(ghost_kernel, last), out_shape=out_shape...  7.24 us
    pallas_call x3, Pallas kernels, inside(): pl.pallas_call(inside_kernel, out_shape=struct(ROWS, 128), in_specs=[spec...  7.09 us
    unnamed x16, local copies, waits for them, and re-layouts  7.05 us
    all_to_all x1, starting transfers between devices, shards(): first = lax.all_to_all(first, 'gx', 0, 0, tiled=True)  3.93 us
    ppermute x12, waiting for transfers between devices, swapped(): return lax.ppermute(value, axis, pairs)  3.86 us
  transfers between devices with their start and end apart: 14, of which 4 were waited for; matrix products, arithmetic and copies ran while one was open for 0% of the time, Pallas kernels for 10%

profile of v6, /device:TPU:0, one launch (start us, length us, event | category | flops | bytes accessed | tf_op | source)
XLA Modules:
  0.0 102.1 jit_solution(8980831777643524930)
XLA Ops:
  6.5 0.0 all-gather.2.cloned.1.call-start
  6.5 0.7 multiply_add_fusion.target_ref
  7.2 0.0 copy-start.1
  7.2 1.5 %copy-done.1 = f32[2,13,16384]{2,0,1:T(2,128)S(1)} copy-done((f32[2,13,16384]{2,0,1:T(2,128)S(1)}, f32[2,13,16384]{2,0,1:T(2,128)}, u32[]{:S(2)}) %copy-start.1) | copy-done | bytes 1703960
  8.7 1.7 %pack.1 = (f32[3328,128]{1,0:T(8,128)S(1)}, f32[16,112,128]{2,1,0:T(8,128)S(1)}, f32[1,1672,128]{2,1,0:T(8,128)}) custom-call(s32[2]{0:T(128)S(1)} %multiply_add_fusion.target_ref, f32[3328,128]{1,0:T(8,128)S(1)} %bitcast.11), custom_call_target="tpu_custom_call" | custom-call | tf_op jit(solution)/shard_map/pack/pallas_call | solution.py:497
  10.4 0.0 copy-start.2
  10.4 1.2 %copy-done.2 = f32[3328,128]{1,0:T(8,128)} copy-done((f32[3328,128]{1,0:T(8,128)}, f32[3328,128]{1,0:T(8,128)S(1)}, u32[]{:S(2)}) %copy-start.2) | copy-done | bytes 1703960
  11.6 0.0 all-gather.2.cloned.1.call-update
  11.6 23.2 %all_to_all.15.pieces_ref = f32[16,112,128]{2,1,0:T(8,128)S(1)} all-to-all(f32[16,112,128]{2,1,0:T(8,128)S(1)} %get-tuple-element.34), channel_id=1, replica_groups=mesh['gx'=16,'gy'=8] {'gx'}, dimensions={0} | all-to-all | bytes 1835008 | tf_op jit(solution)/shard_map/all_to_all | solution.py:506
  34.8 1.4 %sort.1 = (f32[16,112,128]{2,1,0:T(8,128)}, f32[16,112,128]{2,1,0:T(8,128)S(1)}, s32[1]{0:T(128)}) custom-call(f32[16,112,128]{2,1,0:T(8,128)S(1)} %all_to_all.15.pieces_ref), custom_call_target="tpu_custom_call" | custom-call | tf_op jit(solution)/shard_map/sort/pallas_call | solution.py:507
  36.9 0.0 copy-start.7
  36.9 0.0 copy-start.4
  36.9 0.0 copy-start.5
  36.9 0.0 copy-start.6
  36.9 3.9 %all-to-all-start.2 = ((f32[16,112,128]{2,1,0:T(8,128)}), f32[16,112,128]{2,1,0:T(8,128)S(1)}, u32[]{:S(2)}, u32[]{:S(2)}) async-start(f32[16,112,128]{2,1,0:T(8,128)} %get-tuple-element.35), calls=%async_computation.2 | async-start | bytes 1835008 | tf_op jit(solution)/shard_map/all_to_all | solution.py:516
  42.8 12.7 %all-to-all-done.2.first_ref = f32[16,112,128]{2,1,0:T(8,128)S(1)} async-done(((f32[16,112,128]{2,1,0:T(8,128)}), f32[16,112,128]{2,1,0:T(8,128)S(1)}, u32[]{:S(2)}, u32[]{:S(2)}) %all-to-all-start.2) | async-done | bytes 917536 | tf_op jit(solution)/shard_map/all_to_all | solution.py:516
  55.5 0.0 copy-done.7
  55.5 0.0 copy-done.4
  55.5 0.0 copy-done.5
  55.5 0.0 copy-done.6
  55.5 0.0 copy-start.3
  55.5 1.4 %copy-done.3 = f32[3328,128]{1,0:T(8,128)S(1)} copy-done((f32[3328,128]{1,0:T(8,128)S(1)}, f32[3328,128]{1,0:T(8,128)}, u32[]{:S(2)}) %copy-start.3) | copy-done | bytes 1703960
  56.9 1.4 %place.1 = (f32[3328,128]{1,0:T(8,128)S(1)}, f32[296,128]{1,0:T(8,128)S(1)}) custom-call(s32[2]{0:T(128)S(1)} %multiply_add_fusion.target_ref, s32[2,6]{1,0:T(2,128)S(1)} %copy-done.4, f32[13]{0:T(128)S(1)} %copy-done.5, f32[9]{0:T(128)S(1)} %copy-done.6, f32[1]{0:T(128)S(6)} %copy.18.heat_ref, f32[1]{0:T(128)S(6)} %copy.19.pre_ref, f32[1]{0:T(128)S(6)} %copy.20.act_ref, ...), custom_call_target="tpu_custom_call" | custom-call | tf_op jit(solution)/shard_map/place/pallas_call | solution.py:524
  58.4 0.0 all-gather.2.cloned.1.call-done.ally_ref
  58.4 0.0 copy-start
  58.4 2.9 %copy-done = f32[8,1672,128]{2,1,0:T(8,128)S(1)} copy-done((f32[8,1672,128]{2,1,0:T(8,128)S(1)}, f32[8,1672,128]{2,1,0:T(8,128)}, u32[]{:S(2)}) %copy-start) | copy-done | bytes 6848536
  61.3 1.6 %place_y.1 = (f32[3328,128]{1,0:T(8,128)S(1)}, f32[104,128]{1,0:T(8,128)S(1)}, f32[104,128]{1,0:T(8,128)S(1)}, f32[104,128]{1,0:T(8,128)S(1)}, f32[104,128]{1,0:T(8,128)S(1)}) custom-call(f32[3328,128]{1,0:T(8,128)S(1)} %get-tuple-element.39._, f32[8,1672,128]{2,1,0:T(8,128)S(1)} %copy-done), custom_call_target="tpu_custom_call", output_to_operand_aliasing={{0}: (0, {})} | custom-call | tf_op jit(solution)/shard_map/place_y/pallas_call | solution.py:532
  62.9 0.6 collective-permute-start
  63.6 4.4 %collective-permute-start.1 = (f32[104,128]{1,0:T(8,128)S(1)}, f32[104,128]{1,0:T(8,128)S(1)}, u32[]{:S(2)}, u32[]{:S(2)}) collective-permute-start(f32[104,128]{1,0:T(8,128)S(1)} %get-tuple-element.43.refs_1_), channel_id=1, source_target_pairs={{8,16},{16,8},{24,32},{32,24},{40,48},{48,40},{56,64},{64,56},{72,... | collective-permute-start | bytes 159752 | tf_op jit(solution)/shard_map/ppermute | solution.py:36
  68.0 0.0 collective-permute-start.2
  68.0 1.0 collective-permute-start.3
  69.0 2.4 %inside.3.part_ref = f32[3328,128]{1,0:T(8,128)S(1)} custom-call(f32[296,128]{1,0:T(8,128)S(1)} %get-tuple-element.38.table_ref, f32[3328,128]{1,0:T(8,128)S(1)} %get-tuple-element.41.state_ref), custom_call_target="tpu_custom_call" | custom-call | flops 20000000 | bytes 4000000 | tf_op jit(solution)/shard_map/inside/pallas_call | solution.py:453
  71.3 0.0 collective-permute-done.refs_4_
  71.3 0.0 collective-permute-done.1.refs_5_
  71.3 0.0 collective-permute-done.2.refs_6_
  71.4 1.4 %collective-permute-done.3.refs_7_ = f32[104,128]{1,0:T(8,128)S(1)} collective-permute-done((f32[104,128]{1,0:T(8,128)S(1)}, f32[104,128]{1,0:T(8,128)S(1)}, u32[]{:S(2)}, u32[]{:S(2)}) %collective-permute-start.3) | collective-permute-done | bytes 53280 | tf_op jit(solution)/shard_map/ppermute | solution.py:36
  72.8 2.6 %ghosts.2 = (f32[3328,128]{1,0:T(8,128)S(1)}, f32[104,128]{1,0:T(8,128)S(1)}, f32[104,128]{1,0:T(8,128)S(1)}, f32[104,128]{1,0:T(8,128)S(1)}, f32[104,128]{1,0:T(8,128)S(1)}) custom-call(f32[296,128]{1,0:T(8,128)S(1)} %get-tuple-element.38.table_ref, f32[3328,128]{1,0:T(8,128)S(1)} %inside.3.part_ref, f32[104,128]{1,0:T(8,128)S(1)} %get-tuple-element.42.refs_0_, ...), custom_call_target="tpu_custom_call" | custom-call | tf_op jit(solution)/shard_map/ghosts/pallas_call | solution.py:471
  75.3 0.1 collective-permute-start.4
  75.4 2.8 %collective-permute-start.5 = (f32[104,128]{1,0:T(8,128)S(1)}, f32[104,128]{1,0:T(8,128)S(1)}, u32[]{:S(2)}, u32[]{:S(2)}) collective-permute-start(f32[104,128]{1,0:T(8,128)S(1)} %get-tuple-element.48.refs_1_), channel_id=1, source_target_pairs={{8,16},{16,8},{24,32},{32,24},{40,48},{48,40},{56,64},{64,56},{72,... | collective-permute-start | bytes 159752 | tf_op jit(solution)/shard_map/ppermute | solution.py:36
  78.2 0.0 collective-permute-start.6
  78.2 1.0 collective-permute-start.7
  79.2 2.4 %inside.4.part_ref = f32[3328,128]{1,0:T(8,128)S(1)} custom-call(f32[296,128]{1,0:T(8,128)S(1)} %get-tuple-element.38.table_ref, f32[3328,128]{1,0:T(8,128)S(1)} %get-tuple-element.46.state_ref), custom_call_target="tpu_custom_call" | custom-call | flops 20000000 | bytes 4000000 | tf_op jit(solution)/shard_map/inside/pallas_call | solution.py:453
  81.5 0.0 collective-permute-done.4.refs_4_
  81.6 1.4 %collective-permute-done.5.refs_5_ = f32[104,128]{1,0:T(8,128)S(1)} collective-permute-done((f32[104,128]{1,0:T(8,128)S(1)}, f32[104,128]{1,0:T(8,128)S(1)}, u32[]{:S(2)}, u32[]{:S(2)}) %collective-permute-start.5) | collective-permute-done | bytes 53280 | tf_op jit(solution)/shard_map/ppermute | solution.py:36
  83.0 0.0 collective-permute-done.6.refs_6_
  83.0 0.0 collective-permute-done.7.refs_7_
  83.0 2.6 %ghosts.3 = (f32[3328,128]{1,0:T(8,128)S(1)}, f32[104,128]{1,0:T(8,128)S(1)}, f32[104,128]{1,0:T(8,128)S(1)}, f32[104,128]{1,0:T(8,128)S(1)}, f32[104,128]{1,0:T(8,128)S(1)}) custom-call(f32[296,128]{1,0:T(8,128)S(1)} %get-tuple-element.38.table_ref, f32[3328,128]{1,0:T(8,128)S(1)} %inside.4.part_ref, f32[104,128]{1,0:T(8,128)S(1)} %get-tuple-element.47.refs_0_, ...), custom_call_target="tpu_custom_call" | custom-call | tf_op jit(solution)/shard_map/ghosts/pallas_call | solution.py:471
  85.6 0.1 collective-permute-start.8
  85.6 2.8 %collective-permute-start.9 = (f32[104,128]{1,0:T(8,128)S(1)}, f32[104,128]{1,0:T(8,128)S(1)}, u32[]{:S(2)}, u32[]{:S(2)}) collective-permute-start(f32[104,128]{1,0:T(8,128)S(1)} %get-tuple-element.53.refs_1_), channel_id=1, source_target_pairs={{8,16},{16,8},{24,32},{32,24},{40,48},{48,40},{56,64},{64,56},{72,... | collective-permute-start | bytes 159752 | tf_op jit(solution)/shard_map/ppermute | solution.py:36
  88.4 0.0 collective-permute-start.10
  88.4 1.3 %collective-permute-start.11 = (f32[104,128]{1,0:T(8,128)S(1)}, f32[104,128]{1,0:T(8,128)S(1)}, u32[]{:S(2)}, u32[]{:S(2)}) collective-permute-start(f32[104,128]{1,0:T(8,128)S(1)} %get-tuple-element.55.refs_3_), channel_id=1, source_target_pairs={{1,2},{2,1},{3,4},{4,3},{5,6},{6,5},{7,0},{0,7},{9,10},{10,9},{11,... | collective-permute-start | bytes 159752 | tf_op jit(solution)/shard_map/ppermute | solution.py:36
  89.7 2.4 %inside.5.part_ref = f32[3328,128]{1,0:T(8,128)S(1)} custom-call(f32[296,128]{1,0:T(8,128)S(1)} %get-tuple-element.38.table_ref, f32[3328,128]{1,0:T(8,128)S(1)} %get-tuple-element.51.state_ref), custom_call_target="tpu_custom_call" | custom-call | flops 20000000 | bytes 4000000 | tf_op jit(solution)/shard_map/inside/pallas_call | solution.py:453
  92.1 0.0 collective-permute-done.8.refs_4_
  92.1 1.0 %collective-permute-done.9.refs_5_ = f32[104,128]{1,0:T(8,128)S(1)} collective-permute-done((f32[104,128]{1,0:T(8,128)S(1)}, f32[104,128]{1,0:T(8,128)S(1)}, u32[]{:S(2)}, u32[]{:S(2)}) %collective-permute-start.9) | collective-permute-done | bytes 53280 | tf_op jit(solution)/shard_map/ppermute | solution.py:36
  93.2 0.0 collective-permute-done.10.refs_6_
  93.2 0.0 collective-permute-done.11.refs_7_
  93.2 2.0 %ghosts_last.1 = f32[3328,128]{1,0:T(8,128)} custom-call(f32[296,128]{1,0:T(8,128)S(1)} %get-tuple-element.38.table_ref, f32[3328,128]{1,0:T(8,128)S(1)} %inside.5.part_ref, f32[104,128]{1,0:T(8,128)S(1)} %get-tuple-element.52.refs_0_, f32[104,128]{1,0:T(8,128)S(1)} %get-tuple-element.53.refs_1_, f32[104,128]{1,0:T(8,128)S(1)} %get-tuple-element.54.refs_2_, ...), custom_call_target="tpu_custom_call" | custom-call | tf_op jit(solution)/shard_map/ghosts_last/pallas_call | solution.py:471
  (1 shorter events, 0.0 us)
Async XLA Ops:
  6.5 51.8 %all-gather.2.cloned.1.call-start = ((), (), s32[]{:S(2)}) async-start(), calls=%async_computation.3 | async-start | bytes 7704576 | tf_op jit(solution)/shard_map/all_gather | solution.py:505
  7.2 1.5 %copy-start.1 = (f32[2,13,16384]{2,0,1:T(2,128)S(1)}, f32[2,13,16384]{2,0,1:T(2,128)}, u32[]{:S(2)}) copy-start(f32[2,13,16384]{2,0,1:T(2,128)} %param.11) | copy-start | bytes 5111812
  10.4 1.2 %copy-start.2 = (f32[3328,128]{1,0:T(8,128)}, f32[3328,128]{1,0:T(8,128)S(1)}, u32[]{:S(2)}) copy-start(f32[3328,128]{1,0:T(8,128)S(1)} %get-tuple-element.33.box_ref) | copy-start | bytes 5111812
  36.9 18.6 %copy-start.7 = (f32[16,112,128]{2,1,0:T(8,128)}, f32[16,112,128]{2,1,0:T(8,128)S(1)}, u32[]{:S(2)}) copy-start(f32[16,112,128]{2,1,0:T(8,128)S(1)} %get-tuple-element.56.second_ref) | copy-start | bytes 2752516
  36.9 18.6 %copy-start.4 = (s32[2,6]{1,0:T(2,128)S(1)}, s32[2,6]{1,0:T(2,128)}, u32[]{:S(2)}) copy-start(s32[2,6]{1,0:T(2,128)} %near_ref.1) | copy-start | bytes 148
  36.9 18.6 %copy-start.5 = (f32[13]{0:T(128)S(1)}, f32[13]{0:T(128)}, u32[]{:S(2)}) copy-start(f32[13]{0:T(128)} %diff_ref.1) | copy-start | bytes 160
  36.9 18.6 %copy-start.6 = (f32[9]{0:T(128)S(1)}, f32[9]{0:T(128)}, u32[]{:S(2)}) copy-start(f32[9]{0:T(128)} %stoi_ref.1) | copy-start | bytes 112
  36.9 18.5 %all-to-all-start.2 = ((f32[16,112,128]{2,1,0:T(8,128)}), f32[16,112,128]{2,1,0:T(8,128)S(1)}, u32[]{:S(2)}, u32[]{:S(2)}) async-start(f32[16,112,128]{2,1,0:T(8,128)} %get-tuple-element.35), calls=%async_computation.2 | async-start | bytes 1835008 | tf_op jit(solution)/shard_map/all_to_all | solution.py:516
  55.5 1.5 %copy-start.3 = (f32[3328,128]{1,0:T(8,128)S(1)}, f32[3328,128]{1,0:T(8,128)}, u32[]{:S(2)}) copy-start(f32[3328,128]{1,0:T(8,128)} %copy-done.2) | copy-start | bytes 5111812
  58.4 2.9 %copy-start = (f32[8,1672,128]{2,1,0:T(8,128)S(1)}, f32[8,1672,128]{2,1,0:T(8,128)}, u32[]{:S(2)}) copy-start(f32[8,1672,128]{2,1,0:T(8,128)} %all-gather.2.cloned.1.call-done.ally_ref) | copy-start | bytes 20545540
  62.9 8.4 %collective-permute-start = (f32[104,128]{1,0:T(8,128)S(1)}, f32[104,128]{1,0:T(8,128)S(1)}, u32[]{:S(2)}, u32[]{:S(2)}) collective-permute-start(f32[104,128]{1,0:T(8,128)S(1)} %get-tuple-element.42.refs_0_), channel_id=1, source_target_pairs={{0,8},{8,0},{16,24},{24,16},{32,40},{40,32},{48,56},{56,48},{64,72... | collective-permute-start | bytes 159752 | tf_op jit(solution)/shard_map/ppermute | solution.py:36
  63.6 7.8 %collective-permute-start.1 = (f32[104,128]{1,0:T(8,128)S(1)}, f32[104,128]{1,0:T(8,128)S(1)}, u32[]{:S(2)}, u32[]{:S(2)}) collective-permute-start(f32[104,128]{1,0:T(8,128)S(1)} %get-tuple-element.43.refs_1_), channel_id=1, source_target_pairs={{8,16},{16,8},{24,32},{32,24},{40,48},{48,40},{56,64},{64,56},{72,... | collective-permute-start | bytes 159752 | tf_op jit(solution)/shard_map/ppermute | solution.py:36
  68.0 3.4 %collective-permute-start.2 = (f32[104,128]{1,0:T(8,128)S(1)}, f32[104,128]{1,0:T(8,128)S(1)}, u32[]{:S(2)}, u32[]{:S(2)}) collective-permute-start(f32[104,128]{1,0:T(8,128)S(1)} %get-tuple-element.44.refs_2_), channel_id=1, source_target_pairs={{0,1},{1,0},{2,3},{3,2},{4,5},{5,4},{6,7},{7,6},{8,9},{9,8},{10,11... | collective-permute-start | bytes 159752 | tf_op jit(solution)/shard_map/ppermute | solution.py:36
  68.0 4.8 %collective-permute-start.3 = (f32[104,128]{1,0:T(8,128)S(1)}, f32[104,128]{1,0:T(8,128)S(1)}, u32[]{:S(2)}, u32[]{:S(2)}) collective-permute-start(f32[104,128]{1,0:T(8,128)S(1)} %get-tuple-element.45.refs_3_), channel_id=1, source_target_pairs={{1,2},{2,1},{3,4},{4,3},{5,6},{6,5},{7,0},{0,7},{9,10},{10,9},{11,... | collective-permute-start | bytes 159752 | tf_op jit(solution)/shard_map/ppermute | solution.py:36
  75.3 6.2 %collective-permute-start.4 = (f32[104,128]{1,0:T(8,128)S(1)}, f32[104,128]{1,0:T(8,128)S(1)}, u32[]{:S(2)}, u32[]{:S(2)}) collective-permute-start(f32[104,128]{1,0:T(8,128)S(1)} %get-tuple-element.47.refs_0_), channel_id=1, source_target_pairs={{0,8},{8,0},{16,24},{24,16},{32,40},{40,32},{48,56},{56,48},{64,72... | collective-permute-start | bytes 159752 | tf_op jit(solution)/shard_map/ppermute | solution.py:36
  75.4 7.5 %collective-permute-start.5 = (f32[104,128]{1,0:T(8,128)S(1)}, f32[104,128]{1,0:T(8,128)S(1)}, u32[]{:S(2)}, u32[]{:S(2)}) collective-permute-start(f32[104,128]{1,0:T(8,128)S(1)} %get-tuple-element.48.refs_1_), channel_id=1, source_target_pairs={{8,16},{16,8},{24,32},{32,24},{40,48},{48,40},{56,64},{64,56},{72,... | collective-permute-start | bytes 159752 | tf_op jit(solution)/shard_map/ppermute | solution.py:36
  78.2 4.8 %collective-permute-start.6 = (f32[104,128]{1,0:T(8,128)S(1)}, f32[104,128]{1,0:T(8,128)S(1)}, u32[]{:S(2)}, u32[]{:S(2)}) collective-permute-start(f32[104,128]{1,0:T(8,128)S(1)} %get-tuple-element.49.refs_2_), channel_id=1, source_target_pairs={{0,1},{1,0},{2,3},{3,2},{4,5},{5,4},{6,7},{7,6},{8,9},{9,8},{10,11... | collective-permute-start | bytes 159752 | tf_op jit(solution)/shard_map/ppermute | solution.py:36
  78.2 4.8 %collective-permute-start.7 = (f32[104,128]{1,0:T(8,128)S(1)}, f32[104,128]{1,0:T(8,128)S(1)}, u32[]{:S(2)}, u32[]{:S(2)}) collective-permute-start(f32[104,128]{1,0:T(8,128)S(1)} %get-tuple-element.50.refs_3_), channel_id=1, source_target_pairs={{1,2},{2,1},{3,4},{4,3},{5,6},{6,5},{7,0},{0,7},{9,10},{10,9},{11,... | collective-permute-start | bytes 159752 | tf_op jit(solution)/shard_map/ppermute | solution.py:36
  85.6 6.6 %collective-permute-start.8 = (f32[104,128]{1,0:T(8,128)S(1)}, f32[104,128]{1,0:T(8,128)S(1)}, u32[]{:S(2)}, u32[]{:S(2)}) collective-permute-start(f32[104,128]{1,0:T(8,128)S(1)} %get-tuple-element.52.refs_0_), channel_id=1, source_target_pairs={{0,8},{8,0},{16,24},{24,16},{32,40},{40,32},{48,56},{56,48},{64,72... | collective-permute-start | bytes 159752 | tf_op jit(solution)/shard_map/ppermute | solution.py:36
  85.6 7.5 %collective-permute-start.9 = (f32[104,128]{1,0:T(8,128)S(1)}, f32[104,128]{1,0:T(8,128)S(1)}, u32[]{:S(2)}, u32[]{:S(2)}) collective-permute-start(f32[104,128]{1,0:T(8,128)S(1)} %get-tuple-element.53.refs_1_), channel_id=1, source_target_pairs={{8,16},{16,8},{24,32},{32,24},{40,48},{48,40},{56,64},{64,56},{72,... | collective-permute-start | bytes 159752 | tf_op jit(solution)/shard_map/ppermute | solution.py:36
  88.4 4.8 %collective-permute-start.10 = (f32[104,128]{1,0:T(8,128)S(1)}, f32[104,128]{1,0:T(8,128)S(1)}, u32[]{:S(2)}, u32[]{:S(2)}) collective-permute-start(f32[104,128]{1,0:T(8,128)S(1)} %get-tuple-element.54.refs_2_), channel_id=1, source_target_pairs={{0,1},{1,0},{2,3},{3,2},{4,5},{5,4},{6,7},{7,6},{8,9},{9,8},{10,11... | collective-permute-start | bytes 159752 | tf_op jit(solution)/shard_map/ppermute | solution.py:36
  88.4 4.8 %collective-permute-start.11 = (f32[104,128]{1,0:T(8,128)S(1)}, f32[104,128]{1,0:T(8,128)S(1)}, u32[]{:S(2)}, u32[]{:S(2)}) collective-permute-start(f32[104,128]{1,0:T(8,128)S(1)} %get-tuple-element.55.refs_3_), channel_id=1, source_target_pairs={{1,2},{2,1},{3,4},{4,3},{5,6},{6,5},{7,0},{0,7},{9,10},{10,9},{11,... | collective-permute-start | bytes 159752 | tf_op jit(solution)/shard_map/ppermute | solution.py:36
Sparse Core Ops, SparseCore 0:
  11.7 45.7 all-gather.1
